TPU v7x, 32 devices: a whole 2x2x4 slice. The times are simulated.
32 devices in a mesh: sub: 16 (over z, y, core), smp: 2 (over x).
Axes of the slice: x: 2, y: 2, z: 4, core: 2. Of those that a mesh axis runs over, the one named last changes fastest.
Arguments:
- trial: bfloat16 [16, 2, 3, 16, 768], P('sub', None, None, 'smp'), may hold values from -6 to 6
- stiff_lam: bfloat16 [768, 768], replicated
- stiff_mu: bfloat16 [768, 768], replicated
- log_modes: float32 [2, 16, 2, 3, 15], P(None, 'sub'), may hold values from -0.6 to 0.6
- nodes: float32 [16, 15], replicated, may hold values from -1 to 1
- quad_weights: float32 [16], replicated
- chaos_index: int32 [816, 15], replicated, may hold values from 0 to 3, as said below
- bonds: int32 [3, 16, 2, 3], replicated, may hold values 0 or 1
- face_map: int32 [16, 2, 3, 128], P('sub'), may hold values from 0 to 127, each once within a row
Outputs:
- coefficients: bfloat16 [16, 2, 3, 768, 816], P('sub', None, None, 'smp')
Inputs may be any that keep to these rules, and one draw needn't show every extreme that they name: Each row of chaos_index has entries summing to at most 3.
All inputs are finite; a program needn't handle non-finite values.
Results may differ from a plain program's by a relative error of at most 0.0063.
Values may be sent and summed in bfloat16 or wider, within the bound.
No kernel may reach another device: no remote copies, remote signals or barrier semaphores. Data moves between devices by JAX's collectives and lax.ppermute only.
A program may use at most 64 MiB of HBM per device.

v0:
```python
import jax
import jax.numpy as jnp
from jax import lax
from jax.sharding import PartitionSpec as P


def padded(array, sides, width):
    for axis, dim in sides:
        count, length = (lax.axis_size(axis), array.shape[dim])
        up = [(i, (i + 1) % count) for i in range(count - 1)]
        down = [(j, i) for i, j in up]
        last = lax.slice_in_dim(array, length - width, length, axis=dim)
        initial = lax.slice_in_dim(array, 0, width, axis=dim)
        before = lax.ppermute(last, axis, up)
        after = lax.ppermute(initial, axis, down)
        array = jnp.concatenate([before, array, after], axis=dim)
    return array


def legendre(points):
    second = jnp.sqrt(5.0) * (1.5 * points * points - 0.5)
    third = jnp.sqrt(7.0) * (2.5 * points * points * points - 1.5 * points)
    return [jnp.ones_like(points), jnp.sqrt(3.0) * points, second, third]


def chaos_basis(nodes, chaos_index, quad_weights):
    table = jnp.stack(legendre(nodes), axis=-1).reshape(nodes.shape[0], -1)
    columns = jnp.arange(chaos_index.shape[1], dtype=jnp.int32)[:, None] * 4 + chaos_index.T
    picked = jnp.take(table, columns, axis=1)
    total = jnp.prod(picked, axis=1)
    return (quad_weights[:, None] * total).astype(jnp.bfloat16)


def per_device(
    trial, stiff_lam, stiff_mu, log_modes, nodes, quad_weights, chaos_index, bonds, face_map
):
    layers, height, breadth, samples_here, width = trial.shape
    face_size = width // 6
    layer_start = lax.axis_index("sub") * layers
    sample_start = lax.axis_index("smp") * samples_here
    own_nodes = lax.dynamic_slice_in_dim(nodes, sample_start, samples_here, 0)
    moduli = jnp.exp(
        jnp.einsum("czyxk,qk->czyxq", log_modes, own_nodes, precision=lax.Precision.HIGHEST)
    )
    bond_all = jnp.concatenate(
        [jnp.zeros((3, 1, height, breadth), jnp.float32), bonds.astype(jnp.float32)], axis=1
    )
    bond_own = lax.dynamic_slice_in_dim(bond_all, layer_start + 1, layers, 1)[..., None, None]
    bond_under = lax.dynamic_slice_in_dim(bond_all, layer_start, layers, 1)[2][..., None, None]
    face_shape = (layers, height, breadth, samples_here, face_size)
    index = jnp.broadcast_to(face_map[:, :, :, None, :], face_shape)
    inverse = jnp.argsort(face_map, axis=-1)
    reverse = jnp.broadcast_to(inverse[:, :, :, None, :], face_shape)

    def schur(field):
        flattened = field.reshape(-1, width)
        part_one = jnp.dot(flattened, stiff_lam, preferred_element_type=jnp.float32).reshape(
            field.shape
        )
        part_two = jnp.dot(flattened, stiff_mu, preferred_element_type=jnp.float32).reshape(
            field.shape
        )
        return moduli[0][..., None] * part_one + moduli[1][..., None] * part_two

    def face_jumps(field):
        faces = field.reshape(layers, height, breadth, samples_here, 6, face_size)
        minus_x, plus_x = (faces[..., 0, :], faces[..., 1, :])
        minus_y, plus_y = (faces[..., 2, :], faces[..., 3, :])
        minus_z, plus_z = (faces[..., 4, :], faces[..., 5, :])
        bond_x, bond_y, bond_z = (bond_own[0], bond_own[1], bond_own[2])
        jump_mx = jnp.roll(bond_x, 1, axis=2) * (minus_x - jnp.roll(plus_x, 1, axis=2))
        jump_px = bond_x * (plus_x - jnp.roll(minus_x, -1, axis=2))
        jump_my = jnp.roll(bond_y, 1, axis=1) * (minus_y - jnp.roll(plus_y, 1, axis=1))
        jump_py = bond_y * (plus_y - jnp.roll(minus_y, -1, axis=1))
        pushed = jnp.take_along_axis(plus_z, reverse, axis=-1)
        stacked = jnp.stack([minus_z, pushed], axis=3)
        extended = padded(stacked, (("sub", 0),), 1)
        above = extended[2:, :, :, 0]
        below = extended[:-2, :, :, 1]
        jump_pz = bond_z * (plus_z - jnp.take_along_axis(above, index, axis=-1))
        jump_mz = bond_under * (minus_z - below)
        stacked_jumps = jnp.stack([jump_mx, jump_px, jump_my, jump_py, jump_mz, jump_pz], axis=4)
        return stacked_jumps.reshape(field.shape)

    first = schur(trial)
    jump_one = face_jumps(first).astype(jnp.bfloat16)
    second = schur(jump_one)
    jump_two = face_jumps(second).astype(jnp.bfloat16)
    basis = chaos_basis(nodes, chaos_index, quad_weights)
    flattened_jumps = jump_two.reshape(layers * height * breadth, samples_here, width)
    regrouped = jnp.einsum(
        "nqg,qp->ngp",
        lax.all_to_all(flattened_jumps, "smp", split_axis=2, concat_axis=1, tiled=True),
        basis,
        preferred_element_type=jnp.float32,
    ).astype(jnp.bfloat16)
    return regrouped.reshape(layers, height, breadth, width // lax.axis_size("smp"), basis.shape[1])


def solution(mesh):
    return jax.shard_map(
        per_device,
        mesh=mesh,
        in_specs=(
            P("sub", None, None, "smp", None),
            P(),
            P(),
            P(None, "sub", None, None, None),
            P(),
            P(),
            P(),
            P(),
            P("sub", None, None, None),
        ),
        out_specs=P("sub", None, None, "smp", None),
        check_vma=False,
    )
```

profile of v0, /device:TPU:10, one launch (start us, length us, event | category | flops | bytes accessed | tf_op | source)
XLA Modules:
  0.0 267.9 jit_solution(5009278305009623270)
XLA Ops:
  0.0 7.2 %sort.17 = (s32[1,2,3,128]{3,1,2,0:T(2,128)}, s32[1,2,3,128]{3,1,2,0:T(2,128)S(1)}) sort(s32[1,2,3,128]{3,1,2,0:T(2,128)} %param.19, s32[1,2,3,128]{3,1,2,0:T(2,128)S(1)} %iota.12), dimensions={3}, is_stable=true, to_apply=%region_0.0 | sort | flops 7680 | bytes 12288 | tf_op jit(solution)/shard_map/jit(argsort)/sort | solution.py:52
  7.2 0.9 fusion.32
  8.1 1.2 fusion.26
  9.3 1.6 fusion.14
  11.1 45.8 %gather_fusion.1 = f32[6144]{0:T(1024)S(1)} fusion(f32[2,3,8,128]{3,2,1,0:T(8,128)S(1)} %get-tuple-element.19, s32[6144]{0:T(1024)S(1)} %bitcast.287), kind=kCustom, calls=%fused_computation.clone | custom fusion | bytes 147456 | tf_op jit(solution)/shard_map/jit(take_along_axis)/gather | solution.py:75
  56.9 2.8 %collective-permute-start.1 = (f32[1,2,3,2,8,128]{5,4,2,1,3,0:T(8,128)S(1)}, f32[1,2,3,2,8,128]{5,4,2,1,3,0:T(8,128)S(1)}, u32[]{:S(2)}, u32[]{:S(2)}) collective-permute-start(f32[1,2,3,2,8,128]{5,4,2,1,3,0:T(8,128)S(1)} %pad_maximum_fusion), channel_id=1, source_target_pairs={{2,0},{4,2},{6,4},{8,6},{10,8},{12,10},{14,12},{16,14},{18,16},{20... | collective-permute-start | bytes 147464 | tf_op jit(solution)/shard_map/ppermute | solution.py:15
  59.7 1.9 collective-permute-start
  61.8 0.1 pad_dynamic-slice_fusion.3
  61.9 0.1 copy.136
  62.0 0.1 copy.147
  62.1 0.1 copy.148
  62.4 0.1 copy.137
  62.5 0.1 compare_and_fusion
  63.1 0.1 copy.158
  63.2 0.1 copy.154
  63.3 0.1 copy.179
  63.4 41.4 %gather_fusion = f32[12240,16]{1,0:T(8,128)} fusion(f32[16,60]{0,1:T(8,128)S(1)} %reshape.251, s32[12288]{0:T(1024)S(1)} %pad_clamp_fusion), kind=kCustom, calls=%fused_computation.4 | custom fusion | bytes 1615680 | tf_op jit(solution)/shard_map/jit(_take)/gather | solution.py:29
  104.8 45.8 %gather_fusion.2 = f32[6144]{0:T(1024)S(1)} fusion(f32[2,3,8,128]{3,2,1,0:T(8,128)S(1)} %slice_bitcast_fusion.2, s32[6144]{0:T(1024)S(1)} %bitcast.289), kind=kCustom, calls=%fused_computation.1.clone | custom fusion | bytes 147456 | tf_op jit(solution)/shard_map/jit(take_along_axis)/gather | solution.py:80
  150.8 0.3 fusion.29
  151.2 0.3 fusion.23
  151.5 45.8 %gather_fusion.3 = f32[6144]{0:T(1024)S(1)} fusion(f32[2,3,8,128]{3,2,1,0:T(8,128)S(1)} %get-tuple-element.13, s32[6144]{0:T(1024)S(1)} %bitcast.288), kind=kCustom, calls=%fused_computation.2.clone | custom fusion | bytes 147456 | tf_op jit(solution)/shard_map/jit(take_along_axis)/gather | solution.py:75
  197.4 4.5 %collective-permute-start.3 = (f32[1,2,3,2,8,128]{5,4,2,1,3,0:T(8,128)S(1)}, f32[1,2,3,2,8,128]{5,4,2,1,3,0:T(8,128)S(1)}, u32[]{:S(2)}, u32[]{:S(2)}) collective-permute-start(f32[1,2,3,2,8,128]{5,4,2,1,3,0:T(8,128)S(1)} %pad_maximum_fusion.1), channel_id=1, source_target_pairs={{2,0},{4,2},{6,4},{8,6},{10,8},{12,10},{14,12},{16,14},{18,16},{20... | collective-permute-start | bytes 147464 | tf_op jit(solution)/shard_map/ppermute | solution.py:15
  202.0 1.9 collective-permute-start.2
  204.3 45.8 %gather_fusion.4 = f32[6144]{0:T(1024)S(1)} fusion(f32[2,3,8,128]{3,2,1,0:T(8,128)S(1)} %slice_bitcast_fusion, s32[6144]{0:T(1024)S(1)} %bitcast.290), kind=kCustom, calls=%fused_computation.3.clone | custom fusion | bytes 147456 | tf_op jit(solution)/shard_map/jit(take_along_axis)/gather | solution.py:80
  250.3 1.0 copy.177
  251.3 1.9 reshape.351
  253.2 3.8 %all-to-all-start = ((bf16[2,2,9216]{2,1,0:T(2,128)(2,1)}), bf16[2,2,9216]{2,1,0:T(2,128)(2,1)S(1)}, u32[]{:S(2)}, u32[]{:S(2)}) async-start(bf16[2,2,9216]{2,1,0:T(2,128)(2,1)} %reshape.351), calls=%async_computation | async-start | bytes 147456 | tf_op jit(solution)/shard_map/all_to_all | solution.py:93
  257.0 5.3 %select_reduce_fusion = f32[816,16]{1,0:T(8,128)S(1)} fusion(f32[15,816,16]{2,1,0:T(8,128)} %bitcast.291, pred[15,816]{1,0:T(8,128)(4,1)S(1)} %get-tuple-element.8), kind=kLoop, calls=%fused_computation.5 | loop fusion | flops 378624 | bytes 847824 | tf_op jit(solution)/shard_map/reduce_prod | solution.py:30
  262.3 0.1 copy.180
  262.5 1.5 reshape.352
  264.0 0.8 copy.178
  264.8 3.1 %convolution_convert_fusion = bf16[6,384,816]{1,2,0:T(8,128)(2,1)} fusion(bf16[6,8,2,384]{3,1,2,0:T(8,128)(2,1)S(1)} %copy.178, f32[816,16]{0,1:T(8,128)S(1)} %copy.180, f32[16]{0:T(128)S(1)} %copy-done.6), kind=kOutput, calls=%fused_computation.6 | convolution fusion | flops 62068224 | bytes 3886144 | tf_op jit(solution)/shard_map/nqg,qp->ngp/dot_general | solution.py:91
  (74 shorter events, 1.6 us)
Async XLA Ops:
  0.0 8.1 %copy-start = (bf16[768,768]{1,0:T(8,128)(2,1)S(1)}, bf16[768,768]{1,0:T(8,128)(2,1)}, u32[]{:S(2)}) copy-start(bf16[768,768]{1,0:T(8,128)(2,1)} %param.12) | copy-start | bytes 3538948
  11.0 50.6 %copy-start.3 = (s32[1,2,3,128]{3,1,2,0:T(2,128)S(1)}, s32[1,2,3,128]{3,1,2,0:T(2,128)}, u32[]{:S(2)}) copy-start(s32[1,2,3,128]{3,1,2,0:T(2,128)} %param.19) | copy-start | bytes 9220
  11.0 50.6 %copy-start.4 = (f32[16,15]{1,0:T(8,128)S(1)}, f32[16,15]{1,0:T(8,128)}, u32[]{:S(2)}) copy-start(f32[16,15]{1,0:T(8,128)} %param.15) | copy-start | bytes 2884
  11.0 50.7 %copy-start.5 = (s32[3,16,2,3]{1,2,3,0:T(2,128)S(1)}, s32[3,16,2,3]{1,2,3,0:T(2,128)}, u32[]{:S(2)}) copy-start(s32[3,16,2,3]{1,2,3,0:T(2,128)} %param.18) | copy-start | bytes 3460
  11.0 51.4 %copy-start.2 = (s32[816,15]{0,1:T(8,128)S(1)}, s32[816,15]{0,1:T(8,128)}, u32[]{:S(2)}) copy-start(s32[816,15]{0,1:T(8,128)} %param.17) | copy-start | bytes 146884
  56.9 47.9 %collective-permute-start.1 = (f32[1,2,3,2,8,128]{5,4,2,1,3,0:T(8,128)S(1)}, f32[1,2,3,2,8,128]{5,4,2,1,3,0:T(8,128)S(1)}, u32[]{:S(2)}, u32[]{:S(2)}) collective-permute-start(f32[1,2,3,2,8,128]{5,4,2,1,3,0:T(8,128)S(1)} %pad_maximum_fusion), channel_id=1, source_target_pairs={{2,0},{4,2},{6,4},{8,6},{10,8},{12,10},{14,12},{16,14},{18,16},{20... | collective-permute-start | bytes 147464 | tf_op jit(solution)/shard_map/ppermute | solution.py:15
  59.7 91.0 %collective-permute-start = (f32[1,2,3,2,8,128]{5,4,2,1,3,0:T(8,128)S(1)}, f32[1,2,3,2,8,128]{5,4,2,1,3,0:T(8,128)S(1)}, u32[]{:S(2)}, u32[]{:S(2)}) collective-permute-start(f32[1,2,3,2,8,128]{5,4,2,1,3,0:T(8,128)S(1)} %pad_maximum_fusion), channel_id=1, source_target_pairs={{0,2},{2,4},{4,6},{6,8},{8,10},{10,12},{12,14},{14,16},{16,18},{18... | collective-permute-start | bytes 147464 | tf_op jit(solution)/shard_map/ppermute | solution.py:14
  104.8 46.4 %copy-start.1 = (bf16[768,768]{1,0:T(8,128)(2,1)S(1)}, bf16[768,768]{1,0:T(8,128)(2,1)}, u32[]{:S(2)}) copy-start(bf16[768,768]{1,0:T(8,128)(2,1)} %param.13) | copy-start | bytes 3538948
  197.4 6.8 %collective-permute-start.3 = (f32[1,2,3,2,8,128]{5,4,2,1,3,0:T(8,128)S(1)}, f32[1,2,3,2,8,128]{5,4,2,1,3,0:T(8,128)S(1)}, u32[]{:S(2)}, u32[]{:S(2)}) collective-permute-start(f32[1,2,3,2,8,128]{5,4,2,1,3,0:T(8,128)S(1)} %pad_maximum_fusion.1), channel_id=1, source_target_pairs={{2,0},{4,2},{6,4},{8,6},{10,8},{12,10},{14,12},{16,14},{18,16},{20... | collective-permute-start | bytes 147464 | tf_op jit(solution)/shard_map/ppermute | solution.py:15
  202.0 48.1 %collective-permute-start.2 = (f32[1,2,3,2,8,128]{5,4,2,1,3,0:T(8,128)S(1)}, f32[1,2,3,2,8,128]{5,4,2,1,3,0:T(8,128)S(1)}, u32[]{:S(2)}, u32[]{:S(2)}) collective-permute-start(f32[1,2,3,2,8,128]{5,4,2,1,3,0:T(8,128)S(1)} %pad_maximum_fusion.1), channel_id=1, source_target_pairs={{0,2},{2,4},{4,6},{6,8},{8,10},{10,12},{12,14},{14,16},{16,18},{18... | collective-permute-start | bytes 147464 | tf_op jit(solution)/shard_map/ppermute | solution.py:14
  253.2 9.3 %all-to-all-start = ((bf16[2,2,9216]{2,1,0:T(2,128)(2,1)}), bf16[2,2,9216]{2,1,0:T(2,128)(2,1)S(1)}, u32[]{:S(2)}, u32[]{:S(2)}) async-start(bf16[2,2,9216]{2,1,0:T(2,128)(2,1)} %reshape.351), calls=%async_computation | async-start | bytes 147456 | tf_op jit(solution)/shard_map/all_to_all | solution.py:93
  262.3 2.5 copy-start.6
where the time goes:
time: 270 us; the launch traced here: 268 us
  local copies, waits for them, and re-layouts  231 us (86%)
  starting transfers between devices  15 us (6%)
  other arithmetic  13.8 us (5%)
  matrix products  7.5 us (3%)
    gather x2, local copies, waits for them, and re-layouts, face_jumps(): pushed = jnp.take_along_axis(plus_z, reverse, axis=-1)  91.7 us
    gather x2, local copies, waits for them, and re-layouts, face_jumps(): jump_pz = bond_z * (plus_z - jnp.take_along_axis(above, index, axis=-1))  91.7 us
    gather x1, local copies, waits for them, and re-layouts, chaos_basis(): picked = jnp.take(table, columns, axis=1)  41.4 us
    ppermute x2, starting transfers between devices, padded(): after = lax.ppermute(initial, axis, down)  7.29 us
    sort x1, other arithmetic, per_device(): inverse = jnp.argsort(face_map, axis=-1)  7.19 us
  transfers between devices with their start and end apart: 5, of which 0 were waited for; matrix products, arithmetic and copies ran while one was open for 52% of the time, Pallas kernels for 0%

commit v1 on v0

v1 whole, which is shorter than its diff:
```python
import functools

import jax
import jax.numpy as jnp
from jax import lax
from jax.experimental import pallas as pl
from jax.experimental.pallas import tpu as pltpu
from jax.sharding import PartitionSpec as P

F32 = jnp.float32
BF16 = jnp.bfloat16
VMEM = pl.BlockSpec(memory_space=pltpu.VMEM)
SMEM = pl.BlockSpec(memory_space=pltpu.SMEM)
ANY = pl.BlockSpec(memory_space=pl.ANY)


def shaped(shape, dtype=F32):
    return jax.ShapeDtypeStruct(shape, dtype)


def call(body, outs, specs, args, flops=0, scratch=(), out_specs=None):
    return pl.pallas_call(
        body,
        out_shape=outs,
        in_specs=specs,
        out_specs=[VMEM] * len(outs) if out_specs is None else out_specs,
        scratch_shapes=list(scratch),
        cost_estimate=pl.CostEstimate(flops=flops, bytes_accessed=0, transcendentals=0),
        compiler_params=pltpu.CompilerParams(vmem_limit_bytes=24 << 20),
    )(*args)


def dot(a, b):
    return jnp.dot(a, b, preferred_element_type=F32)


def wide(column, width):
    return jnp.concatenate([column] * (width // 128), axis=1)


def schur(rows, lam, mu, mod_lam, mod_mu):
    width = lam.shape[1]
    return wide(mod_lam, width) * dot(rows, lam) + wide(mod_mu, width) * dot(rows, mu)


class Sizes:
    def __init__(self, trial, basis_size, parts):
        _, self.height, self.breadth, self.here, self.width = trial.shape
        self.face = self.width // 6
        self.subs = self.height * self.breadth
        self.parts = parts
        self.samples = self.here * parts
        self.rows = self.subs * self.samples
        self.plane = 4 * self.face
        self.terms = basis_size
        self.share = self.width // parts

    def own(self, n, part):
        return pl.ds(pl.multiple_of(n * self.samples + part * self.here, 8), self.here)

    def block(self, n):
        return slice(n * self.samples, (n + 1) * self.samples)

    def group(self, n):
        return slice(n * self.here, (n + 1) * self.here)


def prepare(
    d, trial, lam, mu, modes, nodes, weights, chaos, faces, mod, maps, basis, plane, zed
):
    points = nodes[...]
    for c in range(2):
        for n in range(d.subs):
            row = modes[c, 0, n // d.breadth, pl.ds(n % d.breadth, 1), :]
            total = jnp.exp(jnp.sum(points * row, axis=1, keepdims=True))
            mod[c, d.block(n), :] = jnp.broadcast_to(total, (d.samples, 128))
    target = lax.broadcasted_iota(jnp.int32, (d.face, d.face), 0)
    source = lax.broadcasted_iota(jnp.int32, (8, d.face), 1).astype(F32).astype(BF16)
    for n in range(d.subs):
        row = faces[0, n // d.breadth, pl.ds(n % d.breadth, 1), :]
        hit = jnp.where(row == target, 1.0, 0.0).astype(BF16)
        back = lax.dot_general(
            source, hit, (((1,), (1,)), ((), ())), preferred_element_type=F32
        )
        maps[0, n] = jnp.broadcast_to(row, (8, d.face))
        maps[1, n] = back.astype(jnp.int32)
    count = points.shape[1]
    same = lax.broadcasted_iota(jnp.int32, (16, count), 0) == lax.broadcasted_iota(
        jnp.int32, (16, count), 1
    )
    degree = lax.dot_general(
        jnp.where(same, 1.0, 0.0).astype(BF16),
        chaos[...].astype(F32).astype(BF16),
        (((1,), (1,)), ((), ())),
        preferred_element_type=F32,
    )
    one = jnp.sqrt(3.0) * points
    two = jnp.sqrt(5.0) * (1.5 * points * points - 0.5)
    three = jnp.sqrt(7.0) * (2.5 * points * points * points - 1.5 * points)
    total = jnp.ones((d.samples, d.terms), F32)
    for k in range(count):
        c = degree[k : k + 1, :]
        high = jnp.where(c > 2.5, three[:, k : k + 1], two[:, k : k + 1])
        low = jnp.where(c > 0.5, one[:, k : k + 1], 1.0)
        total = total * jnp.where(c > 1.5, high, low)
    square = (d.samples, d.samples)
    diagonal = lax.broadcasted_iota(jnp.int32, square, 0) == lax.broadcasted_iota(
        jnp.int32, square, 1
    )
    column = jnp.sum(jnp.where(diagonal, weights[...], 0.0), axis=1, keepdims=True)
    table = (column * total).astype(BF16)
    for n in range(d.subs):
        basis[n] = jnp.zeros((d.rows, d.terms), BF16)
        basis[n, d.block(n), :] = table
    part = lax.axis_index("smp")
    field = trial[...]
    first = dot(field, lam[...])
    second = dot(field, mu[...])
    for n in range(d.subs):
        own = d.own(n, part)
        value = (
            wide(mod[0, own, :], d.width) * first[d.group(n)]
            + wide(mod[1, own, :], d.width) * second[d.group(n)]
        )
        plane[d.group(n), :] = value[:, : d.plane]
        zed[d.group(n), :] = value[:, d.plane :]


def payloads(d, low, high, maps, on_chip, off_chip):
    even = lax.rem(lax.axis_index("sub"), 2) == 0
    for n in range(d.subs):
        back = maps[1, n]
        for start in range(n * d.samples, (n + 1) * d.samples, 8):
            rows = slice(start, start + 8)
            minus = low[rows]
            pushed = jnp.take_along_axis(high[rows], back, axis=1, mode="promise_in_bounds")
            on_chip[rows, :] = jnp.where(even, pushed, minus)
            off_chip[rows, :] = jnp.where(even, minus, pushed)


def part_of(d, shift):
    here = lax.axis_index("smp")
    return lax.rem(here - shift + d.parts, d.parts)


def first_z(d, *refs):
    others = refs[: d.parts - 1]
    lam, mu, mod, maps, zed, field, on_chip, off_chip = refs[d.parts - 1 :]
    part = lax.axis_index("smp")
    for n in range(d.subs):
        field[d.own(n, part), :] = zed[d.group(n), :]
    for shift, other in enumerate(others, 1):
        part = part_of(d, shift)
        rows = other[...]
        first = dot(rows, lam[:, d.plane :])
        second = dot(rows, mu[:, d.plane :])
        for n in range(d.subs):
            own = d.own(n, part)
            field[own, :] = (
                wide(mod[0, own, :], 2 * d.face) * first[d.group(n)]
                + wide(mod[1, own, :], 2 * d.face) * second[d.group(n)]
            )
    payloads(d, field[:, : d.face], field[:, d.face :], maps, on_chip, off_chip)


def plane_jumps(d, field, bonds, out):
    layer = lax.axis_index("sub")

    def bond(axis, n):
        return bonds[axis, layer, n // d.breadth, n % d.breadth].astype(F32)

    for n in range(d.subs):
        y, x = divmod(n, d.breadth)
        left = y * d.breadth + (x - 1) % d.breadth
        right = y * d.breadth + (x + 1) % d.breadth
        front = (y - 1) % d.height * d.breadth + x
        behind = (y + 1) % d.height * d.breadth + x

        def face(which, m):
            return field[d.block(m), which * d.face : (which + 1) * d.face]

        out(0, n, bond(0, left) * (face(0, n) - face(1, left)))
        out(1, n, bond(0, n) * (face(1, n) - face(0, right)))
        out(2, n, bond(1, front) * (face(2, n) - face(3, front)))
        out(3, n, bond(1, n) * (face(3, n) - face(2, behind)))


def z_jumps(d, field, from_chip, from_off, maps, bonds, out):
    layer = lax.axis_index("sub")
    even = lax.rem(layer, 2) == 0
    under = jnp.maximum(layer - 1, 0)
    for n in range(d.subs):
        y, x = divmod(n, d.breadth)
        bond_up = bonds[2, layer, y, x].astype(F32)
        bond_down = jnp.where(layer > 0, bonds[2, under, y, x].astype(F32), 0.0)
        for start in range(n * d.samples, (n + 1) * d.samples, 8):
            rows = slice(start, start + 8)
            near, far = from_chip[rows, :], from_off[rows, :]
            above = jnp.where(even, near, far)
            below = jnp.where(even, far, near)
            matched = jnp.take_along_axis(above, maps[0, n], axis=1, mode="promise_in_bounds")
            out(0, rows, bond_down * (field[rows, : d.face] - below))
            out(1, rows, bond_up * (field[rows, d.face :] - matched))


def first_plane(d, *refs):
    others = refs[: d.parts - 1]
    lam, mu, mod, plane, bonds, jumps, part_lam, part_mu, field = refs[d.parts - 1 :]
    part = lax.axis_index("smp")
    for n in range(d.subs):
        field[d.own(n, part), :] = plane[d.group(n), :]
    for shift, other in enumerate(others, 1):
        part = part_of(d, shift)
        rows = other[...]
        first = dot(rows, lam[:, : d.plane])
        second = dot(rows, mu[:, : d.plane])
        for n in range(d.subs):
            own = d.own(n, part)
            field[own, :] = (
                wide(mod[0, own, :], d.plane) * first[d.group(n)]
                + wide(mod[1, own, :], d.plane) * second[d.group(n)]
            )

    def put(which, n, value):
        jumps[d.block(n), which * d.face : (which + 1) * d.face] = value.astype(BF16)

    plane_jumps(d, field, bonds, put)
    part_lam[...] = dot(jumps[...], lam[: d.plane, d.plane :])
    part_mu[...] = dot(jumps[...], mu[: d.plane, d.plane :])


def second_z(
    d, field, from_chip, from_off, maps, bonds, mod, lam, mu, part_lam, part_mu,
    jumps, result, on_chip, off_chip, held,
):
    def put(which, rows, value):
        held[rows, which * d.face : (which + 1) * d.face] = value

    z_jumps(d, field, from_chip, from_off, maps, bonds, put)
    rounded = held[...].astype(BF16)
    jumps[...] = rounded
    one = part_lam[...] + dot(rounded, lam[d.plane :, d.plane :])
    two = part_mu[...] + dot(rounded, mu[d.plane :, d.plane :])
    result[...] = wide(mod[0], 2 * d.face) * one + wide(mod[1], 2 * d.face) * two
    payloads(d, result[:, : d.face], result[:, d.face :], maps, on_chip, off_chip)


def second_plane(d, plane, zed, lam, mu, mod, bonds, turned, held):
    one = dot(plane[...], lam[: d.plane, : d.plane]) + dot(zed[...], lam[d.plane :, : d.plane])
    two = dot(plane[...], mu[: d.plane, : d.plane]) + dot(zed[...], mu[d.plane :, : d.plane])
    field = wide(mod[0], d.plane) * one + wide(mod[1], d.plane) * two

    def put(which, n, value):
        held[which, d.block(n), :] = value

    plane_jumps(d, field, bonds, put)
    for which in range(4):
        turned[which * d.face : (which + 1) * d.face, :] = held[which].T.astype(BF16)


def project(d, field, from_chip, from_off, maps, bonds, plane, basis, out, held, turned, rows_out, sems):
    def put(which, rows, value):
        held[which, rows, :] = value

    z_jumps(d, field, from_chip, from_off, maps, bonds, put)
    turned[: d.plane, :] = plane[...]
    for which in range(2):
        start = d.plane + which * d.face
        turned[start : start + d.face, :] = held[which].T.astype(BF16)
    start = pl.multiple_of(lax.axis_index("smp") * d.share, 16)
    left = turned[pl.ds(start, d.share), :]
    copies = []
    for n in range(d.subs):
        rows_out[n] = dot(left, basis[n]).astype(BF16)
        copy = pltpu.make_async_copy(
            rows_out.at[n], out.at[0, n // d.breadth, n % d.breadth], sems.at[n]
        )
        copy.start()
        copies.append(copy)
    for copy in copies:
        copy.wait()


def per_device(
    trial, stiff_lam, stiff_mu, log_modes, nodes, quad_weights, chaos_index, bonds, face_map
):
    parts = lax.axis_size("smp")
    layers = lax.axis_size("sub")
    d = Sizes(trial, chaos_index.shape[0], parts)
    rows, face = d.rows, d.face
    own = trial.reshape(d.subs * d.here, d.width)
    others = [
        lax.ppermute(own, "smp", [(i, (i + shift) % parts) for i in range(parts)])
        for shift in range(1, parts)
    ]
    pairs = [(i, i ^ 1) for i in range(layers)]
    ends = [(i, i + 1) for i in range(1, layers - 1, 2)]
    ends = ends + [(j, i) for i, j in ends]

    def exchange(on_chip, off_chip):
        return lax.ppermute(on_chip, "sub", pairs), lax.ppermute(off_chip, "sub", ends)

    def run(body, *args, **options):
        return call(functools.partial(body, d), *args, **options)

    mod, maps, basis, plane, zed = run(
        prepare,
        [
            shaped((2, rows, 128)),
            shaped((2, d.subs, 8, face), jnp.int32),
            shaped((d.subs, rows, d.terms), BF16),
            shaped((d.subs * d.here, d.plane)),
            shaped((d.subs * d.here, 2 * face)),
        ],
        [VMEM] * 8,
        [
            own, stiff_lam, stiff_mu, log_modes, nodes,
            quad_weights.reshape(1, -1), chaos_index, face_map,
        ],
    )
    field, on_chip, off_chip = run(
        first_z,
        [shaped((rows, 2 * face)), shaped((rows, face)), shaped((rows, face))],
        [VMEM] * (parts + 4),
        [*others, stiff_lam, stiff_mu, mod, maps, zed],
    )
    near, far = exchange(on_chip, off_chip)
    jumps_plane, part_lam, part_mu = run(
        first_plane,
        [shaped((rows, d.plane), BF16), shaped((rows, 2 * face)), shaped((rows, 2 * face))],
        [VMEM] * (parts + 3) + [SMEM],
        [*others, stiff_lam, stiff_mu, mod, plane, bonds],
        scratch=[pltpu.VMEM((rows, d.plane), F32)],
    )
    jumps_z, field, on_chip, off_chip = run(
        second_z,
        [
            shaped((rows, 2 * face), BF16),
            shaped((rows, 2 * face)),
            shaped((rows, face)),
            shaped((rows, face)),
        ],
        [VMEM] * 4 + [SMEM] + [VMEM] * 5,
        [field, near, far, maps, bonds, mod, stiff_lam, stiff_mu, part_lam, part_mu],
        scratch=[pltpu.VMEM((rows, 2 * face), F32)],
    )
    near, far = exchange(on_chip, off_chip)
    (turned,) = run(
        second_plane,
        [shaped((d.plane, rows), BF16)],
        [VMEM] * 5 + [SMEM],
        [jumps_plane, jumps_z, stiff_lam, stiff_mu, mod, bonds],
        scratch=[pltpu.VMEM((4, rows, face), F32)],
    )
    (out,) = run(
        project,
        [shaped((1, d.height, d.breadth, d.share, d.terms), BF16)],
        [VMEM] * 4 + [SMEM] + [VMEM] * 2,
        [field, near, far, maps, bonds, turned, basis],
        out_specs=[ANY],
        scratch=[
            pltpu.VMEM((2, rows, face), F32),
            pltpu.VMEM((d.width, rows), BF16),
            pltpu.VMEM((d.subs, d.share, d.terms), BF16),
            pltpu.SemaphoreType.DMA((d.subs,)),
        ],
    )
    return out


def solution(mesh):
    return jax.shard_map(
        per_device,
        mesh=mesh,
        in_specs=(
            P("sub", None, None, "smp", None),
            P(),
            P(),
            P(None, "sub", None, None, None),
            P(),
            P(),
            P(),
            P(),
            P("sub", None, None, None),
        ),
        out_specs=P("sub", None, None, "smp", None),
        check_vma=False,
    )
```

time: 270 us -> 42.2 us (0.16)
  the two profiles are of different devices: /device:TPU:10 before, /device:TPU:13 now
where the time goes in v1:
time: 42.2 us; the launch traced here: 41.6 us
  local copies, waits for them, and re-layouts  18.9 us (45%)
  Pallas kernels  11.6 us (27%)
  starting transfers between devices  8.51 us (20%)
  waiting for transfers between devices  2.44 us (6%)
    unnamed x30, local copies, waits for them, and re-layouts  12.7 us
    pallas_call x6, Pallas kernels, call(): pl.pallas_call(body, out_shape=outs, in_specs=specs, out_specs=[VMEM] * l...  11.6 us
    pallas_call x1, local copies, waits for them, and re-layouts, call(): pl.pallas_call(body, out_shape=outs, in_specs=specs, out_specs=[VMEM] * l...  6.21 us
    ppermute x2, starting transfers between devices, exchange(): lax.ppermute(off_chip, 'sub', ends)  6.21 us
    ppermute x2, waiting for transfers between devices, exchange(): lax.ppermute(off_chip, 'sub', ends)  2.43 us
    ppermute x1, starting transfers between devices, per_device(): lax.ppermute(own, 'smp', [(i, (i + shift) % parts) for i in range(parts)])  1.21 us
    ppermute x2, starting transfers between devices, exchange(): lax.ppermute(on_chip, 'sub', pairs)  1.09 us
  transfers between devices with their start and end apart: 5, of which 2 were waited for; matrix products, arithmetic and copies ran while one was open for 6% of the time, Pallas kernels for 11%

profile of v1, /device:TPU:13, one launch (start us, length us, event | category | flops | bytes accessed | tf_op | source)
XLA Modules:
  0.0 41.6 jit_solution(6274881360934029094)
XLA Ops:
  0.0 1.2 %collective-permute-start = (bf16[48,768]{1,0:T(8,128)(2,1)}, bf16[48,768]{1,0:T(8,128)(2,1)S(1)}, u32[]{:S(2)}, u32[]{:S(2)}) collective-permute-start(bf16[48,768]{1,0:T(8,128)(2,1)} %bitcast.2), channel_id=1, source_target_pairs={{0,1},{1,0},{2,3},{3,2},{4,5},{5,4},{6,7},{7,6},{8,9},{9,8},{10,11... | collective-permute-start | bytes 221192 | tf_op jit(solution)/shard_map/ppermute | solution.py:293
  1.2 0.7 %copy.12.faces = s32[1,2,3,128]{3,2,1,0:T(4,128)S(1)} copy(s32[1,2,3,128]{3,1,2,0:T(2,128)} %param.17) | data formatting | bytes 6144 | tf_op args[8]
  1.9 0.7 %copy.10.modes = f32[2,1,2,3,15]{4,3,2,1,0:T(4,128)S(1)} copy(f32[2,1,2,3,15]{4,2,3,1,0:T(2,128)} %param.12) | data formatting | bytes 1440 | tf_op args[3]
  2.6 1.0 %copy.11.chaos = s32[816,15]{1,0:T(8,128)S(1)} copy(s32[816,15]{0,1:T(8,128)} %param.15) | data formatting | bytes 97920 | tf_op args[6]
  3.6 0.0 copy-start
  3.6 1.3 %copy-done = bf16[768,768]{1,0:T(8,128)(2,1)S(1)} copy-done((bf16[768,768]{1,0:T(8,128)(2,1)S(1)}, bf16[768,768]{1,0:T(8,128)(2,1)}, u32[]{:S(2)}) %copy-start) | copy-done | bytes 1179672
  4.9 1.3 %copy-done.3 = bf16[768,768]{1,0:T(8,128)(2,1)S(1)} copy-done((bf16[768,768]{1,0:T(8,128)(2,1)S(1)}, bf16[768,768]{1,0:T(8,128)(2,1)}, u32[]{:S(2)}) %copy-start.3) | copy-done | bytes 1179672
  6.1 0.9 %copy-done.9 = bf16[1,2,3,8,768]{4,3,2,1,0:T(8,128)(2,1)S(1)} copy-done((bf16[1,2,3,8,768]{4,3,2,1,0:T(8,128)(2,1)S(1)}, bf16[1,2,3,8,768]{4,3,2,1,0:T(8,128)(2,1)}, u32[]{:S(2)}) %copy-start.9) | copy-done | bytes 73752
  7.0 0.7 %copy-done.10 = f32[16,15]{1,0:T(8,128)S(1)} copy-done((f32[16,15]{1,0:T(8,128)S(1)}, f32[16,15]{1,0:T(8,128)}, u32[]{:S(2)}) %copy-start.10) | copy-done | bytes 984
  7.7 0.7 %copy-done.11 = f32[16]{0:T(128)S(1)} copy-done((f32[16]{0:T(128)S(1)}, f32[16]{0:T(128)}, u32[]{:S(2)}) %copy-start.11) | copy-done | bytes 88
  8.4 0.8 %shard_map.91 = (f32[2,96,128]{2,1,0:T(8,128)S(1)}, s32[2,6,8,128]{3,2,1,0:T(8,128)S(1)}, bf16[6,96,816]{2,1,0:T(8,128)(2,1)S(1)}, f32[48,512]{1,0:T(8,128)S(1)}, f32[48,256]{1,0:T(8,128)S(1)}) custom-call(bf16[48,768]{1,0:T(8,128)(2,1)S(1)} %bitcast.3, bf16[768,768]{1,0:T(8,128)(2,1)S(1)} %copy-done, bf16[768,768]{1,0:T(8,128)(2,1)S(1)} %copy-done.3, ...), custom_call_target="tpu_custom_call" | custom-call | tf_op jit(solution)/shard_map/pallas_call | solution.py:22
  9.2 0.0 copy-start.7
  9.2 1.0 %copy-done.7 = bf16[6,96,816]{2,1,0:T(8,128)(2,1)} copy-done((bf16[6,96,816]{2,1,0:T(8,128)(2,1)}, bf16[6,96,816]{2,1,0:T(8,128)(2,1)S(1)}, u32[]{:S(2)}) %copy-start.7) | copy-done | bytes 940056
  10.1 0.0 collective-permute-done.refs_0_
  10.2 1.3 %copy-done.1 = bf16[768,768]{1,0:T(8,128)(2,1)S(1)} copy-done((bf16[768,768]{1,0:T(8,128)(2,1)S(1)}, bf16[768,768]{1,0:T(8,128)(2,1)}, u32[]{:S(2)}) %copy-start.1) | copy-done | bytes 1179672
  11.4 1.3 %copy-done.4 = bf16[768,768]{1,0:T(8,128)(2,1)S(1)} copy-done((bf16[768,768]{1,0:T(8,128)(2,1)S(1)}, bf16[768,768]{1,0:T(8,128)(2,1)}, u32[]{:S(2)}) %copy-start.4) | copy-done | bytes 1179672
  12.7 0.3 shard_map.92
  13.0 1.0 %collective-permute-start.1 = (f32[96,128]{1,0:T(8,128)S(1)}, f32[96,128]{1,0:T(8,128)S(1)}, u32[]{:S(2)}, u32[]{:S(2)}) collective-permute-start(f32[96,128]{1,0:T(8,128)S(1)} %get-tuple-element.24), channel_id=1, source_target_pairs={{0,2},{2,0},{4,6},{6,4},{8,10},{10,8},{12,14},{14,12},{16,18},{18,... | collective-permute-start | bytes 147464 | tf_op jit(solution)/shard_map/ppermute | solution.py:301
  14.1 3.0 %collective-permute-start.2 = (f32[96,128]{1,0:T(8,128)S(1)}, f32[96,128]{1,0:T(8,128)S(1)}, u32[]{:S(2)}, u32[]{:S(2)}) collective-permute-start(f32[96,128]{1,0:T(8,128)S(1)} %get-tuple-element.25), channel_id=1, source_target_pairs={{2,4},{6,8},{10,12},{14,16},{18,20},{22,24},{26,28},{4,2},{8,6},{1... | collective-permute-start | bytes 147464 | tf_op jit(solution)/shard_map/ppermute | solution.py:301
  17.1 0.1 copy.14.refs_5_.bonds
  17.2 0.0 copy-start.8
  17.3 1.9 %shard_map.93 = (bf16[96,512]{1,0:T(8,128)(2,1)S(1)}, f32[96,256]{1,0:T(8,128)S(1)}, f32[96,256]{1,0:T(8,128)S(1)}) custom-call(bf16[48,768]{1,0:T(8,128)(2,1)S(1)} %collective-permute-done.refs_0_, bf16[768,768]{1,0:T(8,128)(2,1)S(1)} %copy-done.2, bf16[768,768]{1,0:T(8,128)(2,1)S(1)} %copy-done.5, f32[2,96,128]{2,1,0:T(8,128)S(1)} %get-tuple-element.20.refs_3_.mod, ...), custom_call_target="tpu_custom_call" | custom-call | tf_op jit(solution)/shard_map/pallas_call | solution.py:22
  19.2 1.1 %collective-permute-done.2.from_off = f32[96,128]{1,0:T(8,128)S(1)} collective-permute-done((f32[96,128]{1,0:T(8,128)S(1)}, f32[96,128]{1,0:T(8,128)S(1)}, u32[]{:S(2)}, u32[]{:S(2)}) %collective-permute-start.2) | collective-permute-done | bytes 49184 | tf_op jit(solution)/shard_map/ppermute | solution.py:301
  20.4 1.6 %shard_map.94 = (bf16[96,256]{1,0:T(8,128)(2,1)S(1)}, f32[96,256]{1,0:T(8,128)S(1)}, f32[96,128]{1,0:T(8,128)S(1)}, f32[96,128]{1,0:T(8,128)S(1)}) custom-call(f32[96,256]{1,0:T(8,128)S(1)} %get-tuple-element.23.field, f32[96,128]{1,0:T(8,128)S(1)} %collective-permute-done.1.from_chip, f32[96,128]{1,0:T(8,128)S(1)} %collective-permute-done.2.from_off, ...), custom_call_target="tpu_custom_call" | custom-call | tf_op jit(solution)/shard_map/pallas_call | solution.py:22
  22.0 0.1 collective-permute-start.3
  22.1 3.2 %collective-permute-start.4 = (f32[96,128]{1,0:T(8,128)S(1)}, f32[96,128]{1,0:T(8,128)S(1)}, u32[]{:S(2)}, u32[]{:S(2)}) collective-permute-start(f32[96,128]{1,0:T(8,128)S(1)} %get-tuple-element.31), channel_id=1, source_target_pairs={{2,4},{6,8},{10,12},{14,16},{18,20},{22,24},{26,28},{4,2},{8,6},{1... | collective-permute-start | bytes 147464 | tf_op jit(solution)/shard_map/ppermute | solution.py:301
  25.3 1.8 %shard_map.95.plane = bf16[512,96]{1,0:T(8,128)(2,1)S(1)} custom-call(bf16[96,512]{1,0:T(8,128)(2,1)S(1)} %get-tuple-element.32.plane, bf16[96,256]{1,0:T(8,128)(2,1)S(1)} %get-tuple-element.33.zed, bf16[768,768]{1,0:T(8,128)(2,1)S(1)} %copy-done.2, bf16[768,768]{1,0:T(8,128)(2,1)S(1)} %copy-done.5, f32[2,96,128]{2,1,0:T(8,128)S(1)} %get-tuple-element.20.refs_3_.mod, ...), custom_call_target="tpu_custom_call" | custom-call | tf_op jit(solution)/shard_map/pallas_call | solution.py:22
  27.1 0.0 collective-permute-done.3.from_chip
  27.1 1.3 %collective-permute-done.4.from_off = f32[96,128]{1,0:T(8,128)S(1)} collective-permute-done((f32[96,128]{1,0:T(8,128)S(1)}, f32[96,128]{1,0:T(8,128)S(1)}, u32[]{:S(2)}, u32[]{:S(2)}) %collective-permute-start.4) | collective-permute-done | bytes 49184 | tf_op jit(solution)/shard_map/ppermute | solution.py:301
  28.4 5.1 %shard_map.96 = bf16[1,2,3,384,816]{4,3,2,1,0:T(8,128)(2,1)S(1)} custom-call(f32[96,256]{1,0:T(8,128)S(1)} %get-tuple-element.29.field, f32[96,128]{1,0:T(8,128)S(1)} %collective-permute-done.3.from_chip, f32[96,128]{1,0:T(8,128)S(1)} %collective-permute-done.4.from_off, s32[2,6,8,128]{3,2,1,0:T(8,128)S(1)} %get-tuple-element.21.refs_4_.maps, ...), custom_call_target="tpu_custom_call" | custom-call | tf_op jit(solution)/shard_map/pallas_call | solution.py:22
  33.5 1.9 %copy-done.6 = bf16[1,2,3,384,816]{4,3,2,1,0:T(8,128)(2,1)} copy-done((bf16[1,2,3,384,816]{4,3,2,1,0:T(8,128)(2,1)}, bf16[1,2,3,384,816]{4,3,2,1,0:T(8,128)(2,1)S(1)}, u32[]{:S(2)}) %copy-start.6) | copy-done | bytes 3760152
  35.4 6.2 %copy.17 = bf16[1,2,3,384,816]{3,4,2,1,0:T(8,128)(2,1)} copy(bf16[1,2,3,384,816]{4,3,2,1,0:T(8,128)(2,1)} %copy-done.6) | data formatting | bytes 7520256 | tf_op jit(solution)/shard_map/pallas_call | solution.py:22
  (15 shorter events, 0.0 us)
Async XLA Ops:
  0.0 17.1 %copy-start.12 = (s32[3,16,2,3]{1,2,3,0:T(2,128)S(1)}, s32[3,16,2,3]{1,2,3,0:T(2,128)}, u32[]{:S(2)}) copy-start(s32[3,16,2,3]{1,2,3,0:T(2,128)} %param.16) | copy-start | bytes 3460
  0.0 10.1 %collective-permute-start = (bf16[48,768]{1,0:T(8,128)(2,1)}, bf16[48,768]{1,0:T(8,128)(2,1)S(1)}, u32[]{:S(2)}, u32[]{:S(2)}) collective-permute-start(bf16[48,768]{1,0:T(8,128)(2,1)} %bitcast.2), channel_id=1, source_target_pairs={{0,1},{1,0},{2,3},{3,2},{4,5},{5,4},{6,7},{7,6},{8,9},{9,8},{10,11... | collective-permute-start | bytes 221192 | tf_op jit(solution)/shard_map/ppermute | solution.py:293
  3.6 1.3 %copy-start = (bf16[768,768]{1,0:T(8,128)(2,1)S(1)}, bf16[768,768]{1,0:T(8,128)(2,1)}, u32[]{:S(2)}) copy-start(bf16[768,768]{1,0:T(8,128)(2,1)} %lam.5) | copy-start | bytes 3538948
  4.9 1.3 %copy-start.3 = (bf16[768,768]{1,0:T(8,128)(2,1)S(1)}, bf16[768,768]{1,0:T(8,128)(2,1)}, u32[]{:S(2)}) copy-start(bf16[768,768]{1,0:T(8,128)(2,1)} %mu.5) | copy-start | bytes 3538948
  6.1 0.9 %copy-start.9 = (bf16[1,2,3,8,768]{4,3,2,1,0:T(8,128)(2,1)S(1)}, bf16[1,2,3,8,768]{4,3,2,1,0:T(8,128)(2,1)}, u32[]{:S(2)}) copy-start(bf16[1,2,3,8,768]{4,3,2,1,0:T(8,128)(2,1)} %param.9) | copy-start | bytes 221188
  7.0 0.7 %copy-start.10 = (f32[16,15]{1,0:T(8,128)S(1)}, f32[16,15]{1,0:T(8,128)}, u32[]{:S(2)}) copy-start(f32[16,15]{1,0:T(8,128)} %nodes.1) | copy-start | bytes 2884
  7.7 0.7 %copy-start.11 = (f32[16]{0:T(128)S(1)}, f32[16]{0:T(128)}, u32[]{:S(2)}) copy-start(f32[16]{0:T(128)} %param.14) | copy-start | bytes 196
  8.4 8.9 %copy-start.2 = (bf16[768,768]{1,0:T(8,128)(2,1)S(1)}, bf16[768,768]{1,0:T(8,128)(2,1)}, u32[]{:S(2)}) copy-start(bf16[768,768]{1,0:T(8,128)(2,1)} %lam.5) | copy-start | bytes 3538948
  8.4 8.9 %copy-start.5 = (bf16[768,768]{1,0:T(8,128)(2,1)S(1)}, bf16[768,768]{1,0:T(8,128)(2,1)}, u32[]{:S(2)}) copy-start(bf16[768,768]{1,0:T(8,128)(2,1)} %mu.5) | copy-start | bytes 3538948
  9.2 1.0 %copy-start.7 = (bf16[6,96,816]{2,1,0:T(8,128)(2,1)}, bf16[6,96,816]{2,1,0:T(8,128)(2,1)S(1)}, u32[]{:S(2)}) copy-start(bf16[6,96,816]{2,1,0:T(8,128)(2,1)S(1)} %get-tuple-element.34.basis) | copy-start | bytes 2820100
  10.2 1.3 %copy-start.1 = (bf16[768,768]{1,0:T(8,128)(2,1)S(1)}, bf16[768,768]{1,0:T(8,128)(2,1)}, u32[]{:S(2)}) copy-start(bf16[768,768]{1,0:T(8,128)(2,1)} %lam.5) | copy-start | bytes 3538948
  11.4 1.3 %copy-start.4 = (bf16[768,768]{1,0:T(8,128)(2,1)S(1)}, bf16[768,768]{1,0:T(8,128)(2,1)}, u32[]{:S(2)}) copy-start(bf16[768,768]{1,0:T(8,128)(2,1)} %mu.5) | copy-start | bytes 3538948
  13.0 6.2 %collective-permute-start.1 = (f32[96,128]{1,0:T(8,128)S(1)}, f32[96,128]{1,0:T(8,128)S(1)}, u32[]{:S(2)}, u32[]{:S(2)}) collective-permute-start(f32[96,128]{1,0:T(8,128)S(1)} %get-tuple-element.24), channel_id=1, source_target_pairs={{0,2},{2,0},{4,6},{6,4},{8,10},{10,8},{12,14},{14,12},{16,18},{18,... | collective-permute-start | bytes 147464 | tf_op jit(solution)/shard_map/ppermute | solution.py:301
  14.1 6.3 %collective-permute-start.2 = (f32[96,128]{1,0:T(8,128)S(1)}, f32[96,128]{1,0:T(8,128)S(1)}, u32[]{:S(2)}, u32[]{:S(2)}) collective-permute-start(f32[96,128]{1,0:T(8,128)S(1)} %get-tuple-element.25), channel_id=1, source_target_pairs={{2,4},{6,8},{10,12},{14,16},{18,20},{22,24},{26,28},{4,2},{8,6},{1... | collective-permute-start | bytes 147464 | tf_op jit(solution)/shard_map/ppermute | solution.py:301
  17.2 11.1 %copy-start.8 = (bf16[6,96,816]{2,1,0:T(8,128)(2,1)S(1)}, bf16[6,96,816]{2,1,0:T(8,128)(2,1)}, u32[]{:S(2)}) copy-start(bf16[6,96,816]{2,1,0:T(8,128)(2,1)} %copy-done.7) | copy-start | bytes 2820100
  22.0 5.1 %collective-permute-start.3 = (f32[96,128]{1,0:T(8,128)S(1)}, f32[96,128]{1,0:T(8,128)S(1)}, u32[]{:S(2)}, u32[]{:S(2)}) collective-permute-start(f32[96,128]{1,0:T(8,128)S(1)} %get-tuple-element.30), channel_id=1, source_target_pairs={{0,2},{2,0},{4,6},{6,4},{8,10},{10,8},{12,14},{14,12},{16,18},{18,... | collective-permute-start | bytes 147464 | tf_op jit(solution)/shard_map/ppermute | solution.py:301
  22.1 6.3 %collective-permute-start.4 = (f32[96,128]{1,0:T(8,128)S(1)}, f32[96,128]{1,0:T(8,128)S(1)}, u32[]{:S(2)}, u32[]{:S(2)}) collective-permute-start(f32[96,128]{1,0:T(8,128)S(1)} %get-tuple-element.31), channel_id=1, source_target_pairs={{2,4},{6,8},{10,12},{14,16},{18,20},{22,24},{26,28},{4,2},{8,6},{1... | collective-permute-start | bytes 147464 | tf_op jit(solution)/shard_map/ppermute | solution.py:301
  33.5 1.9 %copy-start.6 = (bf16[1,2,3,384,816]{4,3,2,1,0:T(8,128)(2,1)}, bf16[1,2,3,384,816]{4,3,2,1,0:T(8,128)(2,1)S(1)}, u32[]{:S(2)}) copy-start(bf16[1,2,3,384,816]{4,3,2,1,0:T(8,128)(2,1)S(1)} %shard_map.96) | copy-start | bytes 11280388

commit v2 on v1

v2 whole, which is shorter than its diff:
```python
import functools

import jax
import jax.numpy as jnp
from jax import lax
from jax.experimental import pallas as pl
from jax.experimental.pallas import tpu as pltpu
from jax.sharding import PartitionSpec as P

F32 = jnp.float32
BF16 = jnp.bfloat16
VMEM = pl.BlockSpec(memory_space=pltpu.VMEM)
CHUNKS = 3
HBM = pl.BlockSpec(memory_space=pltpu.HBM)


def shaped(shape, dtype=F32):
    return jax.ShapeDtypeStruct(shape, dtype)


def call(body, outs, specs, args, flops=0, scratch=(), out_specs=None, grant=24 << 20, aliases=None):
    return pl.pallas_call(
        body,
        out_shape=outs,
        in_specs=specs,
        out_specs=[VMEM] * len(outs) if out_specs is None else out_specs,
        scratch_shapes=list(scratch),
        input_output_aliases=aliases or {},
        cost_estimate=pl.CostEstimate(flops=flops, bytes_accessed=0, transcendentals=0),
        compiler_params=pltpu.CompilerParams(vmem_limit_bytes=grant),
    )(*args)


def dot(a, b):
    return jnp.dot(a, b, preferred_element_type=F32)


def wide(column, width):
    return jnp.concatenate([column] * (width // 128), axis=1)


class Sizes:
    def __init__(self, trial, basis_size, parts):
        _, self.height, self.breadth, self.here, self.width = trial.shape
        self.face = self.width // 6
        self.subs = self.height * self.breadth
        self.parts = parts
        self.samples = self.here * parts
        self.rows = self.subs * self.samples
        self.plane = 4 * self.face
        self.terms = basis_size
        self.share = self.width // parts

    def own(self, n, part):
        return pl.ds(pl.multiple_of(n * self.samples + part * self.here, 8), self.here)

    def block(self, n):
        return slice(n * self.samples, (n + 1) * self.samples)

    def group(self, n):
        return slice(n * self.here, (n + 1) * self.here)


def load(d, lam, mu, lam_here, mu_here, sems):
    copies = [
        pltpu.make_async_copy(lam, lam_here, sems.at[0]),
        pltpu.make_async_copy(mu, mu_here, sems.at[1]),
    ]
    for copy in copies:
        copy.start()
    for copy in copies:
        copy.wait()


def prepare(d, trial, lam, mu, modes, nodes, faces, mod, maps, first, second):
    first[...] = dot(trial[...], lam[...])
    second[...] = dot(trial[...], mu[...])
    points = nodes[...]
    for c in range(2):
        for n in range(d.subs):
            row = modes[c, 0, n % d.breadth, pl.ds(n // d.breadth, 1), :]
            total = jnp.exp(jnp.sum(points * row, axis=1, keepdims=True))
            mod[c, d.block(n), :] = jnp.broadcast_to(total, (d.samples, 128))
    target = lax.broadcasted_iota(jnp.int32, (d.face, d.face), 0)
    source = lax.broadcasted_iota(jnp.int32, (8, d.face), 1).astype(F32).astype(BF16)
    for n in range(d.subs):
        row = faces[0, n % d.breadth, pl.ds(n // d.breadth, 1), :]
        hit = jnp.where(row == target, 1.0, 0.0).astype(BF16)
        back = lax.dot_general(
            source, hit, (((1,), (1,)), ((), ())), preferred_element_type=F32
        )
        maps[0, n] = jnp.broadcast_to(row, (8, d.face))
        maps[1, n] = back.astype(jnp.int32)


def tables(d, nodes, weights, chaos, bonds, basis, masks):
    points = nodes[...]
    layer = lax.axis_index("sub")
    lane = lax.broadcasted_iota(jnp.int32, (d.height, bonds.shape[-1]), 1)

    def at(axis, x, z):
        picked = jnp.where(lane == z, bonds[axis, x].astype(F32), 0.0)
        return jnp.sum(picked, axis=1, keepdims=True)

    along = [[at(axis, x, layer) for x in range(d.breadth)] for axis in range(3)]
    under = [at(2, x, layer - 1) for x in range(d.breadth)]
    for n in range(d.subs):
        y, x = divmod(n, d.breadth)
        columns = [
            (along[0][(x - 1) % d.breadth], y),
            (along[0][x], y),
            (along[1][x], (y - 1) % d.height),
            (along[1][x], y),
            (under[x], y),
            (along[2][x], y),
        ]
        for which, (column, at_y) in enumerate(columns):
            masks[which, n] = jnp.broadcast_to(column[at_y : at_y + 1], (8, 128))
    one = jnp.sqrt(3.0) * points
    two = jnp.sqrt(5.0) * (1.5 * points * points - 0.5)
    three = jnp.sqrt(7.0) * (2.5 * points * points * points - 1.5 * points)
    total = jnp.ones((d.samples, d.terms), F32)
    for k in range(points.shape[1]):
        c = chaos[k : k + 1, :]
        high = jnp.where(c == 3, three[:, k : k + 1], two[:, k : k + 1])
        low = jnp.where(c == 1, one[:, k : k + 1], 1.0)
        total = total * jnp.where(c >= 2, high, low)
    square = (d.samples, d.samples)
    diagonal = lax.broadcasted_iota(jnp.int32, square, 0) == lax.broadcasted_iota(
        jnp.int32, square, 1
    )
    column = jnp.sum(jnp.where(diagonal, weights[...], 0.0), axis=1, keepdims=True)
    basis[...] = (column * total).T.astype(BF16)


def payloads(d, low, high, maps, on_chip, off_chip):
    even = lax.rem(lax.axis_index("sub"), 2) == 0
    for n in range(d.subs):
        back = maps[1, n]
        for start in range(n * d.samples, (n + 1) * d.samples, 8):
            rows = slice(start, start + 8)
            minus = low[rows]
            pushed = jnp.take_along_axis(high[rows], back, axis=1, mode="promise_in_bounds")
            on_chip[rows, :] = jnp.where(even, pushed, minus)
            off_chip[rows, :] = jnp.where(even, minus, pushed)


def part_of(d, shift):
    here = lax.axis_index("smp")
    return lax.rem(here - shift + d.parts, d.parts)


def combine(d, mod, part, first, second, field):
    width = field.shape[1]
    for n in range(d.subs):
        own = d.own(n, part)
        field[own, :] = (
            wide(mod[0, own, :], width) * first[d.group(n), :]
            + wide(mod[1, own, :], width) * second[d.group(n), :]
        )


def first_z(d, *refs):
    others = refs[: d.parts - 1]
    lam, mu, mod, maps, own_lam, own_mu, field, on_chip, off_chip = refs[d.parts - 1 :]
    at = slice(d.plane, d.width)
    combine(d, mod, lax.axis_index("smp"), own_lam.at[:, at], own_mu.at[:, at], field)
    for shift, other in enumerate(others, 1):
        rows = other[...]
        combine(d, mod, part_of(d, shift), dot(rows, lam[:, at]), dot(rows, mu[:, at]), field)
    payloads(d, field[:, : d.face], field[:, d.face :], maps, on_chip, off_chip)


def plane_jumps(d, field, masks, out):
    def mask(which, n):
        return jnp.concatenate([masks[which, n]] * (d.samples // 8), axis=0)

    for n in range(d.subs):
        y, x = divmod(n, d.breadth)
        left = y * d.breadth + (x - 1) % d.breadth
        right = y * d.breadth + (x + 1) % d.breadth
        front = (y - 1) % d.height * d.breadth + x
        behind = (y + 1) % d.height * d.breadth + x

        def face(which, m):
            return field[d.block(m), which * d.face : (which + 1) * d.face]

        out(0, n, mask(0, n) * (face(0, n) - face(1, left)))
        out(1, n, mask(1, n) * (face(1, n) - face(0, right)))
        out(2, n, mask(2, n) * (face(2, n) - face(3, front)))
        out(3, n, mask(3, n) * (face(3, n) - face(2, behind)))


def z_jumps(d, field, from_chip, from_off, maps, masks, out):
    even = lax.rem(lax.axis_index("sub"), 2) == 0
    for n in range(d.subs):
        for start in range(n * d.samples, (n + 1) * d.samples, 8):
            rows = slice(start, start + 8)
            near, far = from_chip[rows, :], from_off[rows, :]
            above = jnp.where(even, near, far)
            below = jnp.where(even, far, near)
            matched = jnp.take_along_axis(above, maps[0, n], axis=1, mode="promise_in_bounds")
            out(0, rows, masks[4, n] * (field[rows, : d.face] - below))
            out(1, rows, masks[5, n] * (field[rows, d.face :] - matched))


def first_plane(d, *refs):
    others = refs[: d.parts - 1]
    lam, mu, mod, own_lam, own_mu, masks, jumps, part_lam, part_mu, field = refs[d.parts - 1 :]
    at = slice(0, d.plane)
    combine(d, mod, lax.axis_index("smp"), own_lam.at[:, at], own_mu.at[:, at], field)
    for shift, other in enumerate(others, 1):
        rows = other[...]
        combine(d, mod, part_of(d, shift), dot(rows, lam[:, at]), dot(rows, mu[:, at]), field)

    def put(which, n, value):
        jumps[d.block(n), which * d.face : (which + 1) * d.face] = value.astype(BF16)

    plane_jumps(d, field, masks, put)
    part_lam[...] = dot(jumps[...], lam[: d.plane, d.plane :])
    part_mu[...] = dot(jumps[...], mu[: d.plane, d.plane :])


def second_z(
    d, field, from_chip, from_off, maps, masks, mod, lam, mu, part_lam, part_mu,
    jumps, result, on_chip, off_chip, held,
):
    def put(which, rows, value):
        held[rows, which * d.face : (which + 1) * d.face] = value

    z_jumps(d, field, from_chip, from_off, maps, masks, put)
    rounded = held[...].astype(BF16)
    jumps[...] = rounded
    one = part_lam[...] + dot(rounded, lam[d.plane :, d.plane :])
    two = part_mu[...] + dot(rounded, mu[d.plane :, d.plane :])
    result[...] = wide(mod[0], 2 * d.face) * one + wide(mod[1], 2 * d.face) * two
    payloads(d, result[:, : d.face], result[:, d.face :], maps, on_chip, off_chip)


def second_plane(d, plane, zed, lam, mu, mod, masks, jumps):
    one = dot(plane[...], lam[: d.plane, : d.plane]) + dot(zed[...], lam[d.plane :, : d.plane])
    two = dot(plane[...], mu[: d.plane, : d.plane]) + dot(zed[...], mu[d.plane :, : d.plane])
    field = wide(mod[0], d.plane) * one + wide(mod[1], d.plane) * two

    def put(which, n, value):
        jumps[d.block(n), which * d.face : (which + 1) * d.face] = value.astype(BF16)

    plane_jumps(d, field, masks, put)


def last_z(d, field, from_chip, from_off, maps, masks, plane, jumps, held):
    def put(which, rows, value):
        held[rows, which * d.face : (which + 1) * d.face] = value

    z_jumps(d, field, from_chip, from_off, maps, masks, put)
    jumps[:, : d.plane] = plane[...]
    jumps[:, d.plane :] = held[...].astype(BF16)


def project_rows(d, picks, lanes, basis, out, rows_out, sems):
    width = lanes.stop - lanes.start
    group = max(g for g in (1, 2, 3, 6) if d.subs % g == 0 and g * width <= 768)
    chunk = d.terms // CHUNKS
    copies = []
    for n in range(0, d.subs, group):
        right = picks[n : n + group]
        right = right[0] if group == 1 else jnp.concatenate(right, axis=1)
        for c in range(CHUNKS):
            rows = slice(c * chunk, (c + 1) * chunk)
            value = dot(basis[rows, :], right)
            for m in range(group):
                rows_out[n + m, rows, :] = value[:, m * width : (m + 1) * width].astype(BF16)
                y, x = divmod(n + m, d.breadth)
                copy = pltpu.make_async_copy(
                    rows_out.at[n + m, rows, :],
                    out.at[0, y, x, rows, lanes],
                    sems.at[n + m, c],
                )
                copy.start()
                copies.append(copy)
    for copy in copies:
        copy.wait()


def project_early(d, plane, basis, out, rows_out, sems):
    start = pl.multiple_of(lax.axis_index("smp") * d.share, 128)
    picks = [plane[d.block(n), pl.ds(start, d.face)] for n in range(d.subs)]
    project_rows(d, picks, slice(0, d.face), basis, out, rows_out, sems)


def project_late(
    d, field, from_chip, from_off, maps, masks, plane, basis, early, out, held, jumps, rows_out, sems
):
    last_z(d, field, from_chip, from_off, maps, masks, plane, jumps, held)
    width = d.share - d.face
    start = pl.multiple_of(lax.axis_index("smp") * d.share + d.face, 128)
    picks = [jumps[d.block(n), pl.ds(start, width)] for n in range(d.subs)]
    project_rows(d, picks, slice(d.face, d.share), basis, out, rows_out, sems)


def project_share(d, jumps, basis, out, rows_out, sems):
    picks = [jumps[d.block(n), :] for n in range(d.subs)]
    project_rows(d, picks, slice(0, d.share), basis, out, rows_out, sems)


def per_device(
    trial, stiff_lam, stiff_mu, log_modes, nodes, quad_weights, chaos_index, bonds, face_map
):
    parts = lax.axis_size("smp")
    layers = lax.axis_size("sub")
    d = Sizes(trial, chaos_index.shape[0], parts)
    rows, face = d.rows, d.face
    own = trial.reshape(d.subs * d.here, d.width)
    others = [
        lax.ppermute(own, "smp", [(i, (i + shift) % parts) for i in range(parts)])
        for shift in range(1, parts)
    ]
    pairs = [(i, i ^ 1) for i in range(layers)]
    ends = [(i, i + 1) for i in range(1, layers - 1, 2)]
    ends = ends + [(j, i) for i, j in ends]

    def exchange(on_chip, off_chip):
        far = lax.ppermute(off_chip, "sub", ends)
        return lax.ppermute(on_chip, "sub", pairs), far

    def run(body, *args, **options):
        return call(functools.partial(body, d), *args, **options)

    product = shaped((d.subs * d.here, d.width))
    lam, mu = run(
        load,
        [shaped(stiff_lam.shape, BF16), shaped(stiff_mu.shape, BF16)],
        [HBM] * 2,
        [stiff_lam, stiff_mu],
        scratch=[pltpu.SemaphoreType.DMA((2,))],
        grant=51 << 20,
    )
    mod, maps, own_lam, own_mu = run(
        prepare,
        [shaped((2, rows, 128)), shaped((2, d.subs, 8, face), jnp.int32), product, product],
        [VMEM] * 6,
        [
            own, lam, mu,
            log_modes.transpose(0, 1, 3, 2, 4), nodes, face_map.transpose(0, 2, 1, 3),
        ],
    )
    field, on_chip, off_chip = run(
        first_z,
        [shaped((rows, 2 * face)), shaped((rows, face)), shaped((rows, face))],
        [VMEM] * (parts + 5),
        [*others, lam, mu, mod, maps, own_lam, own_mu],
    )
    near, far = exchange(on_chip, off_chip)
    basis, masks = run(
        tables,
        [shaped((d.terms, d.samples), BF16), shaped((6, d.subs, 8, 128))],
        [VMEM] * 4,
        [nodes, quad_weights.reshape(1, -1), chaos_index.T, bonds.transpose(0, 3, 2, 1)],
    )
    jumps_plane, part_lam, part_mu = run(
        first_plane,
        [shaped((rows, d.plane), BF16), shaped((rows, 2 * face)), shaped((rows, 2 * face))],
        [VMEM] * (parts + 5),
        [*others, lam, mu, mod, own_lam, own_mu, masks],
        scratch=[pltpu.VMEM((rows, d.plane), F32)],
    )
    jumps_z, field, on_chip, off_chip = run(
        second_z,
        [
            shaped((rows, 2 * face), BF16),
            shaped((rows, 2 * face)),
            shaped((rows, face)),
            shaped((rows, face)),
        ],
        [VMEM] * 10,
        [field, near, far, maps, masks, mod, lam, mu, part_lam, part_mu],
        scratch=[pltpu.VMEM((rows, 2 * face), F32)],
    )
    near, far = exchange(on_chip, off_chip)
    (plane,) = run(
        second_plane,
        [shaped((rows, d.plane), BF16)],
        [VMEM] * 6,
        [jumps_plane, jumps_z, lam, mu, mod, masks],
    )
    last = [field, near, far, maps, masks, plane]
    held = pltpu.VMEM((rows, 2 * face), F32)
    result = [shaped((1, d.height, d.breadth, d.terms, d.share), BF16)]

    def buffers(width):
        return [
            pltpu.VMEM((d.subs, d.terms, width), BF16),
            pltpu.SemaphoreType.DMA((d.subs, CHUNKS)),
        ]

    if d.share == 3 * face:
        (early,) = run(
            project_early,
            result,
            [VMEM] * 2,
            [plane, basis],
            out_specs=[HBM],
            scratch=buffers(face),
        )
        (out,) = run(
            project_late,
            result,
            [VMEM] * 7 + [HBM],
            [*last, basis, early],
            out_specs=[HBM],
            scratch=[held, pltpu.VMEM((rows, d.width), BF16)] + buffers(2 * face),
            aliases={7: 0},
        )
    else:
        (jumps,) = run(last_z, [shaped((rows, d.width), BF16)], [VMEM] * 6, last, scratch=[held])
        start = lax.axis_index("smp") * d.share
        jumps = lax.dynamic_slice_in_dim(jumps, start, d.share, 1)
        (out,) = run(
            project_share, result, [VMEM] * 2, [jumps, basis], out_specs=[HBM], scratch=buffers(d.share)
        )
    return jnp.swapaxes(out, -1, -2)


def solution(mesh):
    return jax.shard_map(
        per_device,
        mesh=mesh,
        in_specs=(
            P("sub", None, None, "smp", None),
            P(),
            P(),
            P(None, "sub", None, None, None),
            P(),
            P(),
            P(),
            P(),
            P("sub", None, None, None),
        ),
        out_specs=P("sub", None, None, "smp", None),
        check_vma=False,
    )
```

time: 42.2 us -> 20.8 us (0.49)
  the two profiles are of different devices: /device:TPU:13 before, /device:TPU:5 now
where the time goes in v2:
time: 20.8 us; the launch traced here: 20.6 us
  starting transfers between devices  9.3 us (45%)
  Pallas kernels  7.7 us (37%)
  waiting for transfers between devices  3.43 us (16%)
    pallas_call x9, Pallas kernels, call(): pl.pallas_call(body, out_shape=outs, in_specs=specs, out_specs=[VMEM] * l...  7.7 us
    ppermute x2, starting transfers between devices, exchange(): far = lax.ppermute(off_chip, 'sub', ends)  6.21 us
    ppermute x2, waiting for transfers between devices, exchange(): far = lax.ppermute(off_chip, 'sub', ends)  3.42 us
    ppermute x2, starting transfers between devices, exchange(): return (lax.ppermute(on_chip, 'sub', pairs), far)  1.82 us
    ppermute x1, starting transfers between devices, per_device(): lax.ppermute(own, 'smp', [(i, (i + shift) % parts) for i in range(parts)])  1.28 us
  transfers between devices with their start and end apart: 5, of which 2 were waited for; matrix products, arithmetic and copies ran while one was open for 0% of the time, Pallas kernels for 25%

profile of v2, /device:TPU:5, one launch (start us, length us, event | category | flops | bytes accessed | tf_op | source)
XLA Modules:
  0.0 20.6 jit_solution(10618928859807983173)
XLA Ops:
  0.0 0.0 copy-start
  0.0 0.0 copy-start.2
  0.0 0.0 copy-start.4
  0.0 0.0 copy-start.5
  0.0 1.3 %collective-permute-start = (bf16[48,768]{1,0:T(8,128)(2,1)}, bf16[48,768]{1,0:T(8,128)(2,1)S(1)}, u32[]{:S(2)}, u32[]{:S(2)}) collective-permute-start(bf16[48,768]{1,0:T(8,128)(2,1)} %bitcast.7), channel_id=1, source_target_pairs={{0,1},{1,0},{2,3},{3,2},{4,5},{5,4},{6,7},{7,6},{8,9},{9,8},{10,11... | collective-permute-start | bytes 221192 | tf_op jit(solution)/shard_map/ppermute | solution.py:315
  1.3 1.6 %shard_map.91 = (bf16[768,768]{1,0:T(8,128)(2,1)S(1)}, bf16[768,768]{1,0:T(8,128)(2,1)S(1)}) custom-call(bf16[768,768]{1,0:T(8,128)(2,1)} %lam.1, bf16[768,768]{1,0:T(8,128)(2,1)} %mu.1), custom_call_target="tpu_custom_call" | custom-call | tf_op jit(solution)/shard_map/pallas_call | solution.py:22
  2.9 0.0 copy-done
  3.0 0.0 copy-done.2
  3.0 0.0 copy-done.4
  3.0 0.0 copy-done.5
  3.0 0.6 %shard_map.92 = (f32[2,96,128]{2,1,0:T(8,128)S(1)}, s32[2,6,8,128]{3,2,1,0:T(8,128)S(1)}, f32[48,768]{1,0:T(8,128)S(1)}, f32[48,768]{1,0:T(8,128)S(1)}) custom-call(bf16[48,768]{1,0:T(8,128)(2,1)S(1)} %bitcast.8, bf16[768,768]{1,0:T(8,128)(2,1)S(1)} %get-tuple-element.23.lam.refs_1_, bf16[768,768]{1,0:T(8,128)(2,1)S(1)} %get-tuple-element.24.mu.refs_2_, ...), custom_call_target="tpu_custom_call" | custom-call | tf_op jit(solution)/shard_map/pallas_call | solution.py:22
  3.6 0.0 collective-permute-done.refs_0_
  3.6 0.0 copy-start.3
  3.6 0.0 copy-start.6
  3.6 0.3 %shard_map.93 = (f32[96,256]{1,0:T(8,128)S(1)}, f32[96,128]{1,0:T(8,128)S(1)}, f32[96,128]{1,0:T(8,128)S(1)}) custom-call(bf16[48,768]{1,0:T(8,128)(2,1)S(1)} %collective-permute-done.refs_0_, bf16[768,768]{1,0:T(8,128)(2,1)S(1)} %get-tuple-element.23.lam.refs_1_, bf16[768,768]{1,0:T(8,128)(2,1)S(1)} %get-tuple-element.24.mu.refs_2_, ...), custom_call_target="tpu_custom_call" | custom-call | tf_op jit(solution)/shard_map/pallas_call | solution.py:22
  4.0 1.7 %collective-permute-start.1 = (f32[96,128]{1,0:T(8,128)S(1)}, f32[96,128]{1,0:T(8,128)S(1)}, u32[]{:S(2)}, u32[]{:S(2)}) collective-permute-start(f32[96,128]{1,0:T(8,128)S(1)} %get-tuple-element.30), channel_id=1, source_target_pairs={{0,2},{2,0},{4,6},{6,4},{8,10},{10,8},{12,14},{14,12},{16,18},{18,... | collective-permute-start | bytes 147464 | tf_op jit(solution)/shard_map/ppermute | solution.py:324
  5.7 3.0 %collective-permute-start.2 = (f32[96,128]{1,0:T(8,128)S(1)}, f32[96,128]{1,0:T(8,128)S(1)}, u32[]{:S(2)}, u32[]{:S(2)}) collective-permute-start(f32[96,128]{1,0:T(8,128)S(1)} %get-tuple-element.31), channel_id=1, source_target_pairs={{2,4},{6,8},{10,12},{14,16},{18,20},{22,24},{26,28},{4,2},{8,6},{1... | collective-permute-start | bytes 147464 | tf_op jit(solution)/shard_map/ppermute | solution.py:323
  8.8 0.0 copy-done.1
  8.8 0.0 copy-done.3
  8.8 0.0 copy-done.6
  8.8 0.5 %shard_map.94 = (bf16[816,16]{1,0:T(8,128)(2,1)S(1)}, f32[6,6,8,128]{3,2,1,0:T(8,128)S(1)}) custom-call(f32[16,15]{1,0:T(8,128)S(1)} %copy-done.2, f32[1,16]{1,0:T(1,128)S(1)} %bitcast.13, s32[15,816]{1,0:T(8,128)S(1)} %bitcast.9, s32[3,3,2,16]{3,2,1,0:T(2,128)S(1)} %bitcast.10), custom_call_target="tpu_custom_call" | custom-call | tf_op jit(solution)/shard_map/pallas_call | solution.py:22
  9.3 0.6 %shard_map.95 = (bf16[96,512]{1,0:T(8,128)(2,1)S(1)}, f32[96,256]{1,0:T(8,128)S(1)}, f32[96,256]{1,0:T(8,128)S(1)}) custom-call(bf16[48,768]{1,0:T(8,128)(2,1)S(1)} %collective-permute-done.refs_0_, bf16[768,768]{1,0:T(8,128)(2,1)S(1)} %get-tuple-element.23.lam.refs_1_, bf16[768,768]{1,0:T(8,128)(2,1)S(1)} %get-tuple-element.24.mu.refs_2_, ...), custom_call_target="tpu_custom_call" | custom-call | tf_op jit(solution)/shard_map/pallas_call | solution.py:22
  9.9 0.0 collective-permute-done.1.from_chip
  9.9 2.1 %collective-permute-done.2.from_off = f32[96,128]{1,0:T(8,128)S(1)} collective-permute-done((f32[96,128]{1,0:T(8,128)S(1)}, f32[96,128]{1,0:T(8,128)S(1)}, u32[]{:S(2)}, u32[]{:S(2)}) %collective-permute-start.2) | collective-permute-done | bytes 49184 | tf_op jit(solution)/shard_map/ppermute | solution.py:323
  12.0 0.3 %shard_map.96 = (bf16[96,256]{1,0:T(8,128)(2,1)S(1)}, f32[96,256]{1,0:T(8,128)S(1)}, f32[96,128]{1,0:T(8,128)S(1)}, f32[96,128]{1,0:T(8,128)S(1)}) custom-call(f32[96,256]{1,0:T(8,128)S(1)} %get-tuple-element.29.field, f32[96,128]{1,0:T(8,128)S(1)} %collective-permute-done.1.from_chip, f32[96,128]{1,0:T(8,128)S(1)} %collective-permute-done.2.from_off, ...), custom_call_target="tpu_custom_call" | custom-call | tf_op jit(solution)/shard_map/pallas_call | solution.py:22
  12.3 0.1 collective-permute-start.3
  12.4 3.2 %collective-permute-start.4 = (f32[96,128]{1,0:T(8,128)S(1)}, f32[96,128]{1,0:T(8,128)S(1)}, u32[]{:S(2)}, u32[]{:S(2)}) collective-permute-start(f32[96,128]{1,0:T(8,128)S(1)} %get-tuple-element.37), channel_id=1, source_target_pairs={{2,4},{6,8},{10,12},{14,16},{18,20},{22,24},{26,28},{4,2},{8,6},{1... | collective-permute-start | bytes 147464 | tf_op jit(solution)/shard_map/ppermute | solution.py:323
  15.6 0.4 %shard_map.97.plane = bf16[96,512]{1,0:T(8,128)(2,1)S(1)} custom-call(bf16[96,512]{1,0:T(8,128)(2,1)S(1)} %get-tuple-element.38.plane, bf16[96,256]{1,0:T(8,128)(2,1)S(1)} %get-tuple-element.39.zed, bf16[768,768]{1,0:T(8,128)(2,1)S(1)} %get-tuple-element.23.lam.refs_1_, bf16[768,768]{1,0:T(8,128)(2,1)S(1)} %get-tuple-element.24.mu.refs_2_, ...), custom_call_target="tpu_custom_call" | custom-call | tf_op jit(solution)/shard_map/pallas_call | solution.py:22
  16.0 1.4 %shard_map.98.early = bf16[1,2,3,816,384]{4,3,2,1,0:T(8,128)(2,1)} custom-call(bf16[96,512]{1,0:T(8,128)(2,1)S(1)} %shard_map.97.plane, bf16[816,16]{1,0:T(8,128)(2,1)S(1)} %get-tuple-element.40.basis), custom_call_target="tpu_custom_call" | custom-call | tf_op jit(solution)/shard_map/pallas_call | solution.py:22
  17.4 0.0 collective-permute-done.3.from_chip
  17.4 1.3 %collective-permute-done.4.from_off = f32[96,128]{1,0:T(8,128)S(1)} collective-permute-done((f32[96,128]{1,0:T(8,128)S(1)}, f32[96,128]{1,0:T(8,128)S(1)}, u32[]{:S(2)}, u32[]{:S(2)}) %collective-permute-start.4) | collective-permute-done | bytes 49184 | tf_op jit(solution)/shard_map/ppermute | solution.py:323
  18.7 1.9 %shard_map.99 = bf16[1,2,3,816,384]{4,3,2,1,0:T(8,128)(2,1)} custom-call(f32[96,256]{1,0:T(8,128)S(1)} %get-tuple-element.35.field, f32[96,128]{1,0:T(8,128)S(1)} %collective-permute-done.3.from_chip, f32[96,128]{1,0:T(8,128)S(1)} %collective-permute-done.4.from_off, ...), custom_call_target="tpu_custom_call", output_to_operand_aliasing={{}: (7, {})} | custom-call | tf_op jit(solution)/shard_map/pallas_call | solution.py:22
  (1 shorter events, 0.0 us)
Async XLA Ops:
  0.0 2.9 %copy-start = (bf16[1,2,3,8,768]{4,3,2,1,0:T(8,128)(2,1)S(1)}, bf16[1,2,3,8,768]{4,3,2,1,0:T(8,128)(2,1)}, u32[]{:S(2)}) copy-start(bf16[1,2,3,8,768]{4,3,2,1,0:T(8,128)(2,1)} %param.9) | copy-start | bytes 221188
  0.0 3.0 %copy-start.2 = (f32[16,15]{1,0:T(8,128)S(1)}, f32[16,15]{1,0:T(8,128)}, u32[]{:S(2)}) copy-start(f32[16,15]{1,0:T(8,128)} %nodes.3) | copy-start | bytes 2884
  0.0 3.0 %copy-start.4 = (f32[2,1,2,3,15]{4,2,3,1,0:T(2,128)S(1)}, f32[2,1,2,3,15]{4,2,3,1,0:T(2,128)}, u32[]{:S(2)}) copy-start(f32[2,1,2,3,15]{4,2,3,1,0:T(2,128)} %param.12) | copy-start | bytes 2164
  0.0 3.0 %copy-start.5 = (s32[1,2,3,128]{3,1,2,0:T(2,128)S(1)}, s32[1,2,3,128]{3,1,2,0:T(2,128)}, u32[]{:S(2)}) copy-start(s32[1,2,3,128]{3,1,2,0:T(2,128)} %param.17) | copy-start | bytes 9220
  0.0 3.6 %collective-permute-start = (bf16[48,768]{1,0:T(8,128)(2,1)}, bf16[48,768]{1,0:T(8,128)(2,1)S(1)}, u32[]{:S(2)}, u32[]{:S(2)}) collective-permute-start(bf16[48,768]{1,0:T(8,128)(2,1)} %bitcast.7), channel_id=1, source_target_pairs={{0,1},{1,0},{2,3},{3,2},{4,5},{5,4},{6,7},{7,6},{8,9},{9,8},{10,11... | collective-permute-start | bytes 221192 | tf_op jit(solution)/shard_map/ppermute | solution.py:315
  3.6 5.2 %copy-start.1 = (s32[816,15]{0,1:T(8,128)S(1)}, s32[816,15]{0,1:T(8,128)}, u32[]{:S(2)}) copy-start(s32[816,15]{0,1:T(8,128)} %param.15) | copy-start | bytes 146884
  3.6 5.2 %copy-start.3 = (s32[3,16,2,3]{1,2,3,0:T(2,128)S(1)}, s32[3,16,2,3]{1,2,3,0:T(2,128)}, u32[]{:S(2)}) copy-start(s32[3,16,2,3]{1,2,3,0:T(2,128)} %param.16) | copy-start | bytes 3460
  3.6 5.2 %copy-start.6 = (f32[16]{0:T(128)S(1)}, f32[16]{0:T(128)}, u32[]{:S(2)}) copy-start(f32[16]{0:T(128)} %param.14) | copy-start | bytes 196
  4.0 6.0 %collective-permute-start.1 = (f32[96,128]{1,0:T(8,128)S(1)}, f32[96,128]{1,0:T(8,128)S(1)}, u32[]{:S(2)}, u32[]{:S(2)}) collective-permute-start(f32[96,128]{1,0:T(8,128)S(1)} %get-tuple-element.30), channel_id=1, source_target_pairs={{0,2},{2,0},{4,6},{6,4},{8,10},{10,8},{12,14},{14,12},{16,18},{18,... | collective-permute-start | bytes 147464 | tf_op jit(solution)/shard_map/ppermute | solution.py:324
  5.7 6.3 %collective-permute-start.2 = (f32[96,128]{1,0:T(8,128)S(1)}, f32[96,128]{1,0:T(8,128)S(1)}, u32[]{:S(2)}, u32[]{:S(2)}) collective-permute-start(f32[96,128]{1,0:T(8,128)S(1)} %get-tuple-element.31), channel_id=1, source_target_pairs={{2,4},{6,8},{10,12},{14,16},{18,20},{22,24},{26,28},{4,2},{8,6},{1... | collective-permute-start | bytes 147464 | tf_op jit(solution)/shard_map/ppermute | solution.py:323
  12.3 5.0 %collective-permute-start.3 = (f32[96,128]{1,0:T(8,128)S(1)}, f32[96,128]{1,0:T(8,128)S(1)}, u32[]{:S(2)}, u32[]{:S(2)}) collective-permute-start(f32[96,128]{1,0:T(8,128)S(1)} %get-tuple-element.36), channel_id=1, source_target_pairs={{0,2},{2,0},{4,6},{6,4},{8,10},{10,8},{12,14},{14,12},{16,18},{18,... | collective-permute-start | bytes 147464 | tf_op jit(solution)/shard_map/ppermute | solution.py:324
  12.4 6.3 %collective-permute-start.4 = (f32[96,128]{1,0:T(8,128)S(1)}, f32[96,128]{1,0:T(8,128)S(1)}, u32[]{:S(2)}, u32[]{:S(2)}) collective-permute-start(f32[96,128]{1,0:T(8,128)S(1)} %get-tuple-element.37), channel_id=1, source_target_pairs={{2,4},{6,8},{10,12},{14,16},{18,20},{22,24},{26,28},{4,2},{8,6},{1... | collective-permute-start | bytes 147464 | tf_op jit(solution)/shard_map/ppermute | solution.py:323

commit v3 on v2

--- a/solution.py
+++ b/solution.py
@@ -191,7 +191,7 @@
         out(3, n, mask(3, n) * (face(3, n) - face(2, behind)))
 
 
-def z_jumps(d, field, from_chip, from_off, maps, masks, out):
+def z_jumps(d, field, from_off, from_chip, maps, masks, out):
     even = lax.rem(lax.axis_index("sub"), 2) == 0
     for n in range(d.subs):
         for start in range(n * d.samples, (n + 1) * d.samples, 8):
@@ -222,13 +222,13 @@
 
 
 def second_z(
-    d, field, from_chip, from_off, maps, masks, mod, lam, mu, part_lam, part_mu,
+    d, field, from_off, from_chip, maps, masks, mod, lam, mu, part_lam, part_mu,
     jumps, result, on_chip, off_chip, held,
 ):
     def put(which, rows, value):
         held[rows, which * d.face : (which + 1) * d.face] = value
 
-    z_jumps(d, field, from_chip, from_off, maps, masks, put)
+    z_jumps(d, field, from_off, from_chip, maps, masks, put)
     rounded = held[...].astype(BF16)
     jumps[...] = rounded
     one = part_lam[...] + dot(rounded, lam[d.plane :, d.plane :])
@@ -248,11 +248,11 @@
     plane_jumps(d, field, masks, put)
 
 
-def last_z(d, field, from_chip, from_off, maps, masks, plane, jumps, held):
+def last_z(d, field, from_off, from_chip, maps, masks, plane, jumps, held):
     def put(which, rows, value):
         held[rows, which * d.face : (which + 1) * d.face] = value
 
-    z_jumps(d, field, from_chip, from_off, maps, masks, put)
+    z_jumps(d, field, from_off, from_chip, maps, masks, put)
     jumps[:, : d.plane] = plane[...]
     jumps[:, d.plane :] = held[...].astype(BF16)
 
@@ -289,9 +289,9 @@
 
 
 def project_late(
-    d, field, from_chip, from_off, maps, masks, plane, basis, early, out, held, jumps, rows_out, sems
+    d, field, from_off, from_chip, maps, masks, plane, basis, early, out, held, jumps, rows_out, sems
 ):
-    last_z(d, field, from_chip, from_off, maps, masks, plane, jumps, held)
+    last_z(d, field, from_off, from_chip, maps, masks, plane, jumps, held)
     width = d.share - d.face
     start = pl.multiple_of(lax.axis_index("smp") * d.share + d.face, 128)
     picks = [jumps[d.block(n), pl.ds(start, width)] for n in range(d.subs)]
@@ -373,7 +373,7 @@
             shaped((rows, face)),
         ],
         [VMEM] * 10,
-        [field, near, far, maps, masks, mod, lam, mu, part_lam, part_mu],
+        [field, far, near, maps, masks, mod, lam, mu, part_lam, part_mu],
         scratch=[pltpu.VMEM((rows, 2 * face), F32)],
     )
     near, far = exchange(on_chip, off_chip)
@@ -383,7 +383,7 @@
         [VMEM] * 6,
         [jumps_plane, jumps_z, lam, mu, mod, masks],
     )
-    last = [field, near, far, maps, masks, plane]
+    last = [field, far, near, maps, masks, plane]
     held = pltpu.VMEM((rows, 2 * face), F32)
     result = [shaped((1, d.height, d.breadth, d.terms, d.share), BF16)]
 

time: 20.8 us -> 20.2 us (0.971)
  the two profiles are of different devices: /device:TPU:5 before, /device:TPU:10 now
where the time goes in v3:
time: 20.2 us; the launch traced here: 19.8 us
  Pallas kernels  7.71 us (38%)
  starting transfers between devices  7.44 us (37%)
  waiting for transfers between devices  4.55 us (23%)
    pallas_call x9, Pallas kernels, call(): pl.pallas_call(body, out_shape=outs, in_specs=specs, out_specs=[VMEM] * l...  7.71 us
    ppermute x2, starting transfers between devices, exchange(): far = lax.ppermute(off_chip, 'sub', ends)  3.95 us
    ppermute x2, starting transfers between devices, exchange(): return (lax.ppermute(on_chip, 'sub', pairs), far)  2.9 us
    ppermute x2, waiting for transfers between devices, exchange(): far = lax.ppermute(off_chip, 'sub', ends)  2.83 us
    ppermute x1, waiting for transfers between devices, per_device(): lax.ppermute(own, 'smp', [(i, (i + shift) % parts) for i in range(parts)])  1.71 us
    ppermute x1, starting transfers between devices, per_device(): lax.ppermute(own, 'smp', [(i, (i + shift) % parts) for i in range(parts)])  0.6 us
  transfers between devices with their start and end apart: 5, of which 3 were waited for; matrix products, arithmetic and copies ran while one was open for 0% of the time, Pallas kernels for 26%

profile of v3, /device:TPU:10, one launch (start us, length us, event | category | flops | bytes accessed | tf_op | source)
XLA Modules:
  0.0 19.8 jit_solution(5364179278241979289)
XLA Ops:
  0.0 0.0 copy-start
  0.0 0.0 copy-start.2
  0.0 0.0 copy-start.4
  0.0 0.0 copy-start.5
  0.0 0.6 %collective-permute-start = (bf16[48,768]{1,0:T(8,128)(2,1)}, bf16[48,768]{1,0:T(8,128)(2,1)S(1)}, u32[]{:S(2)}, u32[]{:S(2)}) collective-permute-start(bf16[48,768]{1,0:T(8,128)(2,1)} %bitcast.7), channel_id=1, source_target_pairs={{0,1},{1,0},{2,3},{3,2},{4,5},{5,4},{6,7},{7,6},{8,9},{9,8},{10,11... | collective-permute-start | bytes 221192 | tf_op jit(solution)/shard_map/ppermute | solution.py:315
  0.6 1.6 %shard_map.91 = (bf16[768,768]{1,0:T(8,128)(2,1)S(1)}, bf16[768,768]{1,0:T(8,128)(2,1)S(1)}) custom-call(bf16[768,768]{1,0:T(8,128)(2,1)} %lam.1, bf16[768,768]{1,0:T(8,128)(2,1)} %mu.1), custom_call_target="tpu_custom_call" | custom-call | tf_op jit(solution)/shard_map/pallas_call | solution.py:22
  2.3 0.0 copy-done
  2.3 0.0 copy-done.2
  2.3 0.0 copy-done.4
  2.3 0.0 copy-done.5
  2.3 0.6 %shard_map.92 = (f32[2,96,128]{2,1,0:T(8,128)S(1)}, s32[2,6,8,128]{3,2,1,0:T(8,128)S(1)}, f32[48,768]{1,0:T(8,128)S(1)}, f32[48,768]{1,0:T(8,128)S(1)}) custom-call(bf16[48,768]{1,0:T(8,128)(2,1)S(1)} %bitcast.8, bf16[768,768]{1,0:T(8,128)(2,1)S(1)} %get-tuple-element.23.lam.refs_1_, bf16[768,768]{1,0:T(8,128)(2,1)S(1)} %get-tuple-element.24.mu.refs_2_, ...), custom_call_target="tpu_custom_call" | custom-call | tf_op jit(solution)/shard_map/pallas_call | solution.py:22
  2.9 1.7 %collective-permute-done.refs_0_ = bf16[48,768]{1,0:T(8,128)(2,1)S(1)} collective-permute-done((bf16[48,768]{1,0:T(8,128)(2,1)}, bf16[48,768]{1,0:T(8,128)(2,1)S(1)}, u32[]{:S(2)}, u32[]{:S(2)}) %collective-permute-start) | collective-permute-done | bytes 73760 | tf_op jit(solution)/shard_map/ppermute | solution.py:315
  4.6 0.0 copy-start.1
  4.7 0.0 copy-start.3
  4.7 0.3 %shard_map.93 = (f32[96,256]{1,0:T(8,128)S(1)}, f32[96,128]{1,0:T(8,128)S(1)}, f32[96,128]{1,0:T(8,128)S(1)}) custom-call(bf16[48,768]{1,0:T(8,128)(2,1)S(1)} %collective-permute-done.refs_0_, bf16[768,768]{1,0:T(8,128)(2,1)S(1)} %get-tuple-element.23.lam.refs_1_, bf16[768,768]{1,0:T(8,128)(2,1)S(1)} %get-tuple-element.24.mu.refs_2_, ...), custom_call_target="tpu_custom_call" | custom-call | tf_op jit(solution)/shard_map/pallas_call | solution.py:22
  5.0 1.9 %collective-permute-start.1 = (f32[96,128]{1,0:T(8,128)S(1)}, f32[96,128]{1,0:T(8,128)S(1)}, u32[]{:S(2)}, u32[]{:S(2)}) collective-permute-start(f32[96,128]{1,0:T(8,128)S(1)} %get-tuple-element.30), channel_id=1, source_target_pairs={{2,4},{6,8},{10,12},{14,16},{18,20},{22,24},{26,28},{4,2},{8,6},{1... | collective-permute-start | bytes 147464 | tf_op jit(solution)/shard_map/ppermute | solution.py:323
  6.9 1.7 %collective-permute-start.2 = (f32[96,128]{1,0:T(8,128)S(1)}, f32[96,128]{1,0:T(8,128)S(1)}, u32[]{:S(2)}, u32[]{:S(2)}) collective-permute-start(f32[96,128]{1,0:T(8,128)S(1)} %get-tuple-element.31), channel_id=1, source_target_pairs={{0,2},{2,0},{4,6},{6,4},{8,10},{10,8},{12,14},{14,12},{16,18},{18,... | collective-permute-start | bytes 147464 | tf_op jit(solution)/shard_map/ppermute | solution.py:324
  8.6 0.0 copy-done.1
  8.6 0.0 copy-done.3
  8.6 0.0 copy-done.6
  8.6 0.5 %shard_map.94 = (bf16[816,16]{1,0:T(8,128)(2,1)S(1)}, f32[6,6,8,128]{3,2,1,0:T(8,128)S(1)}) custom-call(f32[16,15]{1,0:T(8,128)S(1)} %copy-done.2, f32[1,16]{1,0:T(1,128)S(1)} %bitcast.13, s32[15,816]{1,0:T(8,128)S(1)} %bitcast.9, s32[3,3,2,16]{3,2,1,0:T(2,128)S(1)} %bitcast.10), custom_call_target="tpu_custom_call" | custom-call | tf_op jit(solution)/shard_map/pallas_call | solution.py:22
  9.1 0.6 %shard_map.95 = (bf16[96,512]{1,0:T(8,128)(2,1)S(1)}, f32[96,256]{1,0:T(8,128)S(1)}, f32[96,256]{1,0:T(8,128)S(1)}) custom-call(bf16[48,768]{1,0:T(8,128)(2,1)S(1)} %collective-permute-done.refs_0_, bf16[768,768]{1,0:T(8,128)(2,1)S(1)} %get-tuple-element.23.lam.refs_1_, bf16[768,768]{1,0:T(8,128)(2,1)S(1)} %get-tuple-element.24.mu.refs_2_, ...), custom_call_target="tpu_custom_call" | custom-call | tf_op jit(solution)/shard_map/pallas_call | solution.py:22
  9.7 1.6 %collective-permute-done.1.from_off = f32[96,128]{1,0:T(8,128)S(1)} collective-permute-done((f32[96,128]{1,0:T(8,128)S(1)}, f32[96,128]{1,0:T(8,128)S(1)}, u32[]{:S(2)}, u32[]{:S(2)}) %collective-permute-start.1) | collective-permute-done | bytes 49184 | tf_op jit(solution)/shard_map/ppermute | solution.py:323
  11.3 0.0 collective-permute-done.2.from_chip
  11.3 0.3 %shard_map.96 = (bf16[96,256]{1,0:T(8,128)(2,1)S(1)}, f32[96,256]{1,0:T(8,128)S(1)}, f32[96,128]{1,0:T(8,128)S(1)}, f32[96,128]{1,0:T(8,128)S(1)}) custom-call(f32[96,256]{1,0:T(8,128)S(1)} %get-tuple-element.29.field, f32[96,128]{1,0:T(8,128)S(1)} %collective-permute-done.1.from_off, f32[96,128]{1,0:T(8,128)S(1)} %collective-permute-done.2.from_chip, ...), custom_call_target="tpu_custom_call" | custom-call | tf_op jit(solution)/shard_map/pallas_call | solution.py:22
  11.6 2.0 %collective-permute-start.3 = (f32[96,128]{1,0:T(8,128)S(1)}, f32[96,128]{1,0:T(8,128)S(1)}, u32[]{:S(2)}, u32[]{:S(2)}) collective-permute-start(f32[96,128]{1,0:T(8,128)S(1)} %get-tuple-element.36), channel_id=1, source_target_pairs={{2,4},{6,8},{10,12},{14,16},{18,20},{22,24},{26,28},{4,2},{8,6},{1... | collective-permute-start | bytes 147464 | tf_op jit(solution)/shard_map/ppermute | solution.py:323
  13.7 1.2 %collective-permute-start.4 = (f32[96,128]{1,0:T(8,128)S(1)}, f32[96,128]{1,0:T(8,128)S(1)}, u32[]{:S(2)}, u32[]{:S(2)}) collective-permute-start(f32[96,128]{1,0:T(8,128)S(1)} %get-tuple-element.37), channel_id=1, source_target_pairs={{0,2},{2,0},{4,6},{6,4},{8,10},{10,8},{12,14},{14,12},{16,18},{18,... | collective-permute-start | bytes 147464 | tf_op jit(solution)/shard_map/ppermute | solution.py:324
  14.9 0.4 %shard_map.97.plane = bf16[96,512]{1,0:T(8,128)(2,1)S(1)} custom-call(bf16[96,512]{1,0:T(8,128)(2,1)S(1)} %get-tuple-element.38.plane, bf16[96,256]{1,0:T(8,128)(2,1)S(1)} %get-tuple-element.39.zed, bf16[768,768]{1,0:T(8,128)(2,1)S(1)} %get-tuple-element.23.lam.refs_1_, bf16[768,768]{1,0:T(8,128)(2,1)S(1)} %get-tuple-element.24.mu.refs_2_, ...), custom_call_target="tpu_custom_call" | custom-call | tf_op jit(solution)/shard_map/pallas_call | solution.py:22
  15.3 1.4 %shard_map.98.early = bf16[1,2,3,816,384]{4,3,2,1,0:T(8,128)(2,1)} custom-call(bf16[96,512]{1,0:T(8,128)(2,1)S(1)} %shard_map.97.plane, bf16[816,16]{1,0:T(8,128)(2,1)S(1)} %get-tuple-element.40.basis), custom_call_target="tpu_custom_call" | custom-call | tf_op jit(solution)/shard_map/pallas_call | solution.py:22
  16.7 1.3 %collective-permute-done.3.from_off = f32[96,128]{1,0:T(8,128)S(1)} collective-permute-done((f32[96,128]{1,0:T(8,128)S(1)}, f32[96,128]{1,0:T(8,128)S(1)}, u32[]{:S(2)}, u32[]{:S(2)}) %collective-permute-start.3) | collective-permute-done | bytes 49184 | tf_op jit(solution)/shard_map/ppermute | solution.py:323
  17.9 0.0 collective-permute-done.4.from_chip
  17.9 1.9 %shard_map.99 = bf16[1,2,3,816,384]{4,3,2,1,0:T(8,128)(2,1)} custom-call(f32[96,256]{1,0:T(8,128)S(1)} %get-tuple-element.35.field, f32[96,128]{1,0:T(8,128)S(1)} %collective-permute-done.3.from_off, f32[96,128]{1,0:T(8,128)S(1)} %collective-permute-done.4.from_chip, ...), custom_call_target="tpu_custom_call", output_to_operand_aliasing={{}: (7, {})} | custom-call | tf_op jit(solution)/shard_map/pallas_call | solution.py:22
  (1 shorter events, 0.0 us)
Async XLA Ops:
  0.0 2.3 %copy-start = (bf16[1,2,3,8,768]{4,3,2,1,0:T(8,128)(2,1)S(1)}, bf16[1,2,3,8,768]{4,3,2,1,0:T(8,128)(2,1)}, u32[]{:S(2)}) copy-start(bf16[1,2,3,8,768]{4,3,2,1,0:T(8,128)(2,1)} %param.9) | copy-start | bytes 221188
  0.0 2.3 %copy-start.2 = (f32[16,15]{1,0:T(8,128)S(1)}, f32[16,15]{1,0:T(8,128)}, u32[]{:S(2)}) copy-start(f32[16,15]{1,0:T(8,128)} %nodes.3) | copy-start | bytes 2884
  0.0 2.3 %copy-start.4 = (f32[2,1,2,3,15]{4,2,3,1,0:T(2,128)S(1)}, f32[2,1,2,3,15]{4,2,3,1,0:T(2,128)}, u32[]{:S(2)}) copy-start(f32[2,1,2,3,15]{4,2,3,1,0:T(2,128)} %param.12) | copy-start | bytes 2164
  0.0 2.3 %copy-start.5 = (s32[1,2,3,128]{3,1,2,0:T(2,128)S(1)}, s32[1,2,3,128]{3,1,2,0:T(2,128)}, u32[]{:S(2)}) copy-start(s32[1,2,3,128]{3,1,2,0:T(2,128)} %param.17) | copy-start | bytes 9220
  0.0 4.6 %collective-permute-start = (bf16[48,768]{1,0:T(8,128)(2,1)}, bf16[48,768]{1,0:T(8,128)(2,1)S(1)}, u32[]{:S(2)}, u32[]{:S(2)}) collective-permute-start(bf16[48,768]{1,0:T(8,128)(2,1)} %bitcast.7), channel_id=1, source_target_pairs={{0,1},{1,0},{2,3},{3,2},{4,5},{5,4},{6,7},{7,6},{8,9},{9,8},{10,11... | collective-permute-start | bytes 221192 | tf_op jit(solution)/shard_map/ppermute | solution.py:315
  4.6 4.0 %copy-start.1 = (s32[816,15]{0,1:T(8,128)S(1)}, s32[816,15]{0,1:T(8,128)}, u32[]{:S(2)}) copy-start(s32[816,15]{0,1:T(8,128)} %param.15) | copy-start | bytes 146884
  4.7 4.0 %copy-start.3 = (s32[3,16,2,3]{1,2,3,0:T(2,128)S(1)}, s32[3,16,2,3]{1,2,3,0:T(2,128)}, u32[]{:S(2)}) copy-start(s32[3,16,2,3]{1,2,3,0:T(2,128)} %param.16) | copy-start | bytes 3460
  4.7 4.0 %copy-start.6 = (f32[16]{0:T(128)S(1)}, f32[16]{0:T(128)}, u32[]{:S(2)}) copy-start(f32[16]{0:T(128)} %param.14) | copy-start | bytes 196
  5.0 6.3 %collective-permute-start.1 = (f32[96,128]{1,0:T(8,128)S(1)}, f32[96,128]{1,0:T(8,128)S(1)}, u32[]{:S(2)}, u32[]{:S(2)}) collective-permute-start(f32[96,128]{1,0:T(8,128)S(1)} %get-tuple-element.30), channel_id=1, source_target_pairs={{2,4},{6,8},{10,12},{14,16},{18,20},{22,24},{26,28},{4,2},{8,6},{1... | collective-permute-start | bytes 147464 | tf_op jit(solution)/shard_map/ppermute | solution.py:323
  6.9 4.4 %collective-permute-start.2 = (f32[96,128]{1,0:T(8,128)S(1)}, f32[96,128]{1,0:T(8,128)S(1)}, u32[]{:S(2)}, u32[]{:S(2)}) collective-permute-start(f32[96,128]{1,0:T(8,128)S(1)} %get-tuple-element.31), channel_id=1, source_target_pairs={{0,2},{2,0},{4,6},{6,4},{8,10},{10,8},{12,14},{14,12},{16,18},{18,... | collective-permute-start | bytes 147464 | tf_op jit(solution)/shard_map/ppermute | solution.py:324
  11.6 6.3 %collective-permute-start.3 = (f32[96,128]{1,0:T(8,128)S(1)}, f32[96,128]{1,0:T(8,128)S(1)}, u32[]{:S(2)}, u32[]{:S(2)}) collective-permute-start(f32[96,128]{1,0:T(8,128)S(1)} %get-tuple-element.36), channel_id=1, source_target_pairs={{2,4},{6,8},{10,12},{14,16},{18,20},{22,24},{26,28},{4,2},{8,6},{1... | collective-permute-start | bytes 147464 | tf_op jit(solution)/shard_map/ppermute | solution.py:323
  13.7 4.3 %collective-permute-start.4 = (f32[96,128]{1,0:T(8,128)S(1)}, f32[96,128]{1,0:T(8,128)S(1)}, u32[]{:S(2)}, u32[]{:S(2)}) collective-permute-start(f32[96,128]{1,0:T(8,128)S(1)} %get-tuple-element.37), channel_id=1, source_target_pairs={{0,2},{2,0},{4,6},{6,4},{8,10},{10,8},{12,14},{14,12},{16,18},{18,... | collective-permute-start | bytes 147464 | tf_op jit(solution)/shard_map/ppermute | solution.py:324

commit v4 on v3

--- a/solution.py
+++ b/solution.py
@@ -192,11 +192,13 @@
 
 
 def z_jumps(d, field, from_off, from_chip, maps, masks, out):
-    even = lax.rem(lax.axis_index("sub"), 2) == 0
+    layer = lax.axis_index("sub")
+    even = lax.rem(layer, 2) == 0
+    inside = jnp.logical_and(layer > 0, layer < lax.axis_size("sub") - 1)
     for n in range(d.subs):
         for start in range(n * d.samples, (n + 1) * d.samples, 8):
             rows = slice(start, start + 8)
-            near, far = from_chip[rows, :], from_off[rows, :]
+            near, far = from_chip[rows, :], jnp.where(inside, from_off[rows, :], 0.0)
             above = jnp.where(even, near, far)
             below = jnp.where(even, far, near)
             matched = jnp.take_along_axis(above, maps[0, n], axis=1, mode="promise_in_bounds")
@@ -316,11 +318,15 @@
         for shift in range(1, parts)
     ]
     pairs = [(i, i ^ 1) for i in range(layers)]
-    ends = [(i, i + 1) for i in range(1, layers - 1, 2)]
-    ends = ends + [(j, i) for i, j in ends]
+    partner = {i: i + 1 if i % 2 else i - 1 for i in range(1, layers - 1)}
+    across = [
+        (i * parts + s, partner[i] * parts + s if i in partner else i * parts + (s + 1) % parts)
+        for i in range(layers)
+        for s in range(parts)
+    ]
 
     def exchange(on_chip, off_chip):
-        far = lax.ppermute(off_chip, "sub", ends)
+        far = lax.ppermute(off_chip, ("sub", "smp"), across)
         return lax.ppermute(on_chip, "sub", pairs), far
 
     def run(body, *args, **options):

time: 20.2 us -> 16.6 us (0.82)
  the two profiles are of different devices: /device:TPU:10 before, /device:TPU:0 now
where the time goes in v4:
time: 16.6 us; the launch traced here: 16.4 us
  Pallas kernels  7.7 us (46%)
  starting transfers between devices  7.42 us (45%)
  waiting for transfers between devices  1.21 us (7%)
    pallas_call x9, Pallas kernels, call(): pl.pallas_call(body, out_shape=outs, in_specs=specs, out_specs=[VMEM] * l...  7.7 us
    ppermute x2, starting transfers between devices, exchange(): far = lax.ppermute(off_chip, ('sub', 'smp'), across)  4.17 us
    ppermute x1, starting transfers between devices, per_device(): lax.ppermute(own, 'smp', [(i, (i + shift) % parts) for i in range(parts)])  3.01 us
    ppermute x2, waiting for transfers between devices, exchange(): far = lax.ppermute(off_chip, ('sub', 'smp'), across)  0.97 us
  transfers between devices with their start and end apart: 5, of which 3 were waited for; matrix products, arithmetic and copies ran while one was open for 0% of the time, Pallas kernels for 31%

profile of v4, /device:TPU:0, one launch (start us, length us, event | category | flops | bytes accessed | tf_op | source)
XLA Modules:
  0.0 16.4 jit_solution(8137223425653636116)
XLA Ops:
  0.0 0.0 copy-start
  0.0 0.0 copy-start.2
  0.0 0.0 copy-start.4
  0.0 0.0 copy-start.5
  0.0 3.0 %collective-permute-start = (bf16[48,768]{1,0:T(8,128)(2,1)}, bf16[48,768]{1,0:T(8,128)(2,1)S(1)}, u32[]{:S(2)}, u32[]{:S(2)}) collective-permute-start(bf16[48,768]{1,0:T(8,128)(2,1)} %bitcast.7), channel_id=1, source_target_pairs={{0,1},{1,0},{2,3},{3,2},{4,5},{5,4},{6,7},{7,6},{8,9},{9,8},{10,11... | collective-permute-start | bytes 221192 | tf_op jit(solution)/shard_map/ppermute | solution.py:317
  3.0 1.6 %shard_map.91 = (bf16[768,768]{1,0:T(8,128)(2,1)S(1)}, bf16[768,768]{1,0:T(8,128)(2,1)S(1)}) custom-call(bf16[768,768]{1,0:T(8,128)(2,1)} %lam.1, bf16[768,768]{1,0:T(8,128)(2,1)} %mu.1), custom_call_target="tpu_custom_call" | custom-call | tf_op jit(solution)/shard_map/pallas_call | solution.py:22
  4.7 0.0 copy-done
  4.7 0.0 copy-done.2
  4.7 0.0 copy-done.4
  4.7 0.0 copy-done.5
  4.7 0.6 %shard_map.92 = (f32[2,96,128]{2,1,0:T(8,128)S(1)}, s32[2,6,8,128]{3,2,1,0:T(8,128)S(1)}, f32[48,768]{1,0:T(8,128)S(1)}, f32[48,768]{1,0:T(8,128)S(1)}) custom-call(bf16[48,768]{1,0:T(8,128)(2,1)S(1)} %bitcast.8, bf16[768,768]{1,0:T(8,128)(2,1)S(1)} %get-tuple-element.23.lam.refs_1_, bf16[768,768]{1,0:T(8,128)(2,1)S(1)} %get-tuple-element.24.mu.refs_2_, ...), custom_call_target="tpu_custom_call" | custom-call | tf_op jit(solution)/shard_map/pallas_call | solution.py:22
  5.3 0.2 %collective-permute-done.refs_0_ = bf16[48,768]{1,0:T(8,128)(2,1)S(1)} collective-permute-done((bf16[48,768]{1,0:T(8,128)(2,1)}, bf16[48,768]{1,0:T(8,128)(2,1)S(1)}, u32[]{:S(2)}, u32[]{:S(2)}) %collective-permute-start) | collective-permute-done | bytes 73760 | tf_op jit(solution)/shard_map/ppermute | solution.py:317
  5.6 0.0 copy-start.1
  5.6 0.0 copy-start.3
  5.6 0.3 %shard_map.93 = (f32[96,256]{1,0:T(8,128)S(1)}, f32[96,128]{1,0:T(8,128)S(1)}, f32[96,128]{1,0:T(8,128)S(1)}) custom-call(bf16[48,768]{1,0:T(8,128)(2,1)S(1)} %collective-permute-done.refs_0_, bf16[768,768]{1,0:T(8,128)(2,1)S(1)} %get-tuple-element.23.lam.refs_1_, bf16[768,768]{1,0:T(8,128)(2,1)S(1)} %get-tuple-element.24.mu.refs_2_, ...), custom_call_target="tpu_custom_call" | custom-call | tf_op jit(solution)/shard_map/pallas_call | solution.py:22
  5.9 2.1 %collective-permute-start.1 = (f32[96,128]{1,0:T(8,128)S(1)}, f32[96,128]{1,0:T(8,128)S(1)}, u32[]{:S(2)}, u32[]{:S(2)}) collective-permute-start(f32[96,128]{1,0:T(8,128)S(1)} %get-tuple-element.30), channel_id=1, source_target_pairs={{0,1},{1,0},{2,4},{3,5},{4,2},{5,3},{6,8},{7,9},{8,6},{9,7},{10,12... | collective-permute-start | bytes 147464 | tf_op jit(solution)/shard_map/ppermute | solution.py:329
  8.0 0.1 collective-permute-start.2
  8.1 0.0 copy-done.1
  8.1 0.0 copy-done.3
  8.1 0.0 copy-done.6
  8.1 0.5 %shard_map.94 = (bf16[816,16]{1,0:T(8,128)(2,1)S(1)}, f32[6,6,8,128]{3,2,1,0:T(8,128)S(1)}) custom-call(f32[16,15]{1,0:T(8,128)S(1)} %copy-done.2, f32[1,16]{1,0:T(1,128)S(1)} %bitcast.13, s32[15,816]{1,0:T(8,128)S(1)} %bitcast.9, s32[3,3,2,16]{3,2,1,0:T(2,128)S(1)} %bitcast.10), custom_call_target="tpu_custom_call" | custom-call | tf_op jit(solution)/shard_map/pallas_call | solution.py:22
  8.7 0.6 %shard_map.95 = (bf16[96,512]{1,0:T(8,128)(2,1)S(1)}, f32[96,256]{1,0:T(8,128)S(1)}, f32[96,256]{1,0:T(8,128)S(1)}) custom-call(bf16[48,768]{1,0:T(8,128)(2,1)S(1)} %collective-permute-done.refs_0_, bf16[768,768]{1,0:T(8,128)(2,1)S(1)} %get-tuple-element.23.lam.refs_1_, bf16[768,768]{1,0:T(8,128)(2,1)S(1)} %get-tuple-element.24.mu.refs_2_, ...), custom_call_target="tpu_custom_call" | custom-call | tf_op jit(solution)/shard_map/pallas_call | solution.py:22
  9.3 0.8 %collective-permute-done.1.from_off = f32[96,128]{1,0:T(8,128)S(1)} collective-permute-done((f32[96,128]{1,0:T(8,128)S(1)}, f32[96,128]{1,0:T(8,128)S(1)}, u32[]{:S(2)}, u32[]{:S(2)}) %collective-permute-start.1) | collective-permute-done | bytes 49184 | tf_op jit(solution)/shard_map/ppermute | solution.py:329
  10.1 0.0 collective-permute-done.2.from_chip
  10.1 0.3 %shard_map.96 = (bf16[96,256]{1,0:T(8,128)(2,1)S(1)}, f32[96,256]{1,0:T(8,128)S(1)}, f32[96,128]{1,0:T(8,128)S(1)}, f32[96,128]{1,0:T(8,128)S(1)}) custom-call(f32[96,256]{1,0:T(8,128)S(1)} %get-tuple-element.29.field, f32[96,128]{1,0:T(8,128)S(1)} %collective-permute-done.1.from_off, f32[96,128]{1,0:T(8,128)S(1)} %collective-permute-done.2.from_chip, ...), custom_call_target="tpu_custom_call" | custom-call | tf_op jit(solution)/shard_map/pallas_call | solution.py:22
  10.4 2.1 %collective-permute-start.3 = (f32[96,128]{1,0:T(8,128)S(1)}, f32[96,128]{1,0:T(8,128)S(1)}, u32[]{:S(2)}, u32[]{:S(2)}) collective-permute-start(f32[96,128]{1,0:T(8,128)S(1)} %get-tuple-element.36), channel_id=1, source_target_pairs={{0,1},{1,0},{2,4},{3,5},{4,2},{5,3},{6,8},{7,9},{8,6},{9,7},{10,12... | collective-permute-start | bytes 147464 | tf_op jit(solution)/shard_map/ppermute | solution.py:329
  12.5 0.1 collective-permute-start.4
  12.6 0.4 %shard_map.97.plane = bf16[96,512]{1,0:T(8,128)(2,1)S(1)} custom-call(bf16[96,512]{1,0:T(8,128)(2,1)S(1)} %get-tuple-element.38.plane, bf16[96,256]{1,0:T(8,128)(2,1)S(1)} %get-tuple-element.39.zed, bf16[768,768]{1,0:T(8,128)(2,1)S(1)} %get-tuple-element.23.lam.refs_1_, bf16[768,768]{1,0:T(8,128)(2,1)S(1)} %get-tuple-element.24.mu.refs_2_, ...), custom_call_target="tpu_custom_call" | custom-call | tf_op jit(solution)/shard_map/pallas_call | solution.py:22
  13.0 1.4 %shard_map.98.early = bf16[1,2,3,816,384]{4,3,2,1,0:T(8,128)(2,1)} custom-call(bf16[96,512]{1,0:T(8,128)(2,1)S(1)} %shard_map.97.plane, bf16[816,16]{1,0:T(8,128)(2,1)S(1)} %get-tuple-element.40.basis), custom_call_target="tpu_custom_call" | custom-call | tf_op jit(solution)/shard_map/pallas_call | solution.py:22
  14.4 0.2 %collective-permute-done.3.from_off = f32[96,128]{1,0:T(8,128)S(1)} collective-permute-done((f32[96,128]{1,0:T(8,128)S(1)}, f32[96,128]{1,0:T(8,128)S(1)}, u32[]{:S(2)}, u32[]{:S(2)}) %collective-permute-start.3) | collective-permute-done | bytes 49184 | tf_op jit(solution)/shard_map/ppermute | solution.py:329
  14.5 0.0 collective-permute-done.4.from_chip
  14.5 1.9 %shard_map.99 = bf16[1,2,3,816,384]{4,3,2,1,0:T(8,128)(2,1)} custom-call(f32[96,256]{1,0:T(8,128)S(1)} %get-tuple-element.35.field, f32[96,128]{1,0:T(8,128)S(1)} %collective-permute-done.3.from_off, f32[96,128]{1,0:T(8,128)S(1)} %collective-permute-done.4.from_chip, ...), custom_call_target="tpu_custom_call", output_to_operand_aliasing={{}: (7, {})} | custom-call | tf_op jit(solution)/shard_map/pallas_call | solution.py:22
  (1 shorter events, 0.0 us)
Async XLA Ops:
  0.0 4.7 %copy-start = (bf16[1,2,3,8,768]{4,3,2,1,0:T(8,128)(2,1)S(1)}, bf16[1,2,3,8,768]{4,3,2,1,0:T(8,128)(2,1)}, u32[]{:S(2)}) copy-start(bf16[1,2,3,8,768]{4,3,2,1,0:T(8,128)(2,1)} %param.9) | copy-start | bytes 221188
  0.0 4.7 %copy-start.2 = (f32[16,15]{1,0:T(8,128)S(1)}, f32[16,15]{1,0:T(8,128)}, u32[]{:S(2)}) copy-start(f32[16,15]{1,0:T(8,128)} %nodes.3) | copy-start | bytes 2884
  0.0 4.7 %copy-start.4 = (f32[2,1,2,3,15]{4,2,3,1,0:T(2,128)S(1)}, f32[2,1,2,3,15]{4,2,3,1,0:T(2,128)}, u32[]{:S(2)}) copy-start(f32[2,1,2,3,15]{4,2,3,1,0:T(2,128)} %param.12) | copy-start | bytes 2164
  0.0 4.7 %copy-start.5 = (s32[1,2,3,128]{3,1,2,0:T(2,128)S(1)}, s32[1,2,3,128]{3,1,2,0:T(2,128)}, u32[]{:S(2)}) copy-start(s32[1,2,3,128]{3,1,2,0:T(2,128)} %param.17) | copy-start | bytes 9220
  0.0 5.6 %collective-permute-start = (bf16[48,768]{1,0:T(8,128)(2,1)}, bf16[48,768]{1,0:T(8,128)(2,1)S(1)}, u32[]{:S(2)}, u32[]{:S(2)}) collective-permute-start(bf16[48,768]{1,0:T(8,128)(2,1)} %bitcast.7), channel_id=1, source_target_pairs={{0,1},{1,0},{2,3},{3,2},{4,5},{5,4},{6,7},{7,6},{8,9},{9,8},{10,11... | collective-permute-start | bytes 221192 | tf_op jit(solution)/shard_map/ppermute | solution.py:317
  5.6 2.6 %copy-start.1 = (s32[816,15]{0,1:T(8,128)S(1)}, s32[816,15]{0,1:T(8,128)}, u32[]{:S(2)}) copy-start(s32[816,15]{0,1:T(8,128)} %param.15) | copy-start | bytes 146884
  5.6 2.6 %copy-start.3 = (s32[3,16,2,3]{1,2,3,0:T(2,128)S(1)}, s32[3,16,2,3]{1,2,3,0:T(2,128)}, u32[]{:S(2)}) copy-start(s32[3,16,2,3]{1,2,3,0:T(2,128)} %param.16) | copy-start | bytes 3460
  5.6 2.6 %copy-start.6 = (f32[16]{0:T(128)S(1)}, f32[16]{0:T(128)}, u32[]{:S(2)}) copy-start(f32[16]{0:T(128)} %param.14) | copy-start | bytes 196
  5.9 4.2 %collective-permute-start.1 = (f32[96,128]{1,0:T(8,128)S(1)}, f32[96,128]{1,0:T(8,128)S(1)}, u32[]{:S(2)}, u32[]{:S(2)}) collective-permute-start(f32[96,128]{1,0:T(8,128)S(1)} %get-tuple-element.30), channel_id=1, source_target_pairs={{0,1},{1,0},{2,4},{3,5},{4,2},{5,3},{6,8},{7,9},{8,6},{9,7},{10,12... | collective-permute-start | bytes 147464 | tf_op jit(solution)/shard_map/ppermute | solution.py:329
  8.0 2.1 %collective-permute-start.2 = (f32[96,128]{1,0:T(8,128)S(1)}, f32[96,128]{1,0:T(8,128)S(1)}, u32[]{:S(2)}, u32[]{:S(2)}) collective-permute-start(f32[96,128]{1,0:T(8,128)S(1)} %get-tuple-element.31), channel_id=1, source_target_pairs={{0,2},{2,0},{4,6},{6,4},{8,10},{10,8},{12,14},{14,12},{16,18},{18,... | collective-permute-start | bytes 147464 | tf_op jit(solution)/shard_map/ppermute | solution.py:330
  10.4 4.2 %collective-permute-start.3 = (f32[96,128]{1,0:T(8,128)S(1)}, f32[96,128]{1,0:T(8,128)S(1)}, u32[]{:S(2)}, u32[]{:S(2)}) collective-permute-start(f32[96,128]{1,0:T(8,128)S(1)} %get-tuple-element.36), channel_id=1, source_target_pairs={{0,1},{1,0},{2,4},{3,5},{4,2},{5,3},{6,8},{7,9},{8,6},{9,7},{10,12... | collective-permute-start | bytes 147464 | tf_op jit(solution)/shard_map/ppermute | solution.py:329
  12.5 2.1 %collective-permute-start.4 = (f32[96,128]{1,0:T(8,128)S(1)}, f32[96,128]{1,0:T(8,128)S(1)}, u32[]{:S(2)}, u32[]{:S(2)}) collective-permute-start(f32[96,128]{1,0:T(8,128)S(1)} %get-tuple-element.37), channel_id=1, source_target_pairs={{0,2},{2,0},{4,6},{6,4},{8,10},{10,8},{12,14},{14,12},{16,18},{18,... | collective-permute-start | bytes 147464 | tf_op jit(solution)/shard_map/ppermute | solution.py:330

commit v5 on v4

--- a/solution.py
+++ b/solution.py
@@ -10,7 +10,7 @@
 F32 = jnp.float32
 BF16 = jnp.bfloat16
 VMEM = pl.BlockSpec(memory_space=pltpu.VMEM)
-CHUNKS = 3
+CHUNK = 144
 HBM = pl.BlockSpec(memory_space=pltpu.HBM)
 
 
@@ -259,50 +259,43 @@
     jumps[:, d.plane :] = held[...].astype(BF16)
 
 
-def project_rows(d, picks, lanes, basis, out, rows_out, sems):
+def project_rows(d, picks, lanes, basis, out, rows_out, sem):
     width = lanes.stop - lanes.start
     group = max(g for g in (1, 2, 3, 6) if d.subs % g == 0 and g * width <= 768)
-    chunk = d.terms // CHUNKS
-    copies = []
     for n in range(0, d.subs, group):
         right = picks[n : n + group]
         right = right[0] if group == 1 else jnp.concatenate(right, axis=1)
-        for c in range(CHUNKS):
-            rows = slice(c * chunk, (c + 1) * chunk)
+        for start in range(0, d.terms, CHUNK):
+            rows = slice(start, min(start + CHUNK, d.terms))
             value = dot(basis[rows, :], right)
             for m in range(group):
-                rows_out[n + m, rows, :] = value[:, m * width : (m + 1) * width].astype(BF16)
                 y, x = divmod(n + m, d.breadth)
-                copy = pltpu.make_async_copy(
-                    rows_out.at[n + m, rows, :],
-                    out.at[0, y, x, rows, lanes],
-                    sems.at[n + m, c],
-                )
-                copy.start()
-                copies.append(copy)
-    for copy in copies:
-        copy.wait()
-
-
-def project_early(d, plane, basis, out, rows_out, sems):
+                rows_out[y, x, rows, :] = value[:, m * width : (m + 1) * width].astype(BF16)
+                pltpu.make_async_copy(
+                    rows_out.at[y, x, rows, :], out.at[0, y, x, rows, lanes], sem
+                ).start()
+    pltpu.make_async_copy(rows_out, out.at[0, :, :, :, lanes], sem).wait()
+
+
+def project_early(d, plane, basis, out, rows_out, sem):
     start = pl.multiple_of(lax.axis_index("smp") * d.share, 128)
     picks = [plane[d.block(n), pl.ds(start, d.face)] for n in range(d.subs)]
-    project_rows(d, picks, slice(0, d.face), basis, out, rows_out, sems)
+    project_rows(d, picks, slice(0, d.face), basis, out, rows_out, sem)
 
 
 def project_late(
-    d, field, from_off, from_chip, maps, masks, plane, basis, early, out, held, jumps, rows_out, sems
+    d, field, from_off, from_chip, maps, masks, plane, basis, early, out, held, jumps, rows_out, sem
 ):
     last_z(d, field, from_off, from_chip, maps, masks, plane, jumps, held)
     width = d.share - d.face
     start = pl.multiple_of(lax.axis_index("smp") * d.share + d.face, 128)
     picks = [jumps[d.block(n), pl.ds(start, width)] for n in range(d.subs)]
-    project_rows(d, picks, slice(d.face, d.share), basis, out, rows_out, sems)
-
-
-def project_share(d, jumps, basis, out, rows_out, sems):
+    project_rows(d, picks, slice(d.face, d.share), basis, out, rows_out, sem)
+
+
+def project_share(d, jumps, basis, out, rows_out, sem):
     picks = [jumps[d.block(n), :] for n in range(d.subs)]
-    project_rows(d, picks, slice(0, d.share), basis, out, rows_out, sems)
+    project_rows(d, picks, slice(0, d.share), basis, out, rows_out, sem)
 
 
 def per_device(
@@ -395,8 +388,8 @@
 
     def buffers(width):
         return [
-            pltpu.VMEM((d.subs, d.terms, width), BF16),
-            pltpu.SemaphoreType.DMA((d.subs, CHUNKS)),
+            pltpu.VMEM((d.height, d.breadth, d.terms, width), BF16),
+            pltpu.SemaphoreType.DMA(()),
         ]
 
     if d.share == 3 * face:

time: 16.6 us -> 16.4 us (0.988)
  Pallas kernels: 7.7 us -> 7.32 us
  waiting for transfers between devices: 1.21 us -> 1.39 us
    pallas_call x9, Pallas kernels: 7.7 us -> 7.32 us  [call(): pl.pallas_call(body, out_shape=outs, in_specs=specs, out_specs=[VMEM] * l...]
    ppermute x2, waiting for transfers between devices: 0.97 us -> 1.16 us  [exchange(): far = lax.ppermute(off_chip, ('sub', 'smp'), across)]
where the time goes in v5:
time: 16.4 us; the launch traced here: 16.2 us
  starting transfers between devices  7.42 us (45%)
  Pallas kernels  7.32 us (45%)
  waiting for transfers between devices  1.39 us (8%)
    pallas_call x9, Pallas kernels, call(): pl.pallas_call(body, out_shape=outs, in_specs=specs, out_specs=[VMEM] * l...  7.32 us
    ppermute x2, starting transfers between devices, exchange(): far = lax.ppermute(off_chip, ('sub', 'smp'), across)  4.17 us
    ppermute x1, starting transfers between devices, per_device(): lax.ppermute(own, 'smp', [(i, (i + shift) % parts) for i in range(parts)])  3.01 us
    ppermute x2, waiting for transfers between devices, exchange(): far = lax.ppermute(off_chip, ('sub', 'smp'), across)  1.16 us
  transfers between devices with their start and end apart: 5, of which 3 were waited for; matrix products, arithmetic and copies ran while one was open for 0% of the time, Pallas kernels for 31%

profile of v5, /device:TPU:0, one launch (start us, length us, event | category | flops | bytes accessed | tf_op | source)
XLA Modules:
  0.0 16.2 jit_solution(1643520394234953863)
XLA Ops:
  0.0 0.0 copy-start
  0.0 0.0 copy-start.2
  0.0 0.0 copy-start.4
  0.0 0.0 copy-start.5
  0.0 3.0 %collective-permute-start = (bf16[48,768]{1,0:T(8,128)(2,1)}, bf16[48,768]{1,0:T(8,128)(2,1)S(1)}, u32[]{:S(2)}, u32[]{:S(2)}) collective-permute-start(bf16[48,768]{1,0:T(8,128)(2,1)} %bitcast.7), channel_id=1, source_target_pairs={{0,1},{1,0},{2,3},{3,2},{4,5},{5,4},{6,7},{7,6},{8,9},{9,8},{10,11... | collective-permute-start | bytes 221192 | tf_op jit(solution)/shard_map/ppermute | solution.py:310
  3.0 1.6 %shard_map.91 = (bf16[768,768]{1,0:T(8,128)(2,1)S(1)}, bf16[768,768]{1,0:T(8,128)(2,1)S(1)}) custom-call(bf16[768,768]{1,0:T(8,128)(2,1)} %lam.1, bf16[768,768]{1,0:T(8,128)(2,1)} %mu.1), custom_call_target="tpu_custom_call" | custom-call | tf_op jit(solution)/shard_map/pallas_call | solution.py:22
  4.7 0.0 copy-done
  4.7 0.0 copy-done.2
  4.7 0.0 copy-done.4
  4.7 0.0 copy-done.5
  4.7 0.6 %shard_map.92 = (f32[2,96,128]{2,1,0:T(8,128)S(1)}, s32[2,6,8,128]{3,2,1,0:T(8,128)S(1)}, f32[48,768]{1,0:T(8,128)S(1)}, f32[48,768]{1,0:T(8,128)S(1)}) custom-call(bf16[48,768]{1,0:T(8,128)(2,1)S(1)} %bitcast.8, bf16[768,768]{1,0:T(8,128)(2,1)S(1)} %get-tuple-element.23.lam.refs_1_, bf16[768,768]{1,0:T(8,128)(2,1)S(1)} %get-tuple-element.24.mu.refs_2_, ...), custom_call_target="tpu_custom_call" | custom-call | tf_op jit(solution)/shard_map/pallas_call | solution.py:22
  5.3 0.2 %collective-permute-done.refs_0_ = bf16[48,768]{1,0:T(8,128)(2,1)S(1)} collective-permute-done((bf16[48,768]{1,0:T(8,128)(2,1)}, bf16[48,768]{1,0:T(8,128)(2,1)S(1)}, u32[]{:S(2)}, u32[]{:S(2)}) %collective-permute-start) | collective-permute-done | bytes 73760 | tf_op jit(solution)/shard_map/ppermute | solution.py:310
  5.6 0.0 copy-start.1
  5.6 0.0 copy-start.3
  5.6 0.3 %shard_map.93 = (f32[96,256]{1,0:T(8,128)S(1)}, f32[96,128]{1,0:T(8,128)S(1)}, f32[96,128]{1,0:T(8,128)S(1)}) custom-call(bf16[48,768]{1,0:T(8,128)(2,1)S(1)} %collective-permute-done.refs_0_, bf16[768,768]{1,0:T(8,128)(2,1)S(1)} %get-tuple-element.23.lam.refs_1_, bf16[768,768]{1,0:T(8,128)(2,1)S(1)} %get-tuple-element.24.mu.refs_2_, ...), custom_call_target="tpu_custom_call" | custom-call | tf_op jit(solution)/shard_map/pallas_call | solution.py:22
  5.9 2.1 %collective-permute-start.1 = (f32[96,128]{1,0:T(8,128)S(1)}, f32[96,128]{1,0:T(8,128)S(1)}, u32[]{:S(2)}, u32[]{:S(2)}) collective-permute-start(f32[96,128]{1,0:T(8,128)S(1)} %get-tuple-element.30), channel_id=1, source_target_pairs={{0,1},{1,0},{2,4},{3,5},{4,2},{5,3},{6,8},{7,9},{8,6},{9,7},{10,12... | collective-permute-start | bytes 147464 | tf_op jit(solution)/shard_map/ppermute | solution.py:322
  8.0 0.1 collective-permute-start.2
  8.1 0.0 copy-done.1
  8.1 0.0 copy-done.3
  8.1 0.0 copy-done.6
  8.1 0.5 %shard_map.94 = (bf16[816,16]{1,0:T(8,128)(2,1)S(1)}, f32[6,6,8,128]{3,2,1,0:T(8,128)S(1)}) custom-call(f32[16,15]{1,0:T(8,128)S(1)} %copy-done.2, f32[1,16]{1,0:T(1,128)S(1)} %bitcast.13, s32[15,816]{1,0:T(8,128)S(1)} %bitcast.9, s32[3,3,2,16]{3,2,1,0:T(2,128)S(1)} %bitcast.10), custom_call_target="tpu_custom_call" | custom-call | tf_op jit(solution)/shard_map/pallas_call | solution.py:22
  8.7 0.6 %shard_map.95 = (bf16[96,512]{1,0:T(8,128)(2,1)S(1)}, f32[96,256]{1,0:T(8,128)S(1)}, f32[96,256]{1,0:T(8,128)S(1)}) custom-call(bf16[48,768]{1,0:T(8,128)(2,1)S(1)} %collective-permute-done.refs_0_, bf16[768,768]{1,0:T(8,128)(2,1)S(1)} %get-tuple-element.23.lam.refs_1_, bf16[768,768]{1,0:T(8,128)(2,1)S(1)} %get-tuple-element.24.mu.refs_2_, ...), custom_call_target="tpu_custom_call" | custom-call | tf_op jit(solution)/shard_map/pallas_call | solution.py:22
  9.3 0.8 %collective-permute-done.1.from_off = f32[96,128]{1,0:T(8,128)S(1)} collective-permute-done((f32[96,128]{1,0:T(8,128)S(1)}, f32[96,128]{1,0:T(8,128)S(1)}, u32[]{:S(2)}, u32[]{:S(2)}) %collective-permute-start.1) | collective-permute-done | bytes 49184 | tf_op jit(solution)/shard_map/ppermute | solution.py:322
  10.1 0.0 collective-permute-done.2.from_chip
  10.1 0.3 %shard_map.96 = (bf16[96,256]{1,0:T(8,128)(2,1)S(1)}, f32[96,256]{1,0:T(8,128)S(1)}, f32[96,128]{1,0:T(8,128)S(1)}, f32[96,128]{1,0:T(8,128)S(1)}) custom-call(f32[96,256]{1,0:T(8,128)S(1)} %get-tuple-element.29.field, f32[96,128]{1,0:T(8,128)S(1)} %collective-permute-done.1.from_off, f32[96,128]{1,0:T(8,128)S(1)} %collective-permute-done.2.from_chip, ...), custom_call_target="tpu_custom_call" | custom-call | tf_op jit(solution)/shard_map/pallas_call | solution.py:22
  10.4 2.1 %collective-permute-start.3 = (f32[96,128]{1,0:T(8,128)S(1)}, f32[96,128]{1,0:T(8,128)S(1)}, u32[]{:S(2)}, u32[]{:S(2)}) collective-permute-start(f32[96,128]{1,0:T(8,128)S(1)} %get-tuple-element.36), channel_id=1, source_target_pairs={{0,1},{1,0},{2,4},{3,5},{4,2},{5,3},{6,8},{7,9},{8,6},{9,7},{10,12... | collective-permute-start | bytes 147464 | tf_op jit(solution)/shard_map/ppermute | solution.py:322
  12.5 0.1 collective-permute-start.4
  12.6 0.4 %shard_map.97.plane = bf16[96,512]{1,0:T(8,128)(2,1)S(1)} custom-call(bf16[96,512]{1,0:T(8,128)(2,1)S(1)} %get-tuple-element.38.plane, bf16[96,256]{1,0:T(8,128)(2,1)S(1)} %get-tuple-element.39.zed, bf16[768,768]{1,0:T(8,128)(2,1)S(1)} %get-tuple-element.23.lam.refs_1_, bf16[768,768]{1,0:T(8,128)(2,1)S(1)} %get-tuple-element.24.mu.refs_2_, ...), custom_call_target="tpu_custom_call" | custom-call | tf_op jit(solution)/shard_map/pallas_call | solution.py:22
  13.0 1.2 %shard_map.98.early = bf16[1,2,3,816,384]{4,3,2,1,0:T(8,128)(2,1)} custom-call(bf16[96,512]{1,0:T(8,128)(2,1)S(1)} %shard_map.97.plane, bf16[816,16]{1,0:T(8,128)(2,1)S(1)} %get-tuple-element.40.basis), custom_call_target="tpu_custom_call" | custom-call | tf_op jit(solution)/shard_map/pallas_call | solution.py:22
  14.2 0.4 %collective-permute-done.3.from_off = f32[96,128]{1,0:T(8,128)S(1)} collective-permute-done((f32[96,128]{1,0:T(8,128)S(1)}, f32[96,128]{1,0:T(8,128)S(1)}, u32[]{:S(2)}, u32[]{:S(2)}) %collective-permute-start.3) | collective-permute-done | bytes 49184 | tf_op jit(solution)/shard_map/ppermute | solution.py:322
  14.5 0.0 collective-permute-done.4.from_chip
  14.5 1.7 %shard_map.99 = bf16[1,2,3,816,384]{4,3,2,1,0:T(8,128)(2,1)} custom-call(f32[96,256]{1,0:T(8,128)S(1)} %get-tuple-element.35.field, f32[96,128]{1,0:T(8,128)S(1)} %collective-permute-done.3.from_off, f32[96,128]{1,0:T(8,128)S(1)} %collective-permute-done.4.from_chip, ...), custom_call_target="tpu_custom_call", output_to_operand_aliasing={{}: (7, {})} | custom-call | tf_op jit(solution)/shard_map/pallas_call | solution.py:22
  (1 shorter events, 0.0 us)
Async XLA Ops:
  0.0 4.7 %copy-start = (bf16[1,2,3,8,768]{4,3,2,1,0:T(8,128)(2,1)S(1)}, bf16[1,2,3,8,768]{4,3,2,1,0:T(8,128)(2,1)}, u32[]{:S(2)}) copy-start(bf16[1,2,3,8,768]{4,3,2,1,0:T(8,128)(2,1)} %param.9) | copy-start | bytes 221188
  0.0 4.7 %copy-start.2 = (f32[16,15]{1,0:T(8,128)S(1)}, f32[16,15]{1,0:T(8,128)}, u32[]{:S(2)}) copy-start(f32[16,15]{1,0:T(8,128)} %nodes.3) | copy-start | bytes 2884
  0.0 4.7 %copy-start.4 = (f32[2,1,2,3,15]{4,2,3,1,0:T(2,128)S(1)}, f32[2,1,2,3,15]{4,2,3,1,0:T(2,128)}, u32[]{:S(2)}) copy-start(f32[2,1,2,3,15]{4,2,3,1,0:T(2,128)} %param.12) | copy-start | bytes 2164
  0.0 4.7 %copy-start.5 = (s32[1,2,3,128]{3,1,2,0:T(2,128)S(1)}, s32[1,2,3,128]{3,1,2,0:T(2,128)}, u32[]{:S(2)}) copy-start(s32[1,2,3,128]{3,1,2,0:T(2,128)} %param.17) | copy-start | bytes 9220
  0.0 5.6 %collective-permute-start = (bf16[48,768]{1,0:T(8,128)(2,1)}, bf16[48,768]{1,0:T(8,128)(2,1)S(1)}, u32[]{:S(2)}, u32[]{:S(2)}) collective-permute-start(bf16[48,768]{1,0:T(8,128)(2,1)} %bitcast.7), channel_id=1, source_target_pairs={{0,1},{1,0},{2,3},{3,2},{4,5},{5,4},{6,7},{7,6},{8,9},{9,8},{10,11... | collective-permute-start | bytes 221192 | tf_op jit(solution)/shard_map/ppermute | solution.py:310
  5.6 2.6 %copy-start.1 = (s32[816,15]{0,1:T(8,128)S(1)}, s32[816,15]{0,1:T(8,128)}, u32[]{:S(2)}) copy-start(s32[816,15]{0,1:T(8,128)} %param.15) | copy-start | bytes 146884
  5.6 2.6 %copy-start.3 = (s32[3,16,2,3]{1,2,3,0:T(2,128)S(1)}, s32[3,16,2,3]{1,2,3,0:T(2,128)}, u32[]{:S(2)}) copy-start(s32[3,16,2,3]{1,2,3,0:T(2,128)} %param.16) | copy-start | bytes 3460
  5.6 2.6 %copy-start.6 = (f32[16]{0:T(128)S(1)}, f32[16]{0:T(128)}, u32[]{:S(2)}) copy-start(f32[16]{0:T(128)} %param.14) | copy-start | bytes 196
  5.9 4.2 %collective-permute-start.1 = (f32[96,128]{1,0:T(8,128)S(1)}, f32[96,128]{1,0:T(8,128)S(1)}, u32[]{:S(2)}, u32[]{:S(2)}) collective-permute-start(f32[96,128]{1,0:T(8,128)S(1)} %get-tuple-element.30), channel_id=1, source_target_pairs={{0,1},{1,0},{2,4},{3,5},{4,2},{5,3},{6,8},{7,9},{8,6},{9,7},{10,12... | collective-permute-start | bytes 147464 | tf_op jit(solution)/shard_map/ppermute | solution.py:322
  8.0 2.1 %collective-permute-start.2 = (f32[96,128]{1,0:T(8,128)S(1)}, f32[96,128]{1,0:T(8,128)S(1)}, u32[]{:S(2)}, u32[]{:S(2)}) collective-permute-start(f32[96,128]{1,0:T(8,128)S(1)} %get-tuple-element.31), channel_id=1, source_target_pairs={{0,2},{2,0},{4,6},{6,4},{8,10},{10,8},{12,14},{14,12},{16,18},{18,... | collective-permute-start | bytes 147464 | tf_op jit(solution)/shard_map/ppermute | solution.py:323
  10.4 4.2 %collective-permute-start.3 = (f32[96,128]{1,0:T(8,128)S(1)}, f32[96,128]{1,0:T(8,128)S(1)}, u32[]{:S(2)}, u32[]{:S(2)}) collective-permute-start(f32[96,128]{1,0:T(8,128)S(1)} %get-tuple-element.36), channel_id=1, source_target_pairs={{0,1},{1,0},{2,4},{3,5},{4,2},{5,3},{6,8},{7,9},{8,6},{9,7},{10,12... | collective-permute-start | bytes 147464 | tf_op jit(solution)/shard_map/ppermute | solution.py:322
  12.5 2.1 %collective-permute-start.4 = (f32[96,128]{1,0:T(8,128)S(1)}, f32[96,128]{1,0:T(8,128)S(1)}, u32[]{:S(2)}, u32[]{:S(2)}) collective-permute-start(f32[96,128]{1,0:T(8,128)S(1)} %get-tuple-element.37), channel_id=1, source_target_pairs={{0,2},{2,0},{4,6},{6,4},{8,10},{10,8},{12,14},{14,12},{16,18},{18,... | collective-permute-start | bytes 147464 | tf_op jit(solution)/shard_map/ppermute | solution.py:323

commit v6 on v5

--- a/solution.py
+++ b/solution.py
@@ -318,7 +318,16 @@
         for s in range(parts)
     ]
 
-    def exchange(on_chip, off_chip):
+    second = across
+    if parts == 2 and layers >= 4:
+        top = layers - 1
+        steps = {(i, 1): (partner[i], 1) for i in partner}
+        steps.update({(i, 0): (i ^ 1, 0) for i in range(2, layers - 2)})
+        steps.update({(0, 1): (1, 0), (1, 0): (0, 0), (0, 0): (0, 1)})
+        steps.update({(top, 1): (top - 1, 0), (top - 1, 0): (top, 0), (top, 0): (top, 1)})
+        second = sorted((i * 2 + s, j * 2 + t) for (i, s), (j, t) in steps.items())
+
+    def exchange(on_chip, off_chip, across):
         far = lax.ppermute(off_chip, ("sub", "smp"), across)
         return lax.ppermute(on_chip, "sub", pairs), far
 
@@ -349,7 +358,7 @@
         [VMEM] * (parts + 5),
         [*others, lam, mu, mod, maps, own_lam, own_mu],
     )
-    near, far = exchange(on_chip, off_chip)
+    near, far = exchange(on_chip, off_chip, across)
     basis, masks = run(
         tables,
         [shaped((d.terms, d.samples), BF16), shaped((6, d.subs, 8, 128))],
@@ -375,7 +384,7 @@
         [field, far, near, maps, masks, mod, lam, mu, part_lam, part_mu],
         scratch=[pltpu.VMEM((rows, 2 * face), F32)],
     )
-    near, far = exchange(on_chip, off_chip)
+    near, far = exchange(on_chip, off_chip, second)
     (plane,) = run(
         second_plane,
         [shaped((rows, d.plane), BF16)],

time: 16.4 us -> 16.1 us (0.982)
  the two profiles are of different devices: /device:TPU:0 before, /device:TPU:10 now
where the time goes in v6:
time: 16.1 us; the launch traced here: 16 us
  Pallas kernels  7.31 us (45%)
  waiting for transfers between devices  4.92 us (31%)
  starting transfers between devices  3.6 us (22%)
    pallas_call x9, Pallas kernels, call(): pl.pallas_call(body, out_shape=outs, in_specs=specs, out_specs=[VMEM] * l...  7.31 us
    ppermute x2, waiting for transfers between devices, exchange(): far = lax.ppermute(off_chip, ('sub', 'smp'), across)  3.2 us
    ppermute x2, starting transfers between devices, exchange(): return (lax.ppermute(on_chip, 'sub', pairs), far)  2.77 us
    ppermute x1, waiting for transfers between devices, per_device(): lax.ppermute(own, 'smp', [(i, (i + shift) % parts) for i in range(parts)])  1.71 us
    ppermute x1, starting transfers between devices, per_device(): lax.ppermute(own, 'smp', [(i, (i + shift) % parts) for i in range(parts)])  0.6 us
  transfers between devices with their start and end apart: 5, of which 3 were waited for; matrix products, arithmetic and copies ran while one was open for 0% of the time, Pallas kernels for 31%

profile of v6, /device:TPU:10, one launch (start us, length us, event | category | flops | bytes accessed | tf_op | source)
XLA Modules:
  0.0 16.0 jit_solution(16044352829138846732)
XLA Ops:
  0.0 0.0 copy-start
  0.0 0.0 copy-start.2
  0.0 0.0 copy-start.4
  0.0 0.0 copy-start.5
  0.0 0.6 %collective-permute-start = (bf16[48,768]{1,0:T(8,128)(2,1)}, bf16[48,768]{1,0:T(8,128)(2,1)S(1)}, u32[]{:S(2)}, u32[]{:S(2)}) collective-permute-start(bf16[48,768]{1,0:T(8,128)(2,1)} %bitcast.7), channel_id=1, source_target_pairs={{0,1},{1,0},{2,3},{3,2},{4,5},{5,4},{6,7},{7,6},{8,9},{9,8},{10,11... | collective-permute-start | bytes 221192 | tf_op jit(solution)/shard_map/ppermute | solution.py:310
  0.6 1.6 %shard_map.91 = (bf16[768,768]{1,0:T(8,128)(2,1)S(1)}, bf16[768,768]{1,0:T(8,128)(2,1)S(1)}) custom-call(bf16[768,768]{1,0:T(8,128)(2,1)} %lam.1, bf16[768,768]{1,0:T(8,128)(2,1)} %mu.1), custom_call_target="tpu_custom_call" | custom-call | tf_op jit(solution)/shard_map/pallas_call | solution.py:22
  2.3 0.0 copy-done
  2.3 0.0 copy-done.2
  2.3 0.0 copy-done.4
  2.3 0.0 copy-done.5
  2.3 0.6 %shard_map.92 = (f32[2,96,128]{2,1,0:T(8,128)S(1)}, s32[2,6,8,128]{3,2,1,0:T(8,128)S(1)}, f32[48,768]{1,0:T(8,128)S(1)}, f32[48,768]{1,0:T(8,128)S(1)}) custom-call(bf16[48,768]{1,0:T(8,128)(2,1)S(1)} %bitcast.8, bf16[768,768]{1,0:T(8,128)(2,1)S(1)} %get-tuple-element.23.lam.refs_1_, bf16[768,768]{1,0:T(8,128)(2,1)S(1)} %get-tuple-element.24.mu.refs_2_, ...), custom_call_target="tpu_custom_call" | custom-call | tf_op jit(solution)/shard_map/pallas_call | solution.py:22
  2.9 1.7 %collective-permute-done.refs_0_ = bf16[48,768]{1,0:T(8,128)(2,1)S(1)} collective-permute-done((bf16[48,768]{1,0:T(8,128)(2,1)}, bf16[48,768]{1,0:T(8,128)(2,1)S(1)}, u32[]{:S(2)}, u32[]{:S(2)}) %collective-permute-start) | collective-permute-done | bytes 73760 | tf_op jit(solution)/shard_map/ppermute | solution.py:310
  4.7 0.0 copy-start.3
  4.7 0.0 copy-start.6
  4.7 0.3 %shard_map.93 = (f32[96,256]{1,0:T(8,128)S(1)}, f32[96,128]{1,0:T(8,128)S(1)}, f32[96,128]{1,0:T(8,128)S(1)}) custom-call(bf16[48,768]{1,0:T(8,128)(2,1)S(1)} %collective-permute-done.refs_0_, bf16[768,768]{1,0:T(8,128)(2,1)S(1)} %get-tuple-element.23.lam.refs_1_, bf16[768,768]{1,0:T(8,128)(2,1)S(1)} %get-tuple-element.24.mu.refs_2_, ...), custom_call_target="tpu_custom_call" | custom-call | tf_op jit(solution)/shard_map/pallas_call | solution.py:22
  5.0 0.1 collective-permute-start.1
  5.1 1.6 %collective-permute-start.2 = (f32[96,128]{1,0:T(8,128)S(1)}, f32[96,128]{1,0:T(8,128)S(1)}, u32[]{:S(2)}, u32[]{:S(2)}) collective-permute-start(f32[96,128]{1,0:T(8,128)S(1)} %get-tuple-element.31), channel_id=1, source_target_pairs={{0,2},{2,0},{4,6},{6,4},{8,10},{10,8},{12,14},{14,12},{16,18},{18,... | collective-permute-start | bytes 147464 | tf_op jit(solution)/shard_map/ppermute | solution.py:332
  6.7 0.0 copy-done.1
  6.7 0.0 copy-done.3
  6.7 0.0 copy-done.6
  6.7 0.5 %shard_map.94 = (bf16[816,16]{1,0:T(8,128)(2,1)S(1)}, f32[6,6,8,128]{3,2,1,0:T(8,128)S(1)}) custom-call(f32[16,15]{1,0:T(8,128)S(1)} %copy-done.2, f32[1,16]{1,0:T(1,128)S(1)} %bitcast.13, s32[15,816]{1,0:T(8,128)S(1)} %bitcast.9, s32[3,3,2,16]{3,2,1,0:T(2,128)S(1)} %bitcast.10), custom_call_target="tpu_custom_call" | custom-call | tf_op jit(solution)/shard_map/pallas_call | solution.py:22
  7.2 0.6 %shard_map.95 = (bf16[96,512]{1,0:T(8,128)(2,1)S(1)}, f32[96,256]{1,0:T(8,128)S(1)}, f32[96,256]{1,0:T(8,128)S(1)}) custom-call(bf16[48,768]{1,0:T(8,128)(2,1)S(1)} %collective-permute-done.refs_0_, bf16[768,768]{1,0:T(8,128)(2,1)S(1)} %get-tuple-element.23.lam.refs_1_, bf16[768,768]{1,0:T(8,128)(2,1)S(1)} %get-tuple-element.24.mu.refs_2_, ...), custom_call_target="tpu_custom_call" | custom-call | tf_op jit(solution)/shard_map/pallas_call | solution.py:22
  7.8 1.7 %collective-permute-done.1.from_off = f32[96,128]{1,0:T(8,128)S(1)} collective-permute-done((f32[96,128]{1,0:T(8,128)S(1)}, f32[96,128]{1,0:T(8,128)S(1)}, u32[]{:S(2)}, u32[]{:S(2)}) %collective-permute-start.1) | collective-permute-done | bytes 49184 | tf_op jit(solution)/shard_map/ppermute | solution.py:331
  9.5 0.0 collective-permute-done.2.from_chip
  9.5 0.3 %shard_map.96 = (bf16[96,256]{1,0:T(8,128)(2,1)S(1)}, f32[96,256]{1,0:T(8,128)S(1)}, f32[96,128]{1,0:T(8,128)S(1)}, f32[96,128]{1,0:T(8,128)S(1)}) custom-call(f32[96,256]{1,0:T(8,128)S(1)} %get-tuple-element.29.field, f32[96,128]{1,0:T(8,128)S(1)} %collective-permute-done.1.from_off, f32[96,128]{1,0:T(8,128)S(1)} %collective-permute-done.2.from_chip, ...), custom_call_target="tpu_custom_call" | custom-call | tf_op jit(solution)/shard_map/pallas_call | solution.py:22
  9.8 0.2 %collective-permute-start.3 = (f32[96,128]{1,0:T(8,128)S(1)}, f32[96,128]{1,0:T(8,128)S(1)}, u32[]{:S(2)}, u32[]{:S(2)}) collective-permute-start(f32[96,128]{1,0:T(8,128)S(1)} %get-tuple-element.36), channel_id=1, source_target_pairs={{0,1},{1,2},{2,0},{3,5},{4,6},{5,3},{6,4},{7,9},{8,10},{9,7},{10,8... | collective-permute-start | bytes 147464 | tf_op jit(solution)/shard_map/ppermute | solution.py:331
  9.9 1.2 %collective-permute-start.4 = (f32[96,128]{1,0:T(8,128)S(1)}, f32[96,128]{1,0:T(8,128)S(1)}, u32[]{:S(2)}, u32[]{:S(2)}) collective-permute-start(f32[96,128]{1,0:T(8,128)S(1)} %get-tuple-element.37), channel_id=1, source_target_pairs={{0,2},{2,0},{4,6},{6,4},{8,10},{10,8},{12,14},{14,12},{16,18},{18,... | collective-permute-start | bytes 147464 | tf_op jit(solution)/shard_map/ppermute | solution.py:332
  11.1 0.4 %shard_map.97.plane = bf16[96,512]{1,0:T(8,128)(2,1)S(1)} custom-call(bf16[96,512]{1,0:T(8,128)(2,1)S(1)} %get-tuple-element.38.plane, bf16[96,256]{1,0:T(8,128)(2,1)S(1)} %get-tuple-element.39.zed, bf16[768,768]{1,0:T(8,128)(2,1)S(1)} %get-tuple-element.23.lam.refs_1_, bf16[768,768]{1,0:T(8,128)(2,1)S(1)} %get-tuple-element.24.mu.refs_2_, ...), custom_call_target="tpu_custom_call" | custom-call | tf_op jit(solution)/shard_map/pallas_call | solution.py:22
  11.5 1.2 %shard_map.98.early = bf16[1,2,3,816,384]{4,3,2,1,0:T(8,128)(2,1)} custom-call(bf16[96,512]{1,0:T(8,128)(2,1)S(1)} %shard_map.97.plane, bf16[816,16]{1,0:T(8,128)(2,1)S(1)} %get-tuple-element.40.basis), custom_call_target="tpu_custom_call" | custom-call | tf_op jit(solution)/shard_map/pallas_call | solution.py:22
  12.7 1.5 %collective-permute-done.3.from_off = f32[96,128]{1,0:T(8,128)S(1)} collective-permute-done((f32[96,128]{1,0:T(8,128)S(1)}, f32[96,128]{1,0:T(8,128)S(1)}, u32[]{:S(2)}, u32[]{:S(2)}) %collective-permute-start.3) | collective-permute-done | bytes 49184 | tf_op jit(solution)/shard_map/ppermute | solution.py:331
  14.3 0.0 collective-permute-done.4.from_chip
  14.3 1.7 %shard_map.99 = bf16[1,2,3,816,384]{4,3,2,1,0:T(8,128)(2,1)} custom-call(f32[96,256]{1,0:T(8,128)S(1)} %get-tuple-element.35.field, f32[96,128]{1,0:T(8,128)S(1)} %collective-permute-done.3.from_off, f32[96,128]{1,0:T(8,128)S(1)} %collective-permute-done.4.from_chip, ...), custom_call_target="tpu_custom_call", output_to_operand_aliasing={{}: (7, {})} | custom-call | tf_op jit(solution)/shard_map/pallas_call | solution.py:22
  (1 shorter events, 0.0 us)
Async XLA Ops:
  0.0 2.3 %copy-start = (bf16[1,2,3,8,768]{4,3,2,1,0:T(8,128)(2,1)S(1)}, bf16[1,2,3,8,768]{4,3,2,1,0:T(8,128)(2,1)}, u32[]{:S(2)}) copy-start(bf16[1,2,3,8,768]{4,3,2,1,0:T(8,128)(2,1)} %param.9) | copy-start | bytes 221188
  0.0 2.3 %copy-start.2 = (f32[16,15]{1,0:T(8,128)S(1)}, f32[16,15]{1,0:T(8,128)}, u32[]{:S(2)}) copy-start(f32[16,15]{1,0:T(8,128)} %nodes.3) | copy-start | bytes 2884
  0.0 2.3 %copy-start.4 = (f32[2,1,2,3,15]{4,2,3,1,0:T(2,128)S(1)}, f32[2,1,2,3,15]{4,2,3,1,0:T(2,128)}, u32[]{:S(2)}) copy-start(f32[2,1,2,3,15]{4,2,3,1,0:T(2,128)} %param.12) | copy-start | bytes 2164
  0.0 2.3 %copy-start.5 = (s32[1,2,3,128]{3,1,2,0:T(2,128)S(1)}, s32[1,2,3,128]{3,1,2,0:T(2,128)}, u32[]{:S(2)}) copy-start(s32[1,2,3,128]{3,1,2,0:T(2,128)} %param.17) | copy-start | bytes 9220
  0.0 4.6 %collective-permute-start = (bf16[48,768]{1,0:T(8,128)(2,1)}, bf16[48,768]{1,0:T(8,128)(2,1)S(1)}, u32[]{:S(2)}, u32[]{:S(2)}) collective-permute-start(bf16[48,768]{1,0:T(8,128)(2,1)} %bitcast.7), channel_id=1, source_target_pairs={{0,1},{1,0},{2,3},{3,2},{4,5},{5,4},{6,7},{7,6},{8,9},{9,8},{10,11... | collective-permute-start | bytes 221192 | tf_op jit(solution)/shard_map/ppermute | solution.py:310
  4.6 2.0 %copy-start.1 = (s32[816,15]{0,1:T(8,128)S(1)}, s32[816,15]{0,1:T(8,128)}, u32[]{:S(2)}) copy-start(s32[816,15]{0,1:T(8,128)} %param.15) | copy-start | bytes 146884
  4.7 2.0 %copy-start.3 = (s32[3,16,2,3]{1,2,3,0:T(2,128)S(1)}, s32[3,16,2,3]{1,2,3,0:T(2,128)}, u32[]{:S(2)}) copy-start(s32[3,16,2,3]{1,2,3,0:T(2,128)} %param.16) | copy-start | bytes 3460
  4.7 2.0 %copy-start.6 = (f32[16]{0:T(128)S(1)}, f32[16]{0:T(128)}, u32[]{:S(2)}) copy-start(f32[16]{0:T(128)} %param.14) | copy-start | bytes 196
  5.0 4.5 %collective-permute-start.1 = (f32[96,128]{1,0:T(8,128)S(1)}, f32[96,128]{1,0:T(8,128)S(1)}, u32[]{:S(2)}, u32[]{:S(2)}) collective-permute-start(f32[96,128]{1,0:T(8,128)S(1)} %get-tuple-element.30), channel_id=1, source_target_pairs={{0,1},{1,0},{2,4},{3,5},{4,2},{5,3},{6,8},{7,9},{8,6},{9,7},{10,12... | collective-permute-start | bytes 147464 | tf_op jit(solution)/shard_map/ppermute | solution.py:331
  5.1 4.4 %collective-permute-start.2 = (f32[96,128]{1,0:T(8,128)S(1)}, f32[96,128]{1,0:T(8,128)S(1)}, u32[]{:S(2)}, u32[]{:S(2)}) collective-permute-start(f32[96,128]{1,0:T(8,128)S(1)} %get-tuple-element.31), channel_id=1, source_target_pairs={{0,2},{2,0},{4,6},{6,4},{8,10},{10,8},{12,14},{14,12},{16,18},{18,... | collective-permute-start | bytes 147464 | tf_op jit(solution)/shard_map/ppermute | solution.py:332
  9.8 4.5 %collective-permute-start.3 = (f32[96,128]{1,0:T(8,128)S(1)}, f32[96,128]{1,0:T(8,128)S(1)}, u32[]{:S(2)}, u32[]{:S(2)}) collective-permute-start(f32[96,128]{1,0:T(8,128)S(1)} %get-tuple-element.36), channel_id=1, source_target_pairs={{0,1},{1,2},{2,0},{3,5},{4,6},{5,3},{6,4},{7,9},{8,10},{9,7},{10,8... | collective-permute-start | bytes 147464 | tf_op jit(solution)/shard_map/ppermute | solution.py:331
  9.9 4.3 %collective-permute-start.4 = (f32[96,128]{1,0:T(8,128)S(1)}, f32[96,128]{1,0:T(8,128)S(1)}, u32[]{:S(2)}, u32[]{:S(2)}) collective-permute-start(f32[96,128]{1,0:T(8,128)S(1)} %get-tuple-element.37), channel_id=1, source_target_pairs={{0,2},{2,0},{4,6},{6,4},{8,10},{10,8},{12,14},{14,12},{16,18},{18,... | collective-permute-start | bytes 147464 | tf_op jit(solution)/shard_map/ppermute | solution.py:332

commit v7 on v6

--- a/solution.py
+++ b/solution.py
@@ -11,6 +11,7 @@
 BF16 = jnp.bfloat16
 VMEM = pl.BlockSpec(memory_space=pltpu.VMEM)
 CHUNK = 144
+PAD = 8
 HBM = pl.BlockSpec(memory_space=pltpu.HBM)
 
 
@@ -206,6 +207,22 @@
             out(1, rows, masks[5, n] * (field[rows, d.face :] - matched))
 
 
+def side_jumps(d, near, field, taken, maps, masks, out):
+    layer = lax.axis_index("sub")
+    even = lax.rem(layer, 2) == 0
+    up = even if near else jnp.logical_not(even)
+    inside = jnp.logical_and(layer > 0, layer < lax.axis_size("sub") - 1)
+    for n in range(d.subs):
+        for start in range(n * d.samples, (n + 1) * d.samples, 8):
+            rows = slice(start, start + 8)
+            other = taken[rows, :] if near else jnp.where(inside, taken[rows, :], 0.0)
+            matched = jnp.take_along_axis(other, maps[0, n], axis=1, mode="promise_in_bounds")
+            above = masks[5, n] * (field[rows, d.face :] - matched)
+            below = masks[4, n] * (field[rows, : d.face] - other)
+            out[rows, :] = jnp.where(up, above, below)
+    return pl.ds(pl.multiple_of(jnp.where(up, 2, 1) * d.face, 128), d.face)
+
+
 def first_plane(d, *refs):
     others = refs[: d.parts - 1]
     lam, mu, mod, own_lam, own_mu, masks, jumps, part_lam, part_mu, field = refs[d.parts - 1 :]
@@ -237,6 +254,7 @@
     two = part_mu[...] + dot(rounded, mu[d.plane :, d.plane :])
     result[...] = wide(mod[0], 2 * d.face) * one + wide(mod[1], 2 * d.face) * two
     payloads(d, result[:, : d.face], result[:, d.face :], maps, on_chip, off_chip)
+    off_chip[d.rows :, :] = jnp.zeros((PAD, d.face), F32)
 
 
 def second_plane(d, plane, zed, lam, mu, mod, masks, jumps):
@@ -260,7 +278,7 @@
 
 
 def project_rows(d, picks, lanes, basis, out, rows_out, sem):
-    width = lanes.stop - lanes.start
+    width = rows_out.shape[-1]
     group = max(g for g in (1, 2, 3, 6) if d.subs % g == 0 and g * width <= 768)
     for n in range(0, d.subs, group):
         right = picks[n : n + group]
@@ -271,31 +289,52 @@
             for m in range(group):
                 y, x = divmod(n + m, d.breadth)
                 rows_out[y, x, rows, :] = value[:, m * width : (m + 1) * width].astype(BF16)
-                pltpu.make_async_copy(
-                    rows_out.at[y, x, rows, :], out.at[0, y, x, rows, lanes], sem
-                ).start()
-    pltpu.make_async_copy(rows_out, out.at[0, :, :, :, lanes], sem).wait()
-
-
-def project_early(d, plane, basis, out, rows_out, sem):
-    start = pl.multiple_of(lax.axis_index("smp") * d.share, 128)
-    picks = [plane[d.block(n), pl.ds(start, d.face)] for n in range(d.subs)]
-    project_rows(d, picks, slice(0, d.face), basis, out, rows_out, sem)
-
-
-def project_late(
-    d, field, from_off, from_chip, maps, masks, plane, basis, early, out, held, jumps, rows_out, sem
-):
-    last_z(d, field, from_off, from_chip, maps, masks, plane, jumps, held)
-    width = d.share - d.face
-    start = pl.multiple_of(lax.axis_index("smp") * d.share + d.face, 128)
-    picks = [jumps[d.block(n), pl.ds(start, width)] for n in range(d.subs)]
-    project_rows(d, picks, slice(d.face, d.share), basis, out, rows_out, sem)
+                if out is not None:
+                    pltpu.make_async_copy(
+                        rows_out.at[y, x, rows, :], out.at[0, y, x, rows, lanes], sem
+                    ).start()
+    if out is not None:
+        return pltpu.make_async_copy(rows_out, out.at[0, :, :, :, lanes], sem)
+
+
+def project_plane(d, plane, basis, out, plane_out, all_out, sem):
+    part = lax.axis_index("smp")
+
+    @pl.when(part == 0)
+    def _():
+        picks = [plane[d.block(n), : d.share] for n in range(d.subs)]
+        project_rows(d, picks, slice(0, d.share), basis, out, all_out, sem).wait()
+
+    @pl.when(part == 1)
+    def _():
+        picks = [plane[d.block(n), d.share :] for n in range(d.subs)]
+        project_rows(d, picks, None, basis, None, plane_out, None)
+
+
+def project_near(d, field, near, maps, masks, basis, plane_out, early, out, held, near_out, sems):
+    @pl.when(lax.axis_index("smp") == 1)
+    def _():
+        at = slice(0, d.face)
+        first = pltpu.make_async_copy(plane_out, out.at[0, :, :, :, at], sems.at[0])
+        first.start()
+        lanes = side_jumps(d, True, field, near, maps, masks, held)
+        picks = [held[d.block(n), :].astype(BF16) for n in range(d.subs)]
+        second = project_rows(d, picks, lanes, basis, out, near_out, sems.at[1])
+        first.wait()
+        second.wait()
+
+
+def project_late(d, field, far, maps, masks, basis, early, out, held, far_out, sem):
+    @pl.when(lax.axis_index("smp") == 1)
+    def _():
+        lanes = side_jumps(d, False, field, far, maps, masks, held)
+        picks = [held[d.block(n), :].astype(BF16) for n in range(d.subs)]
+        project_rows(d, picks, lanes, basis, out, far_out, sem).wait()
 
 
 def project_share(d, jumps, basis, out, rows_out, sem):
     picks = [jumps[d.block(n), :] for n in range(d.subs)]
-    project_rows(d, picks, slice(0, d.share), basis, out, rows_out, sem)
+    project_rows(d, picks, slice(0, d.share), basis, out, rows_out, sem).wait()
 
 
 def per_device(
@@ -378,7 +417,7 @@
             shaped((rows, 2 * face), BF16),
             shaped((rows, 2 * face)),
             shaped((rows, face)),
-            shaped((rows, face)),
+            shaped((rows + PAD, face)),
         ],
         [VMEM] * 10,
         [field, far, near, maps, masks, mod, lam, mu, part_lam, part_mu],
@@ -391,40 +430,52 @@
         [VMEM] * 6,
         [jumps_plane, jumps_z, lam, mu, mod, masks],
     )
-    last = [field, far, near, maps, masks, plane]
-    held = pltpu.VMEM((rows, 2 * face), F32)
     result = [shaped((1, d.height, d.breadth, d.terms, d.share), BF16)]
 
-    def buffers(width):
-        return [
-            pltpu.VMEM((d.height, d.breadth, d.terms, width), BF16),
-            pltpu.SemaphoreType.DMA(()),
-        ]
-
-    if d.share == 3 * face:
-        (early,) = run(
-            project_early,
-            result,
+    def rows_out(width):
+        return pltpu.VMEM((d.height, d.breadth, d.terms, width), BF16)
+
+    if parts == 2:
+        held = pltpu.VMEM((rows, face), F32)
+        early, plane_out = run(
+            project_plane,
+            result + [shaped((d.height, d.breadth, d.terms, face), BF16)],
             [VMEM] * 2,
             [plane, basis],
+            out_specs=[HBM, VMEM],
+            scratch=[rows_out(d.share), pltpu.SemaphoreType.DMA(())],
+        )
+        (early,) = run(
+            project_near,
+            result,
+            [VMEM] * 6 + [HBM],
+            [field, near, maps, masks, basis, plane_out, early],
             out_specs=[HBM],
-            scratch=buffers(face),
+            scratch=[held, rows_out(face), pltpu.SemaphoreType.DMA((2,))],
+            aliases={6: 0},
         )
         (out,) = run(
             project_late,
             result,
-            [VMEM] * 7 + [HBM],
-            [*last, basis, early],
+            [VMEM] * 5 + [HBM],
+            [field, far, maps, masks, basis, early],
             out_specs=[HBM],
-            scratch=[held, pltpu.VMEM((rows, d.width), BF16)] + buffers(2 * face),
-            aliases={7: 0},
+            scratch=[held, rows_out(face), pltpu.SemaphoreType.DMA(())],
+            aliases={5: 0},
         )
     else:
+        last = [field, far, near, maps, masks, plane]
+        held = pltpu.VMEM((rows, 2 * face), F32)
         (jumps,) = run(last_z, [shaped((rows, d.width), BF16)], [VMEM] * 6, last, scratch=[held])
         start = lax.axis_index("smp") * d.share
         jumps = lax.dynamic_slice_in_dim(jumps, start, d.share, 1)
         (out,) = run(
-            project_share, result, [VMEM] * 2, [jumps, basis], out_specs=[HBM], scratch=buffers(d.share)
+            project_share,
+            result,
+            [VMEM] * 2,
+            [jumps, basis],
+            out_specs=[HBM],
+            scratch=[rows_out(d.share), pltpu.SemaphoreType.DMA(())],
         )
     return jnp.swapaxes(out, -1, -2)
 

time: 16.1 us -> 15.8 us (0.981)
  waiting for transfers between devices: 4.92 us -> 4.11 us
  Pallas kernels: 7.31 us -> 7.71 us
    ppermute x2, waiting for transfers between devices: 3.2 us -> 2.39 us  [exchange(): far = lax.ppermute(off_chip, ('sub', 'smp'), across)]
    pallas_call x9 -> x10, Pallas kernels: 7.31 us -> 7.71 us  [call(): pl.pallas_call(body, out_shape=outs, in_specs=specs, out_specs=[VMEM] * l...]
  transfers between devices with their start and end apart: 5 -> 5, of which waited for: 3 -> 3; matrix products, arithmetic and copies ran while one was open for 0% -> 0% of each run, Pallas kernels for 31% -> 37%
where the time goes in v7:
time: 15.8 us; the launch traced here: 15.6 us
  Pallas kernels  7.71 us (49%)
  waiting for transfers between devices  4.11 us (26%)
  starting transfers between devices  3.6 us (23%)
    pallas_call x10, Pallas kernels, call(): pl.pallas_call(body, out_shape=outs, in_specs=specs, out_specs=[VMEM] * l...  7.71 us
    ppermute x2, starting transfers between devices, exchange(): return (lax.ppermute(on_chip, 'sub', pairs), far)  2.77 us
    ppermute x2, waiting for transfers between devices, exchange(): far = lax.ppermute(off_chip, ('sub', 'smp'), across)  2.39 us
    ppermute x1, waiting for transfers between devices, per_device(): lax.ppermute(own, 'smp', [(i, (i + shift) % parts) for i in range(parts)])  1.71 us
    ppermute x1, starting transfers between devices, per_device(): lax.ppermute(own, 'smp', [(i, (i + shift) % parts) for i in range(parts)])  0.6 us
  transfers between devices with their start and end apart: 5, of which 3 were waited for; matrix products, arithmetic and copies ran while one was open for 0% of the time, Pallas kernels for 37%

profile of v7, /device:TPU:10, one launch (start us, length us, event | category | flops | bytes accessed | tf_op | source)
XLA Modules:
  0.0 15.6 jit_solution(5149743289413136803)
XLA Ops:
  0.0 0.0 copy-start
  0.0 0.0 copy-start.2
  0.0 0.0 copy-start.5
  0.0 0.0 copy-start.4
  0.0 0.6 %collective-permute-start = (bf16[48,768]{1,0:T(8,128)(2,1)}, bf16[48,768]{1,0:T(8,128)(2,1)S(1)}, u32[]{:S(2)}, u32[]{:S(2)}) collective-permute-start(bf16[48,768]{1,0:T(8,128)(2,1)} %bitcast.7), channel_id=1, source_target_pairs={{0,1},{1,0},{2,3},{3,2},{4,5},{5,4},{6,7},{7,6},{8,9},{9,8},{10,11... | collective-permute-start | bytes 221192 | tf_op jit(solution)/shard_map/ppermute | solution.py:349
  0.6 1.6 %shard_map.91 = (bf16[768,768]{1,0:T(8,128)(2,1)S(1)}, bf16[768,768]{1,0:T(8,128)(2,1)S(1)}) custom-call(bf16[768,768]{1,0:T(8,128)(2,1)} %lam.1, bf16[768,768]{1,0:T(8,128)(2,1)} %mu.1), custom_call_target="tpu_custom_call" | custom-call | tf_op jit(solution)/shard_map/pallas_call | solution.py:23
  2.3 0.0 copy-done
  2.3 0.0 copy-done.2
  2.3 0.0 copy-done.5
  2.3 0.0 copy-done.4
  2.3 0.6 %shard_map.92 = (f32[2,96,128]{2,1,0:T(8,128)S(1)}, s32[2,6,8,128]{3,2,1,0:T(8,128)S(1)}, f32[48,768]{1,0:T(8,128)S(1)}, f32[48,768]{1,0:T(8,128)S(1)}) custom-call(bf16[48,768]{1,0:T(8,128)(2,1)S(1)} %bitcast.8, bf16[768,768]{1,0:T(8,128)(2,1)S(1)} %get-tuple-element.25.lam.refs_1_, bf16[768,768]{1,0:T(8,128)(2,1)S(1)} %get-tuple-element.26.mu.refs_2_, ...), custom_call_target="tpu_custom_call" | custom-call | tf_op jit(solution)/shard_map/pallas_call | solution.py:23
  2.9 1.7 %collective-permute-done.refs_0_ = bf16[48,768]{1,0:T(8,128)(2,1)S(1)} collective-permute-done((bf16[48,768]{1,0:T(8,128)(2,1)}, bf16[48,768]{1,0:T(8,128)(2,1)S(1)}, u32[]{:S(2)}, u32[]{:S(2)}) %collective-permute-start) | collective-permute-done | bytes 73760 | tf_op jit(solution)/shard_map/ppermute | solution.py:349
  4.6 0.0 copy-start.1
  4.7 0.3 %shard_map.93 = (f32[96,256]{1,0:T(8,128)S(1)}, f32[96,128]{1,0:T(8,128)S(1)}, f32[96,128]{1,0:T(8,128)S(1)}) custom-call(bf16[48,768]{1,0:T(8,128)(2,1)S(1)} %collective-permute-done.refs_0_, bf16[768,768]{1,0:T(8,128)(2,1)S(1)} %get-tuple-element.25.lam.refs_1_, bf16[768,768]{1,0:T(8,128)(2,1)S(1)} %get-tuple-element.26.mu.refs_2_, ...), custom_call_target="tpu_custom_call" | custom-call | tf_op jit(solution)/shard_map/pallas_call | solution.py:23
  5.0 0.1 collective-permute-start.1
  5.1 1.6 %collective-permute-start.2 = (f32[96,128]{1,0:T(8,128)S(1)}, f32[96,128]{1,0:T(8,128)S(1)}, u32[]{:S(2)}, u32[]{:S(2)}) collective-permute-start(f32[96,128]{1,0:T(8,128)S(1)} %get-tuple-element.33), channel_id=1, source_target_pairs={{0,2},{2,0},{4,6},{6,4},{8,10},{10,8},{12,14},{14,12},{16,18},{18,... | collective-permute-start | bytes 147464 | tf_op jit(solution)/shard_map/ppermute | solution.py:371
  6.7 0.0 copy-done.1
  6.7 0.0 copy-done.3
  6.7 0.0 copy-done.6
  6.7 0.5 %shard_map.94 = (bf16[816,16]{1,0:T(8,128)(2,1)S(1)}, f32[6,6,8,128]{3,2,1,0:T(8,128)S(1)}) custom-call(f32[16,15]{1,0:T(8,128)S(1)} %copy-done.2, f32[1,16]{1,0:T(1,128)S(1)} %bitcast.13, s32[15,816]{1,0:T(8,128)S(1)} %bitcast.9, s32[3,3,2,16]{3,2,1,0:T(2,128)S(1)} %bitcast.10), custom_call_target="tpu_custom_call" | custom-call | tf_op jit(solution)/shard_map/pallas_call | solution.py:23
  7.2 0.6 %shard_map.95 = (bf16[96,512]{1,0:T(8,128)(2,1)S(1)}, f32[96,256]{1,0:T(8,128)S(1)}, f32[96,256]{1,0:T(8,128)S(1)}) custom-call(bf16[48,768]{1,0:T(8,128)(2,1)S(1)} %collective-permute-done.refs_0_, bf16[768,768]{1,0:T(8,128)(2,1)S(1)} %get-tuple-element.25.lam.refs_1_, bf16[768,768]{1,0:T(8,128)(2,1)S(1)} %get-tuple-element.26.mu.refs_2_, ...), custom_call_target="tpu_custom_call" | custom-call | tf_op jit(solution)/shard_map/pallas_call | solution.py:23
  7.8 1.7 %collective-permute-done.1.from_off = f32[96,128]{1,0:T(8,128)S(1)} collective-permute-done((f32[96,128]{1,0:T(8,128)S(1)}, f32[96,128]{1,0:T(8,128)S(1)}, u32[]{:S(2)}, u32[]{:S(2)}) %collective-permute-start.1) | collective-permute-done | bytes 49184 | tf_op jit(solution)/shard_map/ppermute | solution.py:370
  9.5 0.0 collective-permute-done.2.from_chip
  9.5 0.3 %shard_map.96 = (bf16[96,256]{1,0:T(8,128)(2,1)S(1)}, f32[96,256]{1,0:T(8,128)S(1)}, f32[96,128]{1,0:T(8,128)S(1)}, f32[104,128]{1,0:T(8,128)S(1)}) custom-call(f32[96,256]{1,0:T(8,128)S(1)} %get-tuple-element.31.field, f32[96,128]{1,0:T(8,128)S(1)} %collective-permute-done.1.from_off, f32[96,128]{1,0:T(8,128)S(1)} %collective-permute-done.2.from_chip, ...), custom_call_target="tpu_custom_call" | custom-call | tf_op jit(solution)/shard_map/pallas_call | solution.py:23
  9.8 0.2 %collective-permute-start.3 = (f32[104,128]{1,0:T(8,128)S(1)}, f32[104,128]{1,0:T(8,128)S(1)}, u32[]{:S(2)}, u32[]{:S(2)}) collective-permute-start(f32[104,128]{1,0:T(8,128)S(1)} %get-tuple-element.38), channel_id=1, source_target_pairs={{0,1},{1,2},{2,0},{3,5},{4,6},{5,3},{6,4},{7,9},{8,10},{9,7},{10,8... | collective-permute-start | bytes 159752 | tf_op jit(solution)/shard_map/ppermute | solution.py:370
  10.0 1.1 %collective-permute-start.4 = (f32[96,128]{1,0:T(8,128)S(1)}, f32[96,128]{1,0:T(8,128)S(1)}, u32[]{:S(2)}, u32[]{:S(2)}) collective-permute-start(f32[96,128]{1,0:T(8,128)S(1)} %get-tuple-element.40), channel_id=1, source_target_pairs={{0,2},{2,0},{4,6},{6,4},{8,10},{10,8},{12,14},{14,12},{16,18},{18,... | collective-permute-start | bytes 147464 | tf_op jit(solution)/shard_map/ppermute | solution.py:371
  11.1 0.4 %shard_map.97.plane = bf16[96,512]{1,0:T(8,128)(2,1)S(1)} custom-call(bf16[96,512]{1,0:T(8,128)(2,1)S(1)} %get-tuple-element.41.plane, bf16[96,256]{1,0:T(8,128)(2,1)S(1)} %get-tuple-element.42.zed, bf16[768,768]{1,0:T(8,128)(2,1)S(1)} %get-tuple-element.25.lam.refs_1_, bf16[768,768]{1,0:T(8,128)(2,1)S(1)} %get-tuple-element.26.mu.refs_2_, ...), custom_call_target="tpu_custom_call" | custom-call | tf_op jit(solution)/shard_map/pallas_call | solution.py:23
  11.5 0.5 %shard_map.98 = (bf16[1,2,3,816,384]{4,3,2,1,0:T(8,128)(2,1)}, bf16[2,3,816,128]{3,2,1,0:T(8,128)(2,1)S(1)}) custom-call(bf16[96,512]{1,0:T(8,128)(2,1)S(1)} %shard_map.97.plane, bf16[816,16]{1,0:T(8,128)(2,1)S(1)} %get-tuple-element.39.basis), custom_call_target="tpu_custom_call" | custom-call | tf_op jit(solution)/shard_map/pallas_call | solution.py:23
  12.0 0.0 collective-permute-done.4.near
  12.0 1.5 %shard_map.99.early = bf16[1,2,3,816,384]{4,3,2,1,0:T(8,128)(2,1)} custom-call(f32[96,256]{1,0:T(8,128)S(1)} %get-tuple-element.37.field, f32[96,128]{1,0:T(8,128)S(1)} %collective-permute-done.4.near, s32[2,6,8,128]{3,2,1,0:T(8,128)S(1)} %get-tuple-element.28.refs_4_.maps, ...), custom_call_target="tpu_custom_call", output_to_operand_aliasing={{}: (6, {})} | custom-call | tf_op jit(solution)/shard_map/pallas_call | solution.py:23
  13.6 0.7 %collective-permute-done.3.far = f32[104,128]{1,0:T(8,128)S(1)} collective-permute-done((f32[104,128]{1,0:T(8,128)S(1)}, f32[104,128]{1,0:T(8,128)S(1)}, u32[]{:S(2)}, u32[]{:S(2)}) %collective-permute-start.3) | collective-permute-done | bytes 53280 | tf_op jit(solution)/shard_map/ppermute | solution.py:370
  14.3 1.3 %shard_map.100 = bf16[1,2,3,816,384]{4,3,2,1,0:T(8,128)(2,1)} custom-call(f32[96,256]{1,0:T(8,128)S(1)} %get-tuple-element.37.field, f32[104,128]{1,0:T(8,128)S(1)} %collective-permute-done.3.far, s32[2,6,8,128]{3,2,1,0:T(8,128)S(1)} %get-tuple-element.28.refs_4_.maps, ...), custom_call_target="tpu_custom_call", output_to_operand_aliasing={{}: (5, {})} | custom-call | tf_op jit(solution)/shard_map/pallas_call | solution.py:23
  (2 shorter events, 0.0 us)
Async XLA Ops:
  0.0 2.3 %copy-start = (bf16[1,2,3,8,768]{4,3,2,1,0:T(8,128)(2,1)S(1)}, bf16[1,2,3,8,768]{4,3,2,1,0:T(8,128)(2,1)}, u32[]{:S(2)}) copy-start(bf16[1,2,3,8,768]{4,3,2,1,0:T(8,128)(2,1)} %param.9) | copy-start | bytes 221188
  0.0 2.3 %copy-start.2 = (f32[16,15]{1,0:T(8,128)S(1)}, f32[16,15]{1,0:T(8,128)}, u32[]{:S(2)}) copy-start(f32[16,15]{1,0:T(8,128)} %nodes.3) | copy-start | bytes 2884
  0.0 2.3 %copy-start.5 = (s32[1,2,3,128]{3,1,2,0:T(2,128)S(1)}, s32[1,2,3,128]{3,1,2,0:T(2,128)}, u32[]{:S(2)}) copy-start(s32[1,2,3,128]{3,1,2,0:T(2,128)} %param.17) | copy-start | bytes 9220
  0.0 2.3 %copy-start.4 = (f32[2,1,2,3,15]{4,2,3,1,0:T(2,128)S(1)}, f32[2,1,2,3,15]{4,2,3,1,0:T(2,128)}, u32[]{:S(2)}) copy-start(f32[2,1,2,3,15]{4,2,3,1,0:T(2,128)} %param.12) | copy-start | bytes 2164
  0.0 4.6 %collective-permute-start = (bf16[48,768]{1,0:T(8,128)(2,1)}, bf16[48,768]{1,0:T(8,128)(2,1)S(1)}, u32[]{:S(2)}, u32[]{:S(2)}) collective-permute-start(bf16[48,768]{1,0:T(8,128)(2,1)} %bitcast.7), channel_id=1, source_target_pairs={{0,1},{1,0},{2,3},{3,2},{4,5},{5,4},{6,7},{7,6},{8,9},{9,8},{10,11... | collective-permute-start | bytes 221192 | tf_op jit(solution)/shard_map/ppermute | solution.py:349
  4.6 2.0 %copy-start.1 = (s32[816,15]{0,1:T(8,128)S(1)}, s32[816,15]{0,1:T(8,128)}, u32[]{:S(2)}) copy-start(s32[816,15]{0,1:T(8,128)} %param.15) | copy-start | bytes 146884
  4.7 2.0 %copy-start.3 = (s32[3,16,2,3]{1,2,3,0:T(2,128)S(1)}, s32[3,16,2,3]{1,2,3,0:T(2,128)}, u32[]{:S(2)}) copy-start(s32[3,16,2,3]{1,2,3,0:T(2,128)} %param.16) | copy-start | bytes 3460
  4.7 2.0 %copy-start.6 = (f32[16]{0:T(128)S(1)}, f32[16]{0:T(128)}, u32[]{:S(2)}) copy-start(f32[16]{0:T(128)} %param.14) | copy-start | bytes 196
  5.0 4.5 %collective-permute-start.1 = (f32[96,128]{1,0:T(8,128)S(1)}, f32[96,128]{1,0:T(8,128)S(1)}, u32[]{:S(2)}, u32[]{:S(2)}) collective-permute-start(f32[96,128]{1,0:T(8,128)S(1)} %get-tuple-element.32), channel_id=1, source_target_pairs={{0,1},{1,0},{2,4},{3,5},{4,2},{5,3},{6,8},{7,9},{8,6},{9,7},{10,12... | collective-permute-start | bytes 147464 | tf_op jit(solution)/shard_map/ppermute | solution.py:370
  5.1 4.4 %collective-permute-start.2 = (f32[96,128]{1,0:T(8,128)S(1)}, f32[96,128]{1,0:T(8,128)S(1)}, u32[]{:S(2)}, u32[]{:S(2)}) collective-permute-start(f32[96,128]{1,0:T(8,128)S(1)} %get-tuple-element.33), channel_id=1, source_target_pairs={{0,2},{2,0},{4,6},{6,4},{8,10},{10,8},{12,14},{14,12},{16,18},{18,... | collective-permute-start | bytes 147464 | tf_op jit(solution)/shard_map/ppermute | solution.py:371
  9.8 4.5 %collective-permute-start.3 = (f32[104,128]{1,0:T(8,128)S(1)}, f32[104,128]{1,0:T(8,128)S(1)}, u32[]{:S(2)}, u32[]{:S(2)}) collective-permute-start(f32[104,128]{1,0:T(8,128)S(1)} %get-tuple-element.38), channel_id=1, source_target_pairs={{0,1},{1,2},{2,0},{3,5},{4,6},{5,3},{6,4},{7,9},{8,10},{9,7},{10,8... | collective-permute-start | bytes 159752 | tf_op jit(solution)/shard_map/ppermute | solution.py:370
  10.0 2.1 %collective-permute-start.4 = (f32[96,128]{1,0:T(8,128)S(1)}, f32[96,128]{1,0:T(8,128)S(1)}, u32[]{:S(2)}, u32[]{:S(2)}) collective-permute-start(f32[96,128]{1,0:T(8,128)S(1)} %get-tuple-element.40), channel_id=1, source_target_pairs={{0,2},{2,0},{4,6},{6,4},{8,10},{10,8},{12,14},{14,12},{16,18},{18,... | collective-permute-start | bytes 147464 | tf_op jit(solution)/shard_map/ppermute | solution.py:371

commit v8 on v7

--- a/solution.py
+++ b/solution.py
@@ -311,25 +311,56 @@
         project_rows(d, picks, None, basis, None, plane_out, None)
 
 
-def project_near(d, field, near, maps, masks, basis, plane_out, early, out, held, near_out, sems):
-    @pl.when(lax.axis_index("smp") == 1)
+def last_part(even):
+    here = lax.rem(lax.axis_index("sub"), 2) == (0 if even else 1)
+    return jnp.logical_and(lax.axis_index("smp") == 1, here)
+
+
+def plane_copy(d, plane_out, out, sem):
+    return pltpu.make_async_copy(plane_out, out.at[0, :, :, :, slice(0, d.face)], sem)
+
+
+def project_near(d, field, near, maps, masks, basis, plane_out, early, out, near_out, held, sems):
+    def picks():
+        lanes = side_jumps(d, True, field, near, maps, masks, held)
+        return [held[d.block(n), :].astype(BF16) for n in range(d.subs)], lanes
+
+    @pl.when(last_part(True))
     def _():
-        at = slice(0, d.face)
-        first = pltpu.make_async_copy(plane_out, out.at[0, :, :, :, at], sems.at[0])
+        first = plane_copy(d, plane_out, out, sems.at[0])
         first.start()
-        lanes = side_jumps(d, True, field, near, maps, masks, held)
-        picks = [held[d.block(n), :].astype(BF16) for n in range(d.subs)]
-        second = project_rows(d, picks, lanes, basis, out, near_out, sems.at[1])
+        rows, lanes = picks()
+        second = project_rows(d, rows, lanes, basis, out, near_out, sems.at[1])
         first.wait()
         second.wait()
 
-
-def project_late(d, field, far, maps, masks, basis, early, out, held, far_out, sem):
-    @pl.when(lax.axis_index("smp") == 1)
+    @pl.when(last_part(False))
     def _():
+        project_rows(d, picks()[0], None, basis, None, near_out, None)
+
+
+def project_late(
+    d, field, far, maps, masks, basis, plane_out, near_out, early, out, held, far_out, sems
+):
+    def project_far():
         lanes = side_jumps(d, False, field, far, maps, masks, held)
         picks = [held[d.block(n), :].astype(BF16) for n in range(d.subs)]
-        project_rows(d, picks, lanes, basis, out, far_out, sem).wait()
+        return project_rows(d, picks, lanes, basis, out, far_out, sems.at[0])
+
+    @pl.when(last_part(True))
+    def _():
+        project_far().wait()
+
+    @pl.when(last_part(False))
+    def _():
+        at = slice(d.face, 2 * d.face)
+        first = plane_copy(d, plane_out, out, sems.at[1])
+        second = pltpu.make_async_copy(near_out, out.at[0, :, :, :, at], sems.at[2])
+        first.start()
+        second.start()
+        project_far().wait()
+        first.wait()
+        second.wait()
 
 
 def project_share(d, jumps, basis, out, rows_out, sem):
@@ -445,23 +476,23 @@
             out_specs=[HBM, VMEM],
             scratch=[rows_out(d.share), pltpu.SemaphoreType.DMA(())],
         )
-        (early,) = run(
+        early, near_out = run(
             project_near,
-            result,
+            result + [shaped((d.height, d.breadth, d.terms, face), BF16)],
             [VMEM] * 6 + [HBM],
             [field, near, maps, masks, basis, plane_out, early],
-            out_specs=[HBM],
-            scratch=[held, rows_out(face), pltpu.SemaphoreType.DMA((2,))],
+            out_specs=[HBM, VMEM],
+            scratch=[held, pltpu.SemaphoreType.DMA((2,))],
             aliases={6: 0},
         )
         (out,) = run(
             project_late,
             result,
-            [VMEM] * 5 + [HBM],
-            [field, far, maps, masks, basis, early],
+            [VMEM] * 7 + [HBM],
+            [field, far, maps, masks, basis, plane_out, near_out, early],
             out_specs=[HBM],
-            scratch=[held, rows_out(face), pltpu.SemaphoreType.DMA(())],
-            aliases={5: 0},
+            scratch=[held, rows_out(face), pltpu.SemaphoreType.DMA((3,))],
+            aliases={7: 0},
         )
     else:
         last = [field, far, near, maps, masks, plane]

time: 15.8 us -> 15.7 us (level)
  no operation moved by 1% of the time
where the time goes in v8:
time: 15.7 us; the launch traced here: 15.6 us
  Pallas kernels  7.65 us (49%)
  waiting for transfers between devices  4.18 us (27%)
  starting transfers between devices  3.6 us (23%)
    pallas_call x10, Pallas kernels, call(): pl.pallas_call(body, out_shape=outs, in_specs=specs, out_specs=[VMEM] * l...  7.65 us
    ppermute x2, starting transfers between devices, exchange(): return (lax.ppermute(on_chip, 'sub', pairs), far)  2.77 us
    ppermute x2, waiting for transfers between devices, exchange(): far = lax.ppermute(off_chip, ('sub', 'smp'), across)  2.46 us
    ppermute x1, waiting for transfers between devices, per_device(): lax.ppermute(own, 'smp', [(i, (i + shift) % parts) for i in range(parts)])  1.71 us
    ppermute x1, starting transfers between devices, per_device(): lax.ppermute(own, 'smp', [(i, (i + shift) % parts) for i in range(parts)])  0.6 us
  transfers between devices with their start and end apart: 5, of which 3 were waited for; matrix products, arithmetic and copies ran while one was open for 0% of the time, Pallas kernels for 37%

profile of v8, /device:TPU:10, one launch (start us, length us, event | category | flops | bytes accessed | tf_op | source)
XLA Modules:
  0.0 15.6 jit_solution(12646893407358321382)
XLA Ops:
  0.0 0.0 copy-start
  0.0 0.0 copy-start.2
  0.0 0.0 copy-start.5
  0.0 0.0 copy-start.4
  0.0 0.6 %collective-permute-start = (bf16[48,768]{1,0:T(8,128)(2,1)}, bf16[48,768]{1,0:T(8,128)(2,1)S(1)}, u32[]{:S(2)}, u32[]{:S(2)}) collective-permute-start(bf16[48,768]{1,0:T(8,128)(2,1)} %bitcast.7), channel_id=1, source_target_pairs={{0,1},{1,0},{2,3},{3,2},{4,5},{5,4},{6,7},{7,6},{8,9},{9,8},{10,11... | collective-permute-start | bytes 221192 | tf_op jit(solution)/shard_map/ppermute | solution.py:380
  0.6 1.6 %shard_map.91 = (bf16[768,768]{1,0:T(8,128)(2,1)S(1)}, bf16[768,768]{1,0:T(8,128)(2,1)S(1)}) custom-call(bf16[768,768]{1,0:T(8,128)(2,1)} %lam.1, bf16[768,768]{1,0:T(8,128)(2,1)} %mu.1), custom_call_target="tpu_custom_call" | custom-call | tf_op jit(solution)/shard_map/pallas_call | solution.py:23
  2.3 0.0 copy-done
  2.3 0.0 copy-done.2
  2.3 0.0 copy-done.5
  2.3 0.0 copy-done.4
  2.3 0.6 %shard_map.92 = (f32[2,96,128]{2,1,0:T(8,128)S(1)}, s32[2,6,8,128]{3,2,1,0:T(8,128)S(1)}, f32[48,768]{1,0:T(8,128)S(1)}, f32[48,768]{1,0:T(8,128)S(1)}) custom-call(bf16[48,768]{1,0:T(8,128)(2,1)S(1)} %bitcast.8, bf16[768,768]{1,0:T(8,128)(2,1)S(1)} %get-tuple-element.27.lam.refs_1_, bf16[768,768]{1,0:T(8,128)(2,1)S(1)} %get-tuple-element.28.mu.refs_2_, ...), custom_call_target="tpu_custom_call" | custom-call | tf_op jit(solution)/shard_map/pallas_call | solution.py:23
  2.9 1.7 %collective-permute-done.refs_0_ = bf16[48,768]{1,0:T(8,128)(2,1)S(1)} collective-permute-done((bf16[48,768]{1,0:T(8,128)(2,1)}, bf16[48,768]{1,0:T(8,128)(2,1)S(1)}, u32[]{:S(2)}, u32[]{:S(2)}) %collective-permute-start) | collective-permute-done | bytes 73760 | tf_op jit(solution)/shard_map/ppermute | solution.py:380
  4.6 0.0 copy-start.1
  4.7 0.3 %shard_map.93 = (f32[96,256]{1,0:T(8,128)S(1)}, f32[96,128]{1,0:T(8,128)S(1)}, f32[96,128]{1,0:T(8,128)S(1)}) custom-call(bf16[48,768]{1,0:T(8,128)(2,1)S(1)} %collective-permute-done.refs_0_, bf16[768,768]{1,0:T(8,128)(2,1)S(1)} %get-tuple-element.27.lam.refs_1_, bf16[768,768]{1,0:T(8,128)(2,1)S(1)} %get-tuple-element.28.mu.refs_2_, ...), custom_call_target="tpu_custom_call" | custom-call | tf_op jit(solution)/shard_map/pallas_call | solution.py:23
  5.0 0.1 collective-permute-start.1
  5.1 1.6 %collective-permute-start.2 = (f32[96,128]{1,0:T(8,128)S(1)}, f32[96,128]{1,0:T(8,128)S(1)}, u32[]{:S(2)}, u32[]{:S(2)}) collective-permute-start(f32[96,128]{1,0:T(8,128)S(1)} %get-tuple-element.35), channel_id=1, source_target_pairs={{0,2},{2,0},{4,6},{6,4},{8,10},{10,8},{12,14},{14,12},{16,18},{18,... | collective-permute-start | bytes 147464 | tf_op jit(solution)/shard_map/ppermute | solution.py:402
  6.7 0.0 copy-done.1
  6.7 0.0 copy-done.3
  6.7 0.0 copy-done.6
  6.7 0.5 %shard_map.94 = (bf16[816,16]{1,0:T(8,128)(2,1)S(1)}, f32[6,6,8,128]{3,2,1,0:T(8,128)S(1)}) custom-call(f32[16,15]{1,0:T(8,128)S(1)} %copy-done.2, f32[1,16]{1,0:T(1,128)S(1)} %bitcast.13, s32[15,816]{1,0:T(8,128)S(1)} %bitcast.9, s32[3,3,2,16]{3,2,1,0:T(2,128)S(1)} %bitcast.10), custom_call_target="tpu_custom_call" | custom-call | tf_op jit(solution)/shard_map/pallas_call | solution.py:23
  7.2 0.6 %shard_map.95 = (bf16[96,512]{1,0:T(8,128)(2,1)S(1)}, f32[96,256]{1,0:T(8,128)S(1)}, f32[96,256]{1,0:T(8,128)S(1)}) custom-call(bf16[48,768]{1,0:T(8,128)(2,1)S(1)} %collective-permute-done.refs_0_, bf16[768,768]{1,0:T(8,128)(2,1)S(1)} %get-tuple-element.27.lam.refs_1_, bf16[768,768]{1,0:T(8,128)(2,1)S(1)} %get-tuple-element.28.mu.refs_2_, ...), custom_call_target="tpu_custom_call" | custom-call | tf_op jit(solution)/shard_map/pallas_call | solution.py:23
  7.8 1.7 %collective-permute-done.1.from_off = f32[96,128]{1,0:T(8,128)S(1)} collective-permute-done((f32[96,128]{1,0:T(8,128)S(1)}, f32[96,128]{1,0:T(8,128)S(1)}, u32[]{:S(2)}, u32[]{:S(2)}) %collective-permute-start.1) | collective-permute-done | bytes 49184 | tf_op jit(solution)/shard_map/ppermute | solution.py:401
  9.5 0.0 collective-permute-done.2.from_chip
  9.5 0.3 %shard_map.96 = (bf16[96,256]{1,0:T(8,128)(2,1)S(1)}, f32[96,256]{1,0:T(8,128)S(1)}, f32[96,128]{1,0:T(8,128)S(1)}, f32[104,128]{1,0:T(8,128)S(1)}) custom-call(f32[96,256]{1,0:T(8,128)S(1)} %get-tuple-element.33.field, f32[96,128]{1,0:T(8,128)S(1)} %collective-permute-done.1.from_off, f32[96,128]{1,0:T(8,128)S(1)} %collective-permute-done.2.from_chip, ...), custom_call_target="tpu_custom_call" | custom-call | tf_op jit(solution)/shard_map/pallas_call | solution.py:23
  9.8 0.2 %collective-permute-start.3 = (f32[104,128]{1,0:T(8,128)S(1)}, f32[104,128]{1,0:T(8,128)S(1)}, u32[]{:S(2)}, u32[]{:S(2)}) collective-permute-start(f32[104,128]{1,0:T(8,128)S(1)} %get-tuple-element.40), channel_id=1, source_target_pairs={{0,1},{1,2},{2,0},{3,5},{4,6},{5,3},{6,4},{7,9},{8,10},{9,7},{10,8... | collective-permute-start | bytes 159752 | tf_op jit(solution)/shard_map/ppermute | solution.py:401
  10.0 1.1 %collective-permute-start.4 = (f32[96,128]{1,0:T(8,128)S(1)}, f32[96,128]{1,0:T(8,128)S(1)}, u32[]{:S(2)}, u32[]{:S(2)}) collective-permute-start(f32[96,128]{1,0:T(8,128)S(1)} %get-tuple-element.45), channel_id=1, source_target_pairs={{0,2},{2,0},{4,6},{6,4},{8,10},{10,8},{12,14},{14,12},{16,18},{18,... | collective-permute-start | bytes 147464 | tf_op jit(solution)/shard_map/ppermute | solution.py:402
  11.1 0.4 %shard_map.97.plane = bf16[96,512]{1,0:T(8,128)(2,1)S(1)} custom-call(bf16[96,512]{1,0:T(8,128)(2,1)S(1)} %get-tuple-element.42.plane, bf16[96,256]{1,0:T(8,128)(2,1)S(1)} %get-tuple-element.43.zed, bf16[768,768]{1,0:T(8,128)(2,1)S(1)} %get-tuple-element.27.lam.refs_1_, bf16[768,768]{1,0:T(8,128)(2,1)S(1)} %get-tuple-element.28.mu.refs_2_, ...), custom_call_target="tpu_custom_call" | custom-call | tf_op jit(solution)/shard_map/pallas_call | solution.py:23
  11.5 0.5 %shard_map.98 = (bf16[1,2,3,816,384]{4,3,2,1,0:T(8,128)(2,1)}, bf16[2,3,816,128]{3,2,1,0:T(8,128)(2,1)S(1)}) custom-call(bf16[96,512]{1,0:T(8,128)(2,1)S(1)} %shard_map.97.plane, bf16[816,16]{1,0:T(8,128)(2,1)S(1)} %get-tuple-element.41.basis), custom_call_target="tpu_custom_call" | custom-call | tf_op jit(solution)/shard_map/pallas_call | solution.py:23
  12.0 0.0 collective-permute-done.4.near
  12.0 1.5 %shard_map.99 = (bf16[1,2,3,816,384]{4,3,2,1,0:T(8,128)(2,1)}, bf16[2,3,816,128]{3,2,1,0:T(8,128)(2,1)S(1)}) custom-call(f32[96,256]{1,0:T(8,128)S(1)} %get-tuple-element.39.field, f32[96,128]{1,0:T(8,128)S(1)} %collective-permute-done.4.near, s32[2,6,8,128]{3,2,1,0:T(8,128)S(1)} %get-tuple-element.30.refs_4_.maps, ...), custom_call_target="tpu_custom_call", output_to_operand_aliasing={{0}: (6, {})} | custom-call | tf_op jit(solution)/shard_map/pallas_call | solution.py:23
  13.5 0.8 %collective-permute-done.3.far = f32[104,128]{1,0:T(8,128)S(1)} collective-permute-done((f32[104,128]{1,0:T(8,128)S(1)}, f32[104,128]{1,0:T(8,128)S(1)}, u32[]{:S(2)}, u32[]{:S(2)}) %collective-permute-start.3) | collective-permute-done | bytes 53280 | tf_op jit(solution)/shard_map/ppermute | solution.py:401
  14.3 1.3 %shard_map.100 = bf16[1,2,3,816,384]{4,3,2,1,0:T(8,128)(2,1)} custom-call(f32[96,256]{1,0:T(8,128)S(1)} %get-tuple-element.39.field, f32[104,128]{1,0:T(8,128)S(1)} %collective-permute-done.3.far, s32[2,6,8,128]{3,2,1,0:T(8,128)S(1)} %get-tuple-element.30.refs_4_.maps, ...), custom_call_target="tpu_custom_call", output_to_operand_aliasing={{}: (7, {})} | custom-call | tf_op jit(solution)/shard_map/pallas_call | solution.py:23
  (2 shorter events, 0.0 us)
Async XLA Ops:
  0.0 2.3 %copy-start = (bf16[1,2,3,8,768]{4,3,2,1,0:T(8,128)(2,1)S(1)}, bf16[1,2,3,8,768]{4,3,2,1,0:T(8,128)(2,1)}, u32[]{:S(2)}) copy-start(bf16[1,2,3,8,768]{4,3,2,1,0:T(8,128)(2,1)} %param.9) | copy-start | bytes 221188
  0.0 2.3 %copy-start.2 = (f32[16,15]{1,0:T(8,128)S(1)}, f32[16,15]{1,0:T(8,128)}, u32[]{:S(2)}) copy-start(f32[16,15]{1,0:T(8,128)} %nodes.3) | copy-start | bytes 2884
  0.0 2.3 %copy-start.5 = (s32[1,2,3,128]{3,1,2,0:T(2,128)S(1)}, s32[1,2,3,128]{3,1,2,0:T(2,128)}, u32[]{:S(2)}) copy-start(s32[1,2,3,128]{3,1,2,0:T(2,128)} %param.17) | copy-start | bytes 9220
  0.0 2.3 %copy-start.4 = (f32[2,1,2,3,15]{4,2,3,1,0:T(2,128)S(1)}, f32[2,1,2,3,15]{4,2,3,1,0:T(2,128)}, u32[]{:S(2)}) copy-start(f32[2,1,2,3,15]{4,2,3,1,0:T(2,128)} %param.12) | copy-start | bytes 2164
  0.0 4.6 %collective-permute-start = (bf16[48,768]{1,0:T(8,128)(2,1)}, bf16[48,768]{1,0:T(8,128)(2,1)S(1)}, u32[]{:S(2)}, u32[]{:S(2)}) collective-permute-start(bf16[48,768]{1,0:T(8,128)(2,1)} %bitcast.7), channel_id=1, source_target_pairs={{0,1},{1,0},{2,3},{3,2},{4,5},{5,4},{6,7},{7,6},{8,9},{9,8},{10,11... | collective-permute-start | bytes 221192 | tf_op jit(solution)/shard_map/ppermute | solution.py:380
  4.6 2.0 %copy-start.1 = (s32[816,15]{0,1:T(8,128)S(1)}, s32[816,15]{0,1:T(8,128)}, u32[]{:S(2)}) copy-start(s32[816,15]{0,1:T(8,128)} %param.15) | copy-start | bytes 146884
  4.7 2.0 %copy-start.3 = (s32[3,16,2,3]{1,2,3,0:T(2,128)S(1)}, s32[3,16,2,3]{1,2,3,0:T(2,128)}, u32[]{:S(2)}) copy-start(s32[3,16,2,3]{1,2,3,0:T(2,128)} %param.16) | copy-start | bytes 3460
  4.7 2.0 %copy-start.6 = (f32[16]{0:T(128)S(1)}, f32[16]{0:T(128)}, u32[]{:S(2)}) copy-start(f32[16]{0:T(128)} %param.14) | copy-start | bytes 196
  5.0 4.5 %collective-permute-start.1 = (f32[96,128]{1,0:T(8,128)S(1)}, f32[96,128]{1,0:T(8,128)S(1)}, u32[]{:S(2)}, u32[]{:S(2)}) collective-permute-start(f32[96,128]{1,0:T(8,128)S(1)} %get-tuple-element.34), channel_id=1, source_target_pairs={{0,1},{1,0},{2,4},{3,5},{4,2},{5,3},{6,8},{7,9},{8,6},{9,7},{10,12... | collective-permute-start | bytes 147464 | tf_op jit(solution)/shard_map/ppermute | solution.py:401
  5.1 4.4 %collective-permute-start.2 = (f32[96,128]{1,0:T(8,128)S(1)}, f32[96,128]{1,0:T(8,128)S(1)}, u32[]{:S(2)}, u32[]{:S(2)}) collective-permute-start(f32[96,128]{1,0:T(8,128)S(1)} %get-tuple-element.35), channel_id=1, source_target_pairs={{0,2},{2,0},{4,6},{6,4},{8,10},{10,8},{12,14},{14,12},{16,18},{18,... | collective-permute-start | bytes 147464 | tf_op jit(solution)/shard_map/ppermute | solution.py:402
  9.8 4.5 %collective-permute-start.3 = (f32[104,128]{1,0:T(8,128)S(1)}, f32[104,128]{1,0:T(8,128)S(1)}, u32[]{:S(2)}, u32[]{:S(2)}) collective-permute-start(f32[104,128]{1,0:T(8,128)S(1)} %get-tuple-element.40), channel_id=1, source_target_pairs={{0,1},{1,2},{2,0},{3,5},{4,6},{5,3},{6,4},{7,9},{8,10},{9,7},{10,8... | collective-permute-start | bytes 159752 | tf_op jit(solution)/shard_map/ppermute | solution.py:401
  10.0 2.1 %collective-permute-start.4 = (f32[96,128]{1,0:T(8,128)S(1)}, f32[96,128]{1,0:T(8,128)S(1)}, u32[]{:S(2)}, u32[]{:S(2)}) collective-permute-start(f32[96,128]{1,0:T(8,128)S(1)} %get-tuple-element.45), channel_id=1, source_target_pairs={{0,2},{2,0},{4,6},{6,4},{8,10},{10,8},{12,14},{14,12},{16,18},{18,... | collective-permute-start | bytes 147464 | tf_op jit(solution)/shard_map/ppermute | solution.py:402

commit v9 on v8

--- a/solution.py
+++ b/solution.py
@@ -165,11 +165,28 @@
     others = refs[: d.parts - 1]
     lam, mu, mod, maps, own_lam, own_mu, field, on_chip, off_chip = refs[d.parts - 1 :]
     at = slice(d.plane, d.width)
-    combine(d, mod, lax.axis_index("smp"), own_lam.at[:, at], own_mu.at[:, at], field)
+    even = lax.rem(lax.axis_index("sub"), 2) == 0
+
+    def finish(part, first, second):
+        for n in range(d.subs):
+            for start in range(0, d.here, 8):
+                group = slice(n * d.here + start, n * d.here + start + 8)
+                place = n * d.samples + part * d.here + start
+                rows = pl.ds(pl.multiple_of(place, 8), 8)
+                value = (
+                    wide(mod[0, rows, :], 2 * d.face) * first[group, :]
+                    + wide(mod[1, rows, :], 2 * d.face) * second[group, :]
+                )
+                field[rows, :] = value
+                minus, high = value[:, : d.face], value[:, d.face :]
+                pushed = jnp.take_along_axis(high, maps[1, n], axis=1, mode="promise_in_bounds")
+                on_chip[rows, :] = jnp.where(even, pushed, minus)
+                off_chip[rows, :] = jnp.where(even, minus, pushed)
+
+    finish(lax.axis_index("smp"), own_lam[:, at], own_mu[:, at])
     for shift, other in enumerate(others, 1):
         rows = other[...]
-        combine(d, mod, part_of(d, shift), dot(rows, lam[:, at]), dot(rows, mu[:, at]), field)
-    payloads(d, field[:, : d.face], field[:, d.face :], maps, on_chip, off_chip)
+        finish(part_of(d, shift), dot(rows, lam[:, at]), dot(rows, mu[:, at]))
 
 
 def plane_jumps(d, field, masks, out):

time: 15.7 us -> 15.7 us (level)
  no operation moved by 1% of the time
where the time goes in v9:
time: 15.7 us; the launch traced here: 15.5 us
  Pallas kernels  7.65 us (49%)
  waiting for transfers between devices  4.17 us (27%)
  starting transfers between devices  3.58 us (23%)
    pallas_call x10, Pallas kernels, call(): pl.pallas_call(body, out_shape=outs, in_specs=specs, out_specs=[VMEM] * l...  7.65 us
    ppermute x2, starting transfers between devices, exchange(): return (lax.ppermute(on_chip, 'sub', pairs), far)  2.77 us
    ppermute x2, waiting for transfers between devices, exchange(): far = lax.ppermute(off_chip, ('sub', 'smp'), across)  2.45 us
    ppermute x1, waiting for transfers between devices, per_device(): lax.ppermute(own, 'smp', [(i, (i + shift) % parts) for i in range(parts)])  1.71 us
    ppermute x1, starting transfers between devices, per_device(): lax.ppermute(own, 'smp', [(i, (i + shift) % parts) for i in range(parts)])  0.6 us
  transfers between devices with their start and end apart: 5, of which 3 were waited for; matrix products, arithmetic and copies ran while one was open for 0% of the time, Pallas kernels for 37%

profile of v9, /device:TPU:10, one launch (start us, length us, event | category | flops | bytes accessed | tf_op | source)
XLA Modules:
  0.0 15.5 jit_solution(9629733305138442944)
XLA Ops:
  0.0 0.0 copy-start
  0.0 0.0 copy-start.2
  0.0 0.0 copy-start.5
  0.0 0.0 copy-start.4
  0.0 0.6 %collective-permute-start = (bf16[48,768]{1,0:T(8,128)(2,1)}, bf16[48,768]{1,0:T(8,128)(2,1)S(1)}, u32[]{:S(2)}, u32[]{:S(2)}) collective-permute-start(bf16[48,768]{1,0:T(8,128)(2,1)} %bitcast.7), channel_id=1, source_target_pairs={{0,1},{1,0},{2,3},{3,2},{4,5},{5,4},{6,7},{7,6},{8,9},{9,8},{10,11... | collective-permute-start | bytes 221192 | tf_op jit(solution)/shard_map/ppermute | solution.py:397
  0.6 1.6 %shard_map.91 = (bf16[768,768]{1,0:T(8,128)(2,1)S(1)}, bf16[768,768]{1,0:T(8,128)(2,1)S(1)}) custom-call(bf16[768,768]{1,0:T(8,128)(2,1)} %lam.1, bf16[768,768]{1,0:T(8,128)(2,1)} %mu.1), custom_call_target="tpu_custom_call" | custom-call | tf_op jit(solution)/shard_map/pallas_call | solution.py:23
  2.3 0.0 copy-done
  2.3 0.0 copy-done.2
  2.3 0.0 copy-done.5
  2.3 0.0 copy-done.4
  2.3 0.6 %shard_map.92 = (f32[2,96,128]{2,1,0:T(8,128)S(1)}, s32[2,6,8,128]{3,2,1,0:T(8,128)S(1)}, f32[48,768]{1,0:T(8,128)S(1)}, f32[48,768]{1,0:T(8,128)S(1)}) custom-call(bf16[48,768]{1,0:T(8,128)(2,1)S(1)} %bitcast.8, bf16[768,768]{1,0:T(8,128)(2,1)S(1)} %get-tuple-element.27.lam.refs_1_, bf16[768,768]{1,0:T(8,128)(2,1)S(1)} %get-tuple-element.28.mu.refs_2_, ...), custom_call_target="tpu_custom_call" | custom-call | tf_op jit(solution)/shard_map/pallas_call | solution.py:23
  2.9 1.7 %collective-permute-done.refs_0_ = bf16[48,768]{1,0:T(8,128)(2,1)S(1)} collective-permute-done((bf16[48,768]{1,0:T(8,128)(2,1)}, bf16[48,768]{1,0:T(8,128)(2,1)S(1)}, u32[]{:S(2)}, u32[]{:S(2)}) %collective-permute-start) | collective-permute-done | bytes 73760 | tf_op jit(solution)/shard_map/ppermute | solution.py:397
  4.6 0.0 copy-start.1
  4.7 0.3 %shard_map.93 = (f32[96,256]{1,0:T(8,128)S(1)}, f32[96,128]{1,0:T(8,128)S(1)}, f32[96,128]{1,0:T(8,128)S(1)}) custom-call(bf16[48,768]{1,0:T(8,128)(2,1)S(1)} %collective-permute-done.refs_0_, bf16[768,768]{1,0:T(8,128)(2,1)S(1)} %get-tuple-element.27.lam.refs_1_, bf16[768,768]{1,0:T(8,128)(2,1)S(1)} %get-tuple-element.28.mu.refs_2_, ...), custom_call_target="tpu_custom_call" | custom-call | tf_op jit(solution)/shard_map/pallas_call | solution.py:23
  5.0 0.0 collective-permute-start.1
  5.0 1.6 %collective-permute-start.2 = (f32[96,128]{1,0:T(8,128)S(1)}, f32[96,128]{1,0:T(8,128)S(1)}, u32[]{:S(2)}, u32[]{:S(2)}) collective-permute-start(f32[96,128]{1,0:T(8,128)S(1)} %get-tuple-element.35), channel_id=1, source_target_pairs={{0,2},{2,0},{4,6},{6,4},{8,10},{10,8},{12,14},{14,12},{16,18},{18,... | collective-permute-start | bytes 147464 | tf_op jit(solution)/shard_map/ppermute | solution.py:419
  6.6 0.0 copy-done.1
  6.6 0.0 copy-done.3
  6.7 0.0 copy-done.6
  6.7 0.5 %shard_map.94 = (bf16[816,16]{1,0:T(8,128)(2,1)S(1)}, f32[6,6,8,128]{3,2,1,0:T(8,128)S(1)}) custom-call(f32[16,15]{1,0:T(8,128)S(1)} %copy-done.2, f32[1,16]{1,0:T(1,128)S(1)} %bitcast.13, s32[15,816]{1,0:T(8,128)S(1)} %bitcast.9, s32[3,3,2,16]{3,2,1,0:T(2,128)S(1)} %bitcast.10), custom_call_target="tpu_custom_call" | custom-call | tf_op jit(solution)/shard_map/pallas_call | solution.py:23
  7.2 0.6 %shard_map.95 = (bf16[96,512]{1,0:T(8,128)(2,1)S(1)}, f32[96,256]{1,0:T(8,128)S(1)}, f32[96,256]{1,0:T(8,128)S(1)}) custom-call(bf16[48,768]{1,0:T(8,128)(2,1)S(1)} %collective-permute-done.refs_0_, bf16[768,768]{1,0:T(8,128)(2,1)S(1)} %get-tuple-element.27.lam.refs_1_, bf16[768,768]{1,0:T(8,128)(2,1)S(1)} %get-tuple-element.28.mu.refs_2_, ...), custom_call_target="tpu_custom_call" | custom-call | tf_op jit(solution)/shard_map/pallas_call | solution.py:23
  7.8 1.7 %collective-permute-done.1.from_off = f32[96,128]{1,0:T(8,128)S(1)} collective-permute-done((f32[96,128]{1,0:T(8,128)S(1)}, f32[96,128]{1,0:T(8,128)S(1)}, u32[]{:S(2)}, u32[]{:S(2)}) %collective-permute-start.1) | collective-permute-done | bytes 49184 | tf_op jit(solution)/shard_map/ppermute | solution.py:418
  9.4 0.0 collective-permute-done.2.from_chip
  9.4 0.3 %shard_map.96 = (bf16[96,256]{1,0:T(8,128)(2,1)S(1)}, f32[96,256]{1,0:T(8,128)S(1)}, f32[96,128]{1,0:T(8,128)S(1)}, f32[104,128]{1,0:T(8,128)S(1)}) custom-call(f32[96,256]{1,0:T(8,128)S(1)} %get-tuple-element.33.field, f32[96,128]{1,0:T(8,128)S(1)} %collective-permute-done.1.from_off, f32[96,128]{1,0:T(8,128)S(1)} %collective-permute-done.2.from_chip, ...), custom_call_target="tpu_custom_call" | custom-call | tf_op jit(solution)/shard_map/pallas_call | solution.py:23
  9.7 0.2 %collective-permute-start.3 = (f32[104,128]{1,0:T(8,128)S(1)}, f32[104,128]{1,0:T(8,128)S(1)}, u32[]{:S(2)}, u32[]{:S(2)}) collective-permute-start(f32[104,128]{1,0:T(8,128)S(1)} %get-tuple-element.40), channel_id=1, source_target_pairs={{0,1},{1,2},{2,0},{3,5},{4,6},{5,3},{6,4},{7,9},{8,10},{9,7},{10,8... | collective-permute-start | bytes 159752 | tf_op jit(solution)/shard_map/ppermute | solution.py:418
  9.9 1.1 %collective-permute-start.4 = (f32[96,128]{1,0:T(8,128)S(1)}, f32[96,128]{1,0:T(8,128)S(1)}, u32[]{:S(2)}, u32[]{:S(2)}) collective-permute-start(f32[96,128]{1,0:T(8,128)S(1)} %get-tuple-element.45), channel_id=1, source_target_pairs={{0,2},{2,0},{4,6},{6,4},{8,10},{10,8},{12,14},{14,12},{16,18},{18,... | collective-permute-start | bytes 147464 | tf_op jit(solution)/shard_map/ppermute | solution.py:419
  11.1 0.4 %shard_map.97.plane = bf16[96,512]{1,0:T(8,128)(2,1)S(1)} custom-call(bf16[96,512]{1,0:T(8,128)(2,1)S(1)} %get-tuple-element.42.plane, bf16[96,256]{1,0:T(8,128)(2,1)S(1)} %get-tuple-element.43.zed, bf16[768,768]{1,0:T(8,128)(2,1)S(1)} %get-tuple-element.27.lam.refs_1_, bf16[768,768]{1,0:T(8,128)(2,1)S(1)} %get-tuple-element.28.mu.refs_2_, ...), custom_call_target="tpu_custom_call" | custom-call | tf_op jit(solution)/shard_map/pallas_call | solution.py:23
  11.5 0.5 %shard_map.98 = (bf16[1,2,3,816,384]{4,3,2,1,0:T(8,128)(2,1)}, bf16[2,3,816,128]{3,2,1,0:T(8,128)(2,1)S(1)}) custom-call(bf16[96,512]{1,0:T(8,128)(2,1)S(1)} %shard_map.97.plane, bf16[816,16]{1,0:T(8,128)(2,1)S(1)} %get-tuple-element.41.basis), custom_call_target="tpu_custom_call" | custom-call | tf_op jit(solution)/shard_map/pallas_call | solution.py:23
  12.0 0.0 collective-permute-done.4.near
  12.0 1.5 %shard_map.99 = (bf16[1,2,3,816,384]{4,3,2,1,0:T(8,128)(2,1)}, bf16[2,3,816,128]{3,2,1,0:T(8,128)(2,1)S(1)}) custom-call(f32[96,256]{1,0:T(8,128)S(1)} %get-tuple-element.39.field, f32[96,128]{1,0:T(8,128)S(1)} %collective-permute-done.4.near, s32[2,6,8,128]{3,2,1,0:T(8,128)S(1)} %get-tuple-element.30.refs_4_.maps, ...), custom_call_target="tpu_custom_call", output_to_operand_aliasing={{0}: (6, {})} | custom-call | tf_op jit(solution)/shard_map/pallas_call | solution.py:23
  13.5 0.8 %collective-permute-done.3.far = f32[104,128]{1,0:T(8,128)S(1)} collective-permute-done((f32[104,128]{1,0:T(8,128)S(1)}, f32[104,128]{1,0:T(8,128)S(1)}, u32[]{:S(2)}, u32[]{:S(2)}) %collective-permute-start.3) | collective-permute-done | bytes 53280 | tf_op jit(solution)/shard_map/ppermute | solution.py:418
  14.3 1.3 %shard_map.100 = bf16[1,2,3,816,384]{4,3,2,1,0:T(8,128)(2,1)} custom-call(f32[96,256]{1,0:T(8,128)S(1)} %get-tuple-element.39.field, f32[104,128]{1,0:T(8,128)S(1)} %collective-permute-done.3.far, s32[2,6,8,128]{3,2,1,0:T(8,128)S(1)} %get-tuple-element.30.refs_4_.maps, ...), custom_call_target="tpu_custom_call", output_to_operand_aliasing={{}: (7, {})} | custom-call | tf_op jit(solution)/shard_map/pallas_call | solution.py:23
  (2 shorter events, 0.0 us)
Async XLA Ops:
  0.0 2.3 %copy-start = (bf16[1,2,3,8,768]{4,3,2,1,0:T(8,128)(2,1)S(1)}, bf16[1,2,3,8,768]{4,3,2,1,0:T(8,128)(2,1)}, u32[]{:S(2)}) copy-start(bf16[1,2,3,8,768]{4,3,2,1,0:T(8,128)(2,1)} %param.9) | copy-start | bytes 221188
  0.0 2.3 %copy-start.2 = (f32[16,15]{1,0:T(8,128)S(1)}, f32[16,15]{1,0:T(8,128)}, u32[]{:S(2)}) copy-start(f32[16,15]{1,0:T(8,128)} %nodes.3) | copy-start | bytes 2884
  0.0 2.3 %copy-start.5 = (s32[1,2,3,128]{3,1,2,0:T(2,128)S(1)}, s32[1,2,3,128]{3,1,2,0:T(2,128)}, u32[]{:S(2)}) copy-start(s32[1,2,3,128]{3,1,2,0:T(2,128)} %param.17) | copy-start | bytes 9220
  0.0 2.3 %copy-start.4 = (f32[2,1,2,3,15]{4,2,3,1,0:T(2,128)S(1)}, f32[2,1,2,3,15]{4,2,3,1,0:T(2,128)}, u32[]{:S(2)}) copy-start(f32[2,1,2,3,15]{4,2,3,1,0:T(2,128)} %param.12) | copy-start | bytes 2164
  0.0 4.6 %collective-permute-start = (bf16[48,768]{1,0:T(8,128)(2,1)}, bf16[48,768]{1,0:T(8,128)(2,1)S(1)}, u32[]{:S(2)}, u32[]{:S(2)}) collective-permute-start(bf16[48,768]{1,0:T(8,128)(2,1)} %bitcast.7), channel_id=1, source_target_pairs={{0,1},{1,0},{2,3},{3,2},{4,5},{5,4},{6,7},{7,6},{8,9},{9,8},{10,11... | collective-permute-start | bytes 221192 | tf_op jit(solution)/shard_map/ppermute | solution.py:397
  4.6 2.0 %copy-start.1 = (s32[816,15]{0,1:T(8,128)S(1)}, s32[816,15]{0,1:T(8,128)}, u32[]{:S(2)}) copy-start(s32[816,15]{0,1:T(8,128)} %param.15) | copy-start | bytes 146884
  4.7 2.0 %copy-start.3 = (s32[3,16,2,3]{1,2,3,0:T(2,128)S(1)}, s32[3,16,2,3]{1,2,3,0:T(2,128)}, u32[]{:S(2)}) copy-start(s32[3,16,2,3]{1,2,3,0:T(2,128)} %param.16) | copy-start | bytes 3460
  4.7 2.0 %copy-start.6 = (f32[16]{0:T(128)S(1)}, f32[16]{0:T(128)}, u32[]{:S(2)}) copy-start(f32[16]{0:T(128)} %param.14) | copy-start | bytes 196
  5.0 4.5 %collective-permute-start.1 = (f32[96,128]{1,0:T(8,128)S(1)}, f32[96,128]{1,0:T(8,128)S(1)}, u32[]{:S(2)}, u32[]{:S(2)}) collective-permute-start(f32[96,128]{1,0:T(8,128)S(1)} %get-tuple-element.34), channel_id=1, source_target_pairs={{0,1},{1,0},{2,4},{3,5},{4,2},{5,3},{6,8},{7,9},{8,6},{9,7},{10,12... | collective-permute-start | bytes 147464 | tf_op jit(solution)/shard_map/ppermute | solution.py:418
  5.0 4.4 %collective-permute-start.2 = (f32[96,128]{1,0:T(8,128)S(1)}, f32[96,128]{1,0:T(8,128)S(1)}, u32[]{:S(2)}, u32[]{:S(2)}) collective-permute-start(f32[96,128]{1,0:T(8,128)S(1)} %get-tuple-element.35), channel_id=1, source_target_pairs={{0,2},{2,0},{4,6},{6,4},{8,10},{10,8},{12,14},{14,12},{16,18},{18,... | collective-permute-start | bytes 147464 | tf_op jit(solution)/shard_map/ppermute | solution.py:419
  9.7 4.5 %collective-permute-start.3 = (f32[104,128]{1,0:T(8,128)S(1)}, f32[104,128]{1,0:T(8,128)S(1)}, u32[]{:S(2)}, u32[]{:S(2)}) collective-permute-start(f32[104,128]{1,0:T(8,128)S(1)} %get-tuple-element.40), channel_id=1, source_target_pairs={{0,1},{1,2},{2,0},{3,5},{4,6},{5,3},{6,4},{7,9},{8,10},{9,7},{10,8... | collective-permute-start | bytes 159752 | tf_op jit(solution)/shard_map/ppermute | solution.py:418
  9.9 2.1 %collective-permute-start.4 = (f32[96,128]{1,0:T(8,128)S(1)}, f32[96,128]{1,0:T(8,128)S(1)}, u32[]{:S(2)}, u32[]{:S(2)}) collective-permute-start(f32[96,128]{1,0:T(8,128)S(1)} %get-tuple-element.45), channel_id=1, source_target_pairs={{0,2},{2,0},{4,6},{6,4},{8,10},{10,8},{12,14},{14,12},{16,18},{18,... | collective-permute-start | bytes 147464 | tf_op jit(solution)/shard_map/ppermute | solution.py:419

commit v10 on v9

--- a/solution.py
+++ b/solution.py
@@ -259,18 +259,21 @@
 
 def second_z(
     d, field, from_off, from_chip, maps, masks, mod, lam, mu, part_lam, part_mu,
-    jumps, result, on_chip, off_chip, held,
+    jumps, result, on_chip, off_chip,
 ):
-    def put(which, rows, value):
-        held[rows, which * d.face : (which + 1) * d.face] = value
-
-    z_jumps(d, field, from_off, from_chip, maps, masks, put)
-    rounded = held[...].astype(BF16)
+    faces = ([], [])
+    z_jumps(
+        d, field, from_off, from_chip, maps, masks,
+        lambda which, rows, value: faces[which].append(value),
+    )
+    minus, plus = (jnp.concatenate(face, axis=0) for face in faces)
+    rounded = jnp.concatenate([minus, plus], axis=1).astype(BF16)
     jumps[...] = rounded
     one = part_lam[...] + dot(rounded, lam[d.plane :, d.plane :])
     two = part_mu[...] + dot(rounded, mu[d.plane :, d.plane :])
-    result[...] = wide(mod[0], 2 * d.face) * one + wide(mod[1], 2 * d.face) * two
-    payloads(d, result[:, : d.face], result[:, d.face :], maps, on_chip, off_chip)
+    value = wide(mod[0], 2 * d.face) * one + wide(mod[1], 2 * d.face) * two
+    result[...] = value
+    payloads(d, value[:, : d.face], value[:, d.face :], maps, on_chip, off_chip)
     off_chip[d.rows :, :] = jnp.zeros((PAD, d.face), F32)
 
 
@@ -469,7 +472,6 @@
         ],
         [VMEM] * 10,
         [field, far, near, maps, masks, mod, lam, mu, part_lam, part_mu],
-        scratch=[pltpu.VMEM((rows, 2 * face), F32)],
     )
     near, far = exchange(on_chip, off_chip, second)
     (plane,) = run(

time: 15.7 us -> 15.7 us (level)
  no operation moved by 1% of the time
where the time goes in v10:
time: 15.7 us; the launch traced here: 15.5 us
  Pallas kernels  7.64 us (49%)
  waiting for transfers between devices  4.17 us (27%)
  starting transfers between devices  3.58 us (23%)
    pallas_call x10, Pallas kernels, call(): pl.pallas_call(body, out_shape=outs, in_specs=specs, out_specs=[VMEM] * l...  7.64 us
    ppermute x2, starting transfers between devices, exchange(): return (lax.ppermute(on_chip, 'sub', pairs), far)  2.77 us
    ppermute x2, waiting for transfers between devices, exchange(): far = lax.ppermute(off_chip, ('sub', 'smp'), across)  2.45 us
    ppermute x1, waiting for transfers between devices, per_device(): lax.ppermute(own, 'smp', [(i, (i + shift) % parts) for i in range(parts)])  1.71 us
    ppermute x1, starting transfers between devices, per_device(): lax.ppermute(own, 'smp', [(i, (i + shift) % parts) for i in range(parts)])  0.6 us
  transfers between devices with their start and end apart: 5, of which 3 were waited for; matrix products, arithmetic and copies ran while one was open for 0% of the time, Pallas kernels for 37%

profile of v10, /device:TPU:10, one launch (start us, length us, event | category | flops | bytes accessed | tf_op | source)
XLA Modules:
  0.0 15.5 jit_solution(14905513644303086965)
XLA Ops:
  0.0 0.0 copy-start
  0.0 0.0 copy-start.2
  0.0 0.0 copy-start.5
  0.0 0.0 copy-start.4
  0.0 0.6 %collective-permute-start = (bf16[48,768]{1,0:T(8,128)(2,1)}, bf16[48,768]{1,0:T(8,128)(2,1)S(1)}, u32[]{:S(2)}, u32[]{:S(2)}) collective-permute-start(bf16[48,768]{1,0:T(8,128)(2,1)} %bitcast.7), channel_id=1, source_target_pairs={{0,1},{1,0},{2,3},{3,2},{4,5},{5,4},{6,7},{7,6},{8,9},{9,8},{10,11... | collective-permute-start | bytes 221192 | tf_op jit(solution)/shard_map/ppermute | solution.py:400
  0.6 1.6 %shard_map.91 = (bf16[768,768]{1,0:T(8,128)(2,1)S(1)}, bf16[768,768]{1,0:T(8,128)(2,1)S(1)}) custom-call(bf16[768,768]{1,0:T(8,128)(2,1)} %lam.1, bf16[768,768]{1,0:T(8,128)(2,1)} %mu.1), custom_call_target="tpu_custom_call" | custom-call | tf_op jit(solution)/shard_map/pallas_call | solution.py:23
  2.3 0.0 copy-done
  2.3 0.0 copy-done.2
  2.3 0.0 copy-done.5
  2.3 0.0 copy-done.4
  2.3 0.6 %shard_map.92 = (f32[2,96,128]{2,1,0:T(8,128)S(1)}, s32[2,6,8,128]{3,2,1,0:T(8,128)S(1)}, f32[48,768]{1,0:T(8,128)S(1)}, f32[48,768]{1,0:T(8,128)S(1)}) custom-call(bf16[48,768]{1,0:T(8,128)(2,1)S(1)} %bitcast.8, bf16[768,768]{1,0:T(8,128)(2,1)S(1)} %get-tuple-element.27.lam.refs_1_, bf16[768,768]{1,0:T(8,128)(2,1)S(1)} %get-tuple-element.28.mu.refs_2_, ...), custom_call_target="tpu_custom_call" | custom-call | tf_op jit(solution)/shard_map/pallas_call | solution.py:23
  2.9 1.7 %collective-permute-done.refs_0_ = bf16[48,768]{1,0:T(8,128)(2,1)S(1)} collective-permute-done((bf16[48,768]{1,0:T(8,128)(2,1)}, bf16[48,768]{1,0:T(8,128)(2,1)S(1)}, u32[]{:S(2)}, u32[]{:S(2)}) %collective-permute-start) | collective-permute-done | bytes 73760 | tf_op jit(solution)/shard_map/ppermute | solution.py:400
  4.6 0.0 copy-start.1
  4.7 0.3 %shard_map.93 = (f32[96,256]{1,0:T(8,128)S(1)}, f32[96,128]{1,0:T(8,128)S(1)}, f32[96,128]{1,0:T(8,128)S(1)}) custom-call(bf16[48,768]{1,0:T(8,128)(2,1)S(1)} %collective-permute-done.refs_0_, bf16[768,768]{1,0:T(8,128)(2,1)S(1)} %get-tuple-element.27.lam.refs_1_, bf16[768,768]{1,0:T(8,128)(2,1)S(1)} %get-tuple-element.28.mu.refs_2_, ...), custom_call_target="tpu_custom_call" | custom-call | tf_op jit(solution)/shard_map/pallas_call | solution.py:23
  5.0 0.0 collective-permute-start.1
  5.0 1.6 %collective-permute-start.2 = (f32[96,128]{1,0:T(8,128)S(1)}, f32[96,128]{1,0:T(8,128)S(1)}, u32[]{:S(2)}, u32[]{:S(2)}) collective-permute-start(f32[96,128]{1,0:T(8,128)S(1)} %get-tuple-element.35), channel_id=1, source_target_pairs={{0,2},{2,0},{4,6},{6,4},{8,10},{10,8},{12,14},{14,12},{16,18},{18,... | collective-permute-start | bytes 147464 | tf_op jit(solution)/shard_map/ppermute | solution.py:422
  6.6 0.0 copy-done.1
  6.6 0.0 copy-done.3
  6.7 0.0 copy-done.6
  6.7 0.5 %shard_map.94 = (bf16[816,16]{1,0:T(8,128)(2,1)S(1)}, f32[6,6,8,128]{3,2,1,0:T(8,128)S(1)}) custom-call(f32[16,15]{1,0:T(8,128)S(1)} %copy-done.2, f32[1,16]{1,0:T(1,128)S(1)} %bitcast.13, s32[15,816]{1,0:T(8,128)S(1)} %bitcast.9, s32[3,3,2,16]{3,2,1,0:T(2,128)S(1)} %bitcast.10), custom_call_target="tpu_custom_call" | custom-call | tf_op jit(solution)/shard_map/pallas_call | solution.py:23
  7.2 0.6 %shard_map.95 = (bf16[96,512]{1,0:T(8,128)(2,1)S(1)}, f32[96,256]{1,0:T(8,128)S(1)}, f32[96,256]{1,0:T(8,128)S(1)}) custom-call(bf16[48,768]{1,0:T(8,128)(2,1)S(1)} %collective-permute-done.refs_0_, bf16[768,768]{1,0:T(8,128)(2,1)S(1)} %get-tuple-element.27.lam.refs_1_, bf16[768,768]{1,0:T(8,128)(2,1)S(1)} %get-tuple-element.28.mu.refs_2_, ...), custom_call_target="tpu_custom_call" | custom-call | tf_op jit(solution)/shard_map/pallas_call | solution.py:23
  7.8 1.7 %collective-permute-done.1.from_off = f32[96,128]{1,0:T(8,128)S(1)} collective-permute-done((f32[96,128]{1,0:T(8,128)S(1)}, f32[96,128]{1,0:T(8,128)S(1)}, u32[]{:S(2)}, u32[]{:S(2)}) %collective-permute-start.1) | collective-permute-done | bytes 49184 | tf_op jit(solution)/shard_map/ppermute | solution.py:421
  9.4 0.0 collective-permute-done.2.from_chip
  9.4 0.3 %shard_map.96 = (bf16[96,256]{1,0:T(8,128)(2,1)S(1)}, f32[96,256]{1,0:T(8,128)S(1)}, f32[96,128]{1,0:T(8,128)S(1)}, f32[104,128]{1,0:T(8,128)S(1)}) custom-call(f32[96,256]{1,0:T(8,128)S(1)} %get-tuple-element.33.field, f32[96,128]{1,0:T(8,128)S(1)} %collective-permute-done.1.from_off, f32[96,128]{1,0:T(8,128)S(1)} %collective-permute-done.2.from_chip, ...), custom_call_target="tpu_custom_call" | custom-call | tf_op jit(solution)/shard_map/pallas_call | solution.py:23
  9.7 0.2 %collective-permute-start.3 = (f32[104,128]{1,0:T(8,128)S(1)}, f32[104,128]{1,0:T(8,128)S(1)}, u32[]{:S(2)}, u32[]{:S(2)}) collective-permute-start(f32[104,128]{1,0:T(8,128)S(1)} %get-tuple-element.40), channel_id=1, source_target_pairs={{0,1},{1,2},{2,0},{3,5},{4,6},{5,3},{6,4},{7,9},{8,10},{9,7},{10,8... | collective-permute-start | bytes 159752 | tf_op jit(solution)/shard_map/ppermute | solution.py:421
  9.9 1.1 %collective-permute-start.4 = (f32[96,128]{1,0:T(8,128)S(1)}, f32[96,128]{1,0:T(8,128)S(1)}, u32[]{:S(2)}, u32[]{:S(2)}) collective-permute-start(f32[96,128]{1,0:T(8,128)S(1)} %get-tuple-element.45), channel_id=1, source_target_pairs={{0,2},{2,0},{4,6},{6,4},{8,10},{10,8},{12,14},{14,12},{16,18},{18,... | collective-permute-start | bytes 147464 | tf_op jit(solution)/shard_map/ppermute | solution.py:422
  11.1 0.4 %shard_map.97.plane = bf16[96,512]{1,0:T(8,128)(2,1)S(1)} custom-call(bf16[96,512]{1,0:T(8,128)(2,1)S(1)} %get-tuple-element.42.plane, bf16[96,256]{1,0:T(8,128)(2,1)S(1)} %get-tuple-element.43.zed, bf16[768,768]{1,0:T(8,128)(2,1)S(1)} %get-tuple-element.27.lam.refs_1_, bf16[768,768]{1,0:T(8,128)(2,1)S(1)} %get-tuple-element.28.mu.refs_2_, ...), custom_call_target="tpu_custom_call" | custom-call | tf_op jit(solution)/shard_map/pallas_call | solution.py:23
  11.5 0.5 %shard_map.98 = (bf16[1,2,3,816,384]{4,3,2,1,0:T(8,128)(2,1)}, bf16[2,3,816,128]{3,2,1,0:T(8,128)(2,1)S(1)}) custom-call(bf16[96,512]{1,0:T(8,128)(2,1)S(1)} %shard_map.97.plane, bf16[816,16]{1,0:T(8,128)(2,1)S(1)} %get-tuple-element.41.basis), custom_call_target="tpu_custom_call" | custom-call | tf_op jit(solution)/shard_map/pallas_call | solution.py:23
  12.0 0.0 collective-permute-done.4.near
  12.0 1.5 %shard_map.99 = (bf16[1,2,3,816,384]{4,3,2,1,0:T(8,128)(2,1)}, bf16[2,3,816,128]{3,2,1,0:T(8,128)(2,1)S(1)}) custom-call(f32[96,256]{1,0:T(8,128)S(1)} %get-tuple-element.39.field, f32[96,128]{1,0:T(8,128)S(1)} %collective-permute-done.4.near, s32[2,6,8,128]{3,2,1,0:T(8,128)S(1)} %get-tuple-element.30.refs_4_.maps, ...), custom_call_target="tpu_custom_call", output_to_operand_aliasing={{0}: (6, {})} | custom-call | tf_op jit(solution)/shard_map/pallas_call | solution.py:23
  13.4 0.8 %collective-permute-done.3.far = f32[104,128]{1,0:T(8,128)S(1)} collective-permute-done((f32[104,128]{1,0:T(8,128)S(1)}, f32[104,128]{1,0:T(8,128)S(1)}, u32[]{:S(2)}, u32[]{:S(2)}) %collective-permute-start.3) | collective-permute-done | bytes 53280 | tf_op jit(solution)/shard_map/ppermute | solution.py:421
  14.2 1.3 %shard_map.100 = bf16[1,2,3,816,384]{4,3,2,1,0:T(8,128)(2,1)} custom-call(f32[96,256]{1,0:T(8,128)S(1)} %get-tuple-element.39.field, f32[104,128]{1,0:T(8,128)S(1)} %collective-permute-done.3.far, s32[2,6,8,128]{3,2,1,0:T(8,128)S(1)} %get-tuple-element.30.refs_4_.maps, ...), custom_call_target="tpu_custom_call", output_to_operand_aliasing={{}: (7, {})} | custom-call | tf_op jit(solution)/shard_map/pallas_call | solution.py:23
  (2 shorter events, 0.0 us)
Async XLA Ops:
  0.0 2.3 %copy-start = (bf16[1,2,3,8,768]{4,3,2,1,0:T(8,128)(2,1)S(1)}, bf16[1,2,3,8,768]{4,3,2,1,0:T(8,128)(2,1)}, u32[]{:S(2)}) copy-start(bf16[1,2,3,8,768]{4,3,2,1,0:T(8,128)(2,1)} %param.9) | copy-start | bytes 221188
  0.0 2.3 %copy-start.2 = (f32[16,15]{1,0:T(8,128)S(1)}, f32[16,15]{1,0:T(8,128)}, u32[]{:S(2)}) copy-start(f32[16,15]{1,0:T(8,128)} %nodes.3) | copy-start | bytes 2884
  0.0 2.3 %copy-start.5 = (s32[1,2,3,128]{3,1,2,0:T(2,128)S(1)}, s32[1,2,3,128]{3,1,2,0:T(2,128)}, u32[]{:S(2)}) copy-start(s32[1,2,3,128]{3,1,2,0:T(2,128)} %param.17) | copy-start | bytes 9220
  0.0 2.3 %copy-start.4 = (f32[2,1,2,3,15]{4,2,3,1,0:T(2,128)S(1)}, f32[2,1,2,3,15]{4,2,3,1,0:T(2,128)}, u32[]{:S(2)}) copy-start(f32[2,1,2,3,15]{4,2,3,1,0:T(2,128)} %param.12) | copy-start | bytes 2164
  0.0 4.6 %collective-permute-start = (bf16[48,768]{1,0:T(8,128)(2,1)}, bf16[48,768]{1,0:T(8,128)(2,1)S(1)}, u32[]{:S(2)}, u32[]{:S(2)}) collective-permute-start(bf16[48,768]{1,0:T(8,128)(2,1)} %bitcast.7), channel_id=1, source_target_pairs={{0,1},{1,0},{2,3},{3,2},{4,5},{5,4},{6,7},{7,6},{8,9},{9,8},{10,11... | collective-permute-start | bytes 221192 | tf_op jit(solution)/shard_map/ppermute | solution.py:400
  4.6 2.0 %copy-start.1 = (s32[816,15]{0,1:T(8,128)S(1)}, s32[816,15]{0,1:T(8,128)}, u32[]{:S(2)}) copy-start(s32[816,15]{0,1:T(8,128)} %param.15) | copy-start | bytes 146884
  4.7 2.0 %copy-start.3 = (s32[3,16,2,3]{1,2,3,0:T(2,128)S(1)}, s32[3,16,2,3]{1,2,3,0:T(2,128)}, u32[]{:S(2)}) copy-start(s32[3,16,2,3]{1,2,3,0:T(2,128)} %param.16) | copy-start | bytes 3460
  4.7 2.0 %copy-start.6 = (f32[16]{0:T(128)S(1)}, f32[16]{0:T(128)}, u32[]{:S(2)}) copy-start(f32[16]{0:T(128)} %param.14) | copy-start | bytes 196
  5.0 4.5 %collective-permute-start.1 = (f32[96,128]{1,0:T(8,128)S(1)}, f32[96,128]{1,0:T(8,128)S(1)}, u32[]{:S(2)}, u32[]{:S(2)}) collective-permute-start(f32[96,128]{1,0:T(8,128)S(1)} %get-tuple-element.34), channel_id=1, source_target_pairs={{0,1},{1,0},{2,4},{3,5},{4,2},{5,3},{6,8},{7,9},{8,6},{9,7},{10,12... | collective-permute-start | bytes 147464 | tf_op jit(solution)/shard_map/ppermute | solution.py:421
  5.0 4.4 %collective-permute-start.2 = (f32[96,128]{1,0:T(8,128)S(1)}, f32[96,128]{1,0:T(8,128)S(1)}, u32[]{:S(2)}, u32[]{:S(2)}) collective-permute-start(f32[96,128]{1,0:T(8,128)S(1)} %get-tuple-element.35), channel_id=1, source_target_pairs={{0,2},{2,0},{4,6},{6,4},{8,10},{10,8},{12,14},{14,12},{16,18},{18,... | collective-permute-start | bytes 147464 | tf_op jit(solution)/shard_map/ppermute | solution.py:422
  9.7 4.5 %collective-permute-start.3 = (f32[104,128]{1,0:T(8,128)S(1)}, f32[104,128]{1,0:T(8,128)S(1)}, u32[]{:S(2)}, u32[]{:S(2)}) collective-permute-start(f32[104,128]{1,0:T(8,128)S(1)} %get-tuple-element.40), channel_id=1, source_target_pairs={{0,1},{1,2},{2,0},{3,5},{4,6},{5,3},{6,4},{7,9},{8,10},{9,7},{10,8... | collective-permute-start | bytes 159752 | tf_op jit(solution)/shard_map/ppermute | solution.py:421
  9.9 2.1 %collective-permute-start.4 = (f32[96,128]{1,0:T(8,128)S(1)}, f32[96,128]{1,0:T(8,128)S(1)}, u32[]{:S(2)}, u32[]{:S(2)}) collective-permute-start(f32[96,128]{1,0:T(8,128)S(1)} %get-tuple-element.45), channel_id=1, source_target_pairs={{0,2},{2,0},{4,6},{6,4},{8,10},{10,8},{12,14},{14,12},{16,18},{18,... | collective-permute-start | bytes 147464 | tf_op jit(solution)/shard_map/ppermute | solution.py:422
